TPU v7x, 256 devices: a whole 4x4x8 slice. The times are simulated.
256 devices in a mesh: section: 16 (over z, y_lo), dp: 16 (over y_hi, x, core).
Axes of the slice: x: 4, y: 4 (y_hi: 2, y_lo: 2; y = y_hi * 2 + y_lo), z: 8, core: 2. Of those that a mesh axis runs over, the one named last changes fastest.
Arguments:
- inputs: bfloat16 [4, 512, 7168], P(None, 'dp'), may hold values from -6 to 6
- cotangent: bfloat16 [4, 512, 7168], P(None, 'dp'), may hold values from -0.3125 to 0.3125
- w_down: bfloat16 [16, 7168, 128], P('section'), may hold values from -0.0625 to 0.0625
- w_up: bfloat16 [16, 128, 7168], P('section'), may hold values from -0.5 to 0.5
Outputs:
- grad_down: bfloat16 [16, 7168, 128], P('section')
- grad_up: bfloat16 [16, 128, 7168], P('section')
- advance: bfloat16 [16, 4, 512, 7168], P('section', None, 'dp')
All inputs are finite; a program needn't handle non-finite values.
Results may differ from a plain program's by a relative error of at most 0.035.
Values may be sent and summed in bfloat16 or wider, within the bound.
A program may use at most 128 MiB of HBM per device.

v0:
```python
import jax
import jax.numpy as jnp
from jax import lax
from jax.sharding import PartitionSpec as P

eps = 1e-05
learn_rate = 0.05


def shifted(x, axis, by):
    peers = lax.axis_size(axis)
    pairs = [(i, i + by) for i in range(peers) if 0 <= i + by < peers]
    return lax.ppermute(x, axis, pairs)


def normalize(hidden):
    values = hidden.astype(jnp.float32)
    scaled = lax.rsqrt(jnp.mean(values * values, axis=-1, keepdims=True) + eps)
    return (values, values * scaled, scaled)


def gelu_slope(pre_act):
    return jax.grad(lambda entries: jnp.sum(jax.nn.gelu(entries)))(pre_act)


def layer_apply(hidden, down, upward):
    values, unit, scaled = normalize(hidden)
    pre_act = jnp.dot(unit.astype(jnp.bfloat16), down, preferred_element_type=jnp.float32)
    active = jax.nn.gelu(pre_act).astype(jnp.bfloat16)
    output = (values + jnp.dot(active, upward, preferred_element_type=jnp.float32)).astype(
        jnp.bfloat16
    )
    return (output, pre_act)


def layer_back(hidden, pre_act, incoming, down, upward):
    values, unit, scaled = normalize(hidden)
    back_act = jnp.dot(incoming, upward.T, preferred_element_type=jnp.float32)
    back_pre = (back_act * gelu_slope(pre_act)).astype(jnp.bfloat16)
    back_unit = jnp.dot(back_pre, down.T, preferred_element_type=jnp.float32)
    mixing = jnp.mean(back_unit * unit, axis=-1, keepdims=True)
    outgoing = (incoming.astype(jnp.float32) + scaled * (back_unit - unit * mixing)).astype(
        jnp.bfloat16
    )
    return (outgoing, back_pre)


def weight_terms(hidden, pre_act, incoming, back_pre):
    values, unit, scaled = normalize(hidden)
    unit_low = unit.astype(jnp.bfloat16)
    active = jax.nn.gelu(pre_act).astype(jnp.bfloat16)
    contract = (((0,), (0,)), ((), ()))
    term_down = lax.dot_general(unit_low, back_pre, contract, preferred_element_type=jnp.float32)
    term_up = lax.dot_general(active, incoming, contract, preferred_element_type=jnp.float32)
    return (term_down, term_up)


def put_slot(buffer, slot, value, valid):
    current = lax.dynamic_index_in_dim(buffer, slot, 0, keepdims=False)
    return lax.dynamic_update_index_in_dim(buffer, jnp.where(valid, value, current), slot, 0)


def per_device(inputs, cotangent, w_down, w_up):
    down = w_down[0]
    upward = w_up[0]
    micro, batch_rows, width = inputs.shape
    inner = down.shape[1]
    sections = lax.axis_size("section")
    section_index = lax.axis_index("section")
    ticks = micro + sections - 1

    def forward_tick(tick, state):
        arriving, saved_in, saved_pre, saved_out = state
        slot_raw = tick - section_index
        valid = (slot_raw >= 0) & (slot_raw < micro)
        slot = jnp.clip(slot_raw, 0, micro - 1)
        fresh = lax.dynamic_index_in_dim(inputs, jnp.clip(tick, 0, micro - 1), 0, keepdims=False)
        hidden = jnp.where(section_index == 0, fresh, arriving)
        output, pre_act = layer_apply(hidden, down, upward)
        saved_in = put_slot(saved_in, slot, hidden, valid)
        saved_pre = put_slot(saved_pre, slot, pre_act, valid)
        saved_out = put_slot(saved_out, slot, output, valid)
        arriving = shifted(output, "section", 1)
        return (arriving, saved_in, saved_pre, saved_out)

    act_zero = jnp.zeros((micro, batch_rows, width), jnp.bfloat16)
    pre_zero = jnp.zeros((micro, batch_rows, inner), jnp.float32)
    start_state = (jnp.zeros((batch_rows, width), jnp.bfloat16), act_zero, pre_zero, act_zero)
    unused, saved_in, saved_pre, saved_out = lax.fori_loop(0, ticks, forward_tick, start_state)

    def backward_tick(tick, state):
        arriving, saved_grad, saved_back = state
        slot_raw = tick - (sections - 1 - section_index)
        valid = (slot_raw >= 0) & (slot_raw < micro)
        slot = jnp.clip(slot_raw, 0, micro - 1)
        fresh = lax.dynamic_index_in_dim(cotangent, jnp.clip(tick, 0, micro - 1), 0, keepdims=False)
        incoming = jnp.where(section_index == sections - 1, fresh, arriving)
        hidden = lax.dynamic_index_in_dim(saved_in, slot, 0, keepdims=False)
        pre_act = lax.dynamic_index_in_dim(saved_pre, slot, 0, keepdims=False)
        outgoing, back_pre = layer_back(hidden, pre_act, incoming, down, upward)
        saved_grad = put_slot(saved_grad, slot, incoming, valid)
        saved_back = put_slot(saved_back, slot, back_pre, valid)
        arriving = shifted(outgoing, "section", -1)
        return (arriving, saved_grad, saved_back)

    back_state = (
        jnp.zeros((batch_rows, width), jnp.bfloat16),
        act_zero,
        jnp.zeros((micro, batch_rows, inner), jnp.bfloat16),
    )
    unused, saved_grad, saved_back = lax.fori_loop(0, ticks, backward_tick, back_state)
    total_rows = micro * batch_rows
    local_down, local_up = weight_terms(
        saved_in.reshape(total_rows, width),
        saved_pre.reshape(total_rows, inner),
        saved_grad.reshape(total_rows, width),
        saved_back.reshape(total_rows, inner),
    )
    outputs_flat = saved_out.reshape(total_rows, width)
    total_down, total_up = (
        lax.psum(local_down.astype(jnp.bfloat16), "dp").astype(jnp.float32),
        lax.psum(local_up.astype(jnp.bfloat16), "dp").astype(jnp.float32),
    )
    grad_down = total_down.astype(jnp.bfloat16)
    grad_up = total_up.astype(jnp.bfloat16)
    fresh_down = (down.astype(jnp.float32) - learn_rate * total_down).astype(jnp.bfloat16)
    fresh_up = (upward.astype(jnp.float32) - learn_rate * total_up).astype(jnp.bfloat16)
    next_down, next_up = shifted((fresh_down, fresh_up), "section", -1)
    ahead, unused = layer_apply(outputs_flat, next_down, next_up)
    advance = ahead.reshape(1, micro, batch_rows, width)
    return (grad_down[None], grad_up[None], advance)


def solution(mesh):
    in_specs = (
        P(None, "dp", None),
        P(None, "dp", None),
        P("section", None, None),
        P("section", None, None),
    )
    out_specs = (P("section", None, None), P("section", None, None), P("section", None, "dp", None))
    return jax.shard_map(
        per_device, mesh=mesh, in_specs=in_specs, out_specs=out_specs, check_vma=False
    )
```

profile of v0, /device:TPU:1, one launch (start us, length us, event | category | flops | bytes accessed | tf_op | source)
XLA Modules:
  0.0 1037.4 jit_solution(11862234986152714076)
XLA Ops:
  10.1 335.1 %while.39 = (s32[]{:T(128)}, bf16[32,7168]{1,0:T(8,128)(2,1)S(1)}, bf16[4,32,7168]{2,1,0:T(8,128)(2,1)}, f32[4,32,128]{2,1,0:T(8,128)S(1)}, bf16[4,32,7168]{2,1,...) while((s32[]{:T(128)}, bf16[32,7168]{1,0:T(8,128)(2,1)S(1)}, ...), condition=%wide.region_2.3_spmd, body=%wide.region_0.2_spmd.sunk | while | flops 120234024 | bytes 19826356 | solution.py:89
  20.0 9.1 collective-permute-done
  39.2 8.2 collective-permute-done
  57.6 7.3 collective-permute-done
  75.8 6.4 collective-permute-done
  88.0 5.0 collective-permute-start
  93.0 5.4 collective-permute-done
  109.3 5.4 collective-permute-done
  120.5 5.1 collective-permute-start
  125.6 5.4 collective-permute-done
  141.6 5.4 collective-permute-done
  157.5 5.4 collective-permute-done
  173.5 5.4 collective-permute-done
  189.4 5.4 collective-permute-done
  205.4 5.5 collective-permute-done
  221.8 6.5 collective-permute-done
  239.2 7.6 collective-permute-done
  257.7 8.7 collective-permute-done
  272.3 5.0 collective-permute-start
  277.3 9.8 collective-permute-done
  293.0 5.1 collective-permute-start
  298.1 9.7 collective-permute-done
  318.2 8.5 collective-permute-done
  337.6 7.6 collective-permute-done
  348.6 370.2 %while.40 = (s32[]{:T(128)}, bf16[32,7168]{1,0:T(8,128)(2,1)S(1)}, bf16[4,32,7168]{2,1,0:T(8,128)(2,1)}, bf16[4,32,128]{2,1,0:T(8,128)(2,1)S(1)}, pred[]{:T(512)...) while((s32[]{:T(128)}, bf16[32,7168]{1,0:T(8,128)(2,1)S(1)}, ...), condition=%wide.region_7.8_spmd, body=%wide.region_4.7_spmd.sunk | while | flops 121421864 | bytes 28051424 | solution.py:111
  356.3 10.4 %collective-permute-done.1 = bf16[32,7168]{1,0:T(8,128)(2,1)S(1)} collective-permute-done((bf16[32,7168]{1,0:T(8,128)(2,1)S(1)}, bf16[32,7168]{1,0:T(8,128)(2,1)S(1)}, u32[]{:S(2)}, u32[]{:S(2)}) %collective-permute-start.1) | collective-permute-done | bytes 458784 | tf_op jit(solution)/shard_map/while/body/eval_jaxpr/ppermute | solution.py:13
  374.4 18.1 %collective-permute-done.1 = bf16[32,7168]{1,0:T(8,128)(2,1)S(1)} collective-permute-done((bf16[32,7168]{1,0:T(8,128)(2,1)S(1)}, bf16[32,7168]{1,0:T(8,128)(2,1)S(1)}, u32[]{:S(2)}, u32[]{:S(2)}) %collective-permute-start.1) | collective-permute-done | bytes 458784 | tf_op jit(solution)/shard_map/while/body/eval_jaxpr/ppermute | solution.py:13
  400.2 13.6 %collective-permute-done.1 = bf16[32,7168]{1,0:T(8,128)(2,1)S(1)} collective-permute-done((bf16[32,7168]{1,0:T(8,128)(2,1)S(1)}, bf16[32,7168]{1,0:T(8,128)(2,1)S(1)}, u32[]{:S(2)}, u32[]{:S(2)}) %collective-permute-start.1) | collective-permute-done | bytes 458784 | tf_op jit(solution)/shard_map/while/body/eval_jaxpr/ppermute | solution.py:13
  421.4 12.8 %collective-permute-done.1 = bf16[32,7168]{1,0:T(8,128)(2,1)S(1)} collective-permute-done((bf16[32,7168]{1,0:T(8,128)(2,1)S(1)}, bf16[32,7168]{1,0:T(8,128)(2,1)S(1)}, u32[]{:S(2)}, u32[]{:S(2)}) %collective-permute-start.1) | collective-permute-done | bytes 458784 | tf_op jit(solution)/shard_map/while/body/eval_jaxpr/ppermute | solution.py:13
  441.8 9.3 collective-permute-done.1
  458.8 8.5 collective-permute-done.1
  474.9 8.8 collective-permute-done.1
  491.4 8.8 collective-permute-done.1
  507.9 17.0 %collective-permute-done.1 = bf16[32,7168]{1,0:T(8,128)(2,1)S(1)} collective-permute-done((bf16[32,7168]{1,0:T(8,128)(2,1)S(1)}, bf16[32,7168]{1,0:T(8,128)(2,1)S(1)}, u32[]{:S(2)}, u32[]{:S(2)}) %collective-permute-start.1) | collective-permute-done | bytes 458784 | tf_op jit(solution)/shard_map/while/body/eval_jaxpr/ppermute | solution.py:13
  532.5 9.2 collective-permute-done.1
  549.3 9.3 collective-permute-done.1
  566.3 10.0 collective-permute-done.1
  584.0 10.0 collective-permute-done.1
  601.7 10.0 collective-permute-done.1
  619.3 11.0 %collective-permute-done.1 = bf16[32,7168]{1,0:T(8,128)(2,1)S(1)} collective-permute-done((bf16[32,7168]{1,0:T(8,128)(2,1)S(1)}, bf16[32,7168]{1,0:T(8,128)(2,1)S(1)}, u32[]{:S(2)}, u32[]{:S(2)}) %collective-permute-start.1) | collective-permute-done | bytes 458784 | tf_op jit(solution)/shard_map/while/body/eval_jaxpr/ppermute | solution.py:13
  637.9 12.5 %collective-permute-done.1 = bf16[32,7168]{1,0:T(8,128)(2,1)S(1)} collective-permute-done((bf16[32,7168]{1,0:T(8,128)(2,1)S(1)}, bf16[32,7168]{1,0:T(8,128)(2,1)S(1)}, u32[]{:S(2)}, u32[]{:S(2)}) %collective-permute-start.1) | collective-permute-done | bytes 458784 | tf_op jit(solution)/shard_map/while/body/eval_jaxpr/ppermute | solution.py:13
  658.1 13.9 %collective-permute-done.1 = bf16[32,7168]{1,0:T(8,128)(2,1)S(1)} collective-permute-done((bf16[32,7168]{1,0:T(8,128)(2,1)S(1)}, bf16[32,7168]{1,0:T(8,128)(2,1)S(1)}, u32[]{:S(2)}, u32[]{:S(2)}) %collective-permute-start.1) | collective-permute-done | bytes 458784 | tf_op jit(solution)/shard_map/while/body/eval_jaxpr/ppermute | solution.py:13
  679.7 15.2 %collective-permute-done.1 = bf16[32,7168]{1,0:T(8,128)(2,1)S(1)} collective-permute-done((bf16[32,7168]{1,0:T(8,128)(2,1)S(1)}, bf16[32,7168]{1,0:T(8,128)(2,1)S(1)}, u32[]{:S(2)}, u32[]{:S(2)}) %collective-permute-start.1) | collective-permute-done | bytes 458784 | tf_op jit(solution)/shard_map/while/body/eval_jaxpr/ppermute | solution.py:13
  702.5 16.4 %collective-permute-done.1 = bf16[32,7168]{1,0:T(8,128)(2,1)S(1)} collective-permute-done((bf16[32,7168]{1,0:T(8,128)(2,1)S(1)}, bf16[32,7168]{1,0:T(8,128)(2,1)S(1)}, u32[]{:S(2)}, u32[]{:S(2)}) %collective-permute-start.1) | collective-permute-done | bytes 458784 | tf_op jit(solution)/shard_map/while/body/eval_jaxpr/ppermute | solution.py:13
  726.4 209.7 %all-reduce.3.cloned.1.call-done = (bf16[7168,128]{1,0:T(8,128)(2,1)}, bf16[128,7168]{1,0:T(8,128)(2,1)}) async-done(((bf16[7168,128]{1,0:T(8,128)(2,1)}, bf16[128,7168]{1,0:T(8,128)(2,1)}), (bf16[7168,128]{1,0:T(8,128)(2,1)}, bf16[128,7168]{1,0:T(8,128)(2,1)})) %all-reduce.3.cloned.1.call-update) | async-done | bytes 3670032 | tf_op jit(solution)/shard_map/psum | solution.py:121
  945.7 36.3 %collective-permute-done.2 = bf16[7168,128]{1,0:T(8,128)(2,1)} collective-permute-done((bf16[7168,128]{1,0:T(8,128)(2,1)}, bf16[7168,128]{1,0:T(8,128)(2,1)}, u32[]{:S(2)}, u32[]{:S(2)}) %collective-permute-start.2) | collective-permute-done | bytes 1835040 | tf_op jit(solution)/shard_map/ppermute | solution.py:13
  982.0 39.3 %collective-permute-done.3 = bf16[128,7168]{1,0:T(8,128)(2,1)} collective-permute-done((bf16[128,7168]{1,0:T(8,128)(2,1)}, bf16[128,7168]{1,0:T(8,128)(2,1)}, u32[]{:S(2)}, u32[]{:S(2)}) %collective-permute-start.3) | collective-permute-done | bytes 1835040 | tf_op jit(solution)/shard_map/ppermute | solution.py:13
  1021.3 5.1 fusion.41
  (487 shorter events, 353.2 us)
Async XLA Ops:
  7.2 929.0 %all-reduce.3.cloned.1.call-start = ((), (), s32[]{:S(2)}) async-start(), calls=%async_computation | async-start | bytes 7340032 | tf_op jit(solution)/shard_map/psum | solution.py:121
  7.2 2.9 copy-start
  16.0 13.2 %collective-permute-start = (bf16[32,7168]{1,0:T(8,128)(2,1)S(1)}, bf16[32,7168]{1,0:T(8,128)(2,1)S(1)}, u32[]{:S(2)}, u32[]{:S(2)}) collective-permute-start(bf16[32,7168]{1,0:T(8,128)(2,1)S(1)} %get-tuple-element.645), channel_id=1, source_target_pairs={{0,16},{16,32},{32,48},{48,64},{64,80},{80,96},{96,112},{112,128},... | collective-permute-start | bytes 1376264 | tf_op jit(solution)/shard_map/while/body/eval_jaxpr/ppermute | solution.py:13
  35.0 12.3 %collective-permute-start = (bf16[32,7168]{1,0:T(8,128)(2,1)S(1)}, bf16[32,7168]{1,0:T(8,128)(2,1)S(1)}, u32[]{:S(2)}, u32[]{:S(2)}) collective-permute-start(bf16[32,7168]{1,0:T(8,128)(2,1)S(1)} %get-tuple-element.645), channel_id=1, source_target_pairs={{0,16},{16,32},{32,48},{48,64},{64,80},{80,96},{96,112},{112,128},... | collective-permute-start | bytes 1376264 | tf_op jit(solution)/shard_map/while/body/eval_jaxpr/ppermute | solution.py:13
  53.2 11.6 %collective-permute-start = (bf16[32,7168]{1,0:T(8,128)(2,1)S(1)}, bf16[32,7168]{1,0:T(8,128)(2,1)S(1)}, u32[]{:S(2)}, u32[]{:S(2)}) collective-permute-start(bf16[32,7168]{1,0:T(8,128)(2,1)S(1)} %get-tuple-element.645), channel_id=1, source_target_pairs={{0,16},{16,32},{32,48},{48,64},{64,80},{80,96},{96,112},{112,128},... | collective-permute-start | bytes 1376264 | tf_op jit(solution)/shard_map/while/body/eval_jaxpr/ppermute | solution.py:13
  70.7 11.4 %collective-permute-start = (bf16[32,7168]{1,0:T(8,128)(2,1)S(1)}, bf16[32,7168]{1,0:T(8,128)(2,1)S(1)}, u32[]{:S(2)}, u32[]{:S(2)}) collective-permute-start(bf16[32,7168]{1,0:T(8,128)(2,1)S(1)} %get-tuple-element.645), channel_id=1, source_target_pairs={{0,16},{16,32},{32,48},{48,64},{64,80},{80,96},{96,112},{112,128},... | collective-permute-start | bytes 1376264 | tf_op jit(solution)/shard_map/while/body/eval_jaxpr/ppermute | solution.py:13
  88.0 10.4 %collective-permute-start = (bf16[32,7168]{1,0:T(8,128)(2,1)S(1)}, bf16[32,7168]{1,0:T(8,128)(2,1)S(1)}, u32[]{:S(2)}, u32[]{:S(2)}) collective-permute-start(bf16[32,7168]{1,0:T(8,128)(2,1)S(1)} %get-tuple-element.645), channel_id=1, source_target_pairs={{0,16},{16,32},{32,48},{48,64},{64,80},{80,96},{96,112},{112,128},... | collective-permute-start | bytes 1376264 | tf_op jit(solution)/shard_map/while/body/eval_jaxpr/ppermute | solution.py:13
  104.2 10.4 %collective-permute-start = (bf16[32,7168]{1,0:T(8,128)(2,1)S(1)}, bf16[32,7168]{1,0:T(8,128)(2,1)S(1)}, u32[]{:S(2)}, u32[]{:S(2)}) collective-permute-start(bf16[32,7168]{1,0:T(8,128)(2,1)S(1)} %get-tuple-element.645), channel_id=1, source_target_pairs={{0,16},{16,32},{32,48},{48,64},{64,80},{80,96},{96,112},{112,128},... | collective-permute-start | bytes 1376264 | tf_op jit(solution)/shard_map/while/body/eval_jaxpr/ppermute | solution.py:13
  120.5 10.5 %collective-permute-start = (bf16[32,7168]{1,0:T(8,128)(2,1)S(1)}, bf16[32,7168]{1,0:T(8,128)(2,1)S(1)}, u32[]{:S(2)}, u32[]{:S(2)}) collective-permute-start(bf16[32,7168]{1,0:T(8,128)(2,1)S(1)} %get-tuple-element.645), channel_id=1, source_target_pairs={{0,16},{16,32},{32,48},{48,64},{64,80},{80,96},{96,112},{112,128},... | collective-permute-start | bytes 1376264 | tf_op jit(solution)/shard_map/while/body/eval_jaxpr/ppermute | solution.py:13
  136.8 10.1 collective-permute-start
  152.8 10.1 collective-permute-start
  168.7 10.1 collective-permute-start
  184.7 10.1 collective-permute-start
  200.7 10.2 collective-permute-start
  216.7 11.6 %collective-permute-start = (bf16[32,7168]{1,0:T(8,128)(2,1)S(1)}, bf16[32,7168]{1,0:T(8,128)(2,1)S(1)}, u32[]{:S(2)}, u32[]{:S(2)}) collective-permute-start(bf16[32,7168]{1,0:T(8,128)(2,1)S(1)} %get-tuple-element.645), channel_id=1, source_target_pairs={{0,16},{16,32},{32,48},{48,64},{64,80},{80,96},{96,112},{112,128},... | collective-permute-start | bytes 1376264 | tf_op jit(solution)/shard_map/while/body/eval_jaxpr/ppermute | solution.py:13
  234.2 12.7 %collective-permute-start = (bf16[32,7168]{1,0:T(8,128)(2,1)S(1)}, bf16[32,7168]{1,0:T(8,128)(2,1)S(1)}, u32[]{:S(2)}, u32[]{:S(2)}) collective-permute-start(bf16[32,7168]{1,0:T(8,128)(2,1)S(1)} %get-tuple-element.645), channel_id=1, source_target_pairs={{0,16},{16,32},{32,48},{48,64},{64,80},{80,96},{96,112},{112,128},... | collective-permute-start | bytes 1376264 | tf_op jit(solution)/shard_map/while/body/eval_jaxpr/ppermute | solution.py:13
  252.7 13.7 %collective-permute-start = (bf16[32,7168]{1,0:T(8,128)(2,1)S(1)}, bf16[32,7168]{1,0:T(8,128)(2,1)S(1)}, u32[]{:S(2)}, u32[]{:S(2)}) collective-permute-start(bf16[32,7168]{1,0:T(8,128)(2,1)S(1)} %get-tuple-element.645), channel_id=1, source_target_pairs={{0,16},{16,32},{32,48},{48,64},{64,80},{80,96},{96,112},{112,128},... | collective-permute-start | bytes 1376264 | tf_op jit(solution)/shard_map/while/body/eval_jaxpr/ppermute | solution.py:13
  272.3 14.9 %collective-permute-start = (bf16[32,7168]{1,0:T(8,128)(2,1)S(1)}, bf16[32,7168]{1,0:T(8,128)(2,1)S(1)}, u32[]{:S(2)}, u32[]{:S(2)}) collective-permute-start(bf16[32,7168]{1,0:T(8,128)(2,1)S(1)} %get-tuple-element.645), channel_id=1, source_target_pairs={{0,16},{16,32},{32,48},{48,64},{64,80},{80,96},{96,112},{112,128},... | collective-permute-start | bytes 1376264 | tf_op jit(solution)/shard_map/while/body/eval_jaxpr/ppermute | solution.py:13
  293.0 14.8 %collective-permute-start = (bf16[32,7168]{1,0:T(8,128)(2,1)S(1)}, bf16[32,7168]{1,0:T(8,128)(2,1)S(1)}, u32[]{:S(2)}, u32[]{:S(2)}) collective-permute-start(bf16[32,7168]{1,0:T(8,128)(2,1)S(1)} %get-tuple-element.645), channel_id=1, source_target_pairs={{0,16},{16,32},{32,48},{48,64},{64,80},{80,96},{96,112},{112,128},... | collective-permute-start | bytes 1376264 | tf_op jit(solution)/shard_map/while/body/eval_jaxpr/ppermute | solution.py:13
  313.6 13.1 %collective-permute-start = (bf16[32,7168]{1,0:T(8,128)(2,1)S(1)}, bf16[32,7168]{1,0:T(8,128)(2,1)S(1)}, u32[]{:S(2)}, u32[]{:S(2)}) collective-permute-start(bf16[32,7168]{1,0:T(8,128)(2,1)S(1)} %get-tuple-element.645), channel_id=1, source_target_pairs={{0,16},{16,32},{32,48},{48,64},{64,80},{80,96},{96,112},{112,128},... | collective-permute-start | bytes 1376264 | tf_op jit(solution)/shard_map/while/body/eval_jaxpr/ppermute | solution.py:13
  332.6 12.6 %collective-permute-start = (bf16[32,7168]{1,0:T(8,128)(2,1)S(1)}, bf16[32,7168]{1,0:T(8,128)(2,1)S(1)}, u32[]{:S(2)}, u32[]{:S(2)}) collective-permute-start(bf16[32,7168]{1,0:T(8,128)(2,1)S(1)} %get-tuple-element.645), channel_id=1, source_target_pairs={{0,16},{16,32},{32,48},{48,64},{64,80},{80,96},{96,112},{112,128},... | collective-permute-start | bytes 1376264 | tf_op jit(solution)/shard_map/while/body/eval_jaxpr/ppermute | solution.py:13
  351.0 2.9 copy-start.4
  355.0 11.8 %collective-permute-start.1 = (bf16[32,7168]{1,0:T(8,128)(2,1)S(1)}, bf16[32,7168]{1,0:T(8,128)(2,1)S(1)}, u32[]{:S(2)}, u32[]{:S(2)}) collective-permute-start(bf16[32,7168]{1,0:T(8,128)(2,1)S(1)} %fusion.113), channel_id=1, source_target_pairs={{16,0},{32,16},{48,32},{64,48},{80,64},{96,80},{112,96},{128,112},... | collective-permute-start | bytes 1376264 | tf_op jit(solution)/shard_map/while/body/eval_jaxpr/ppermute | solution.py:13
  373.1 19.4 %collective-permute-start.1 = (bf16[32,7168]{1,0:T(8,128)(2,1)S(1)}, bf16[32,7168]{1,0:T(8,128)(2,1)S(1)}, u32[]{:S(2)}, u32[]{:S(2)}) collective-permute-start(bf16[32,7168]{1,0:T(8,128)(2,1)S(1)} %fusion.113), channel_id=1, source_target_pairs={{16,0},{32,16},{48,32},{64,48},{80,64},{96,80},{112,96},{128,112},... | collective-permute-start | bytes 1376264 | tf_op jit(solution)/shard_map/while/body/eval_jaxpr/ppermute | solution.py:13
  398.9 14.9 %collective-permute-start.1 = (bf16[32,7168]{1,0:T(8,128)(2,1)S(1)}, bf16[32,7168]{1,0:T(8,128)(2,1)S(1)}, u32[]{:S(2)}, u32[]{:S(2)}) collective-permute-start(bf16[32,7168]{1,0:T(8,128)(2,1)S(1)} %fusion.113), channel_id=1, source_target_pairs={{16,0},{32,16},{48,32},{64,48},{80,64},{96,80},{112,96},{128,112},... | collective-permute-start | bytes 1376264 | tf_op jit(solution)/shard_map/while/body/eval_jaxpr/ppermute | solution.py:13
  420.1 14.1 %collective-permute-start.1 = (bf16[32,7168]{1,0:T(8,128)(2,1)S(1)}, bf16[32,7168]{1,0:T(8,128)(2,1)S(1)}, u32[]{:S(2)}, u32[]{:S(2)}) collective-permute-start(bf16[32,7168]{1,0:T(8,128)(2,1)S(1)} %fusion.113), channel_id=1, source_target_pairs={{16,0},{32,16},{48,32},{64,48},{80,64},{96,80},{112,96},{128,112},... | collective-permute-start | bytes 1376264 | tf_op jit(solution)/shard_map/while/body/eval_jaxpr/ppermute | solution.py:13
  440.5 10.6 %collective-permute-start.1 = (bf16[32,7168]{1,0:T(8,128)(2,1)S(1)}, bf16[32,7168]{1,0:T(8,128)(2,1)S(1)}, u32[]{:S(2)}, u32[]{:S(2)}) collective-permute-start(bf16[32,7168]{1,0:T(8,128)(2,1)S(1)} %fusion.113), channel_id=1, source_target_pairs={{16,0},{32,16},{48,32},{64,48},{80,64},{96,80},{112,96},{128,112},... | collective-permute-start | bytes 1376264 | tf_op jit(solution)/shard_map/while/body/eval_jaxpr/ppermute | solution.py:13
  457.5 9.8 collective-permute-start.1
  473.6 10.1 collective-permute-start.1
  490.1 10.1 collective-permute-start.1
  506.6 18.3 %collective-permute-start.1 = (bf16[32,7168]{1,0:T(8,128)(2,1)S(1)}, bf16[32,7168]{1,0:T(8,128)(2,1)S(1)}, u32[]{:S(2)}, u32[]{:S(2)}) collective-permute-start(bf16[32,7168]{1,0:T(8,128)(2,1)S(1)} %fusion.113), channel_id=1, source_target_pairs={{16,0},{32,16},{48,32},{64,48},{80,64},{96,80},{112,96},{128,112},... | collective-permute-start | bytes 1376264 | tf_op jit(solution)/shard_map/while/body/eval_jaxpr/ppermute | solution.py:13
  531.2 10.5 %collective-permute-start.1 = (bf16[32,7168]{1,0:T(8,128)(2,1)S(1)}, bf16[32,7168]{1,0:T(8,128)(2,1)S(1)}, u32[]{:S(2)}, u32[]{:S(2)}) collective-permute-start(bf16[32,7168]{1,0:T(8,128)(2,1)S(1)} %fusion.113), channel_id=1, source_target_pairs={{16,0},{32,16},{48,32},{64,48},{80,64},{96,80},{112,96},{128,112},... | collective-permute-start | bytes 1376264 | tf_op jit(solution)/shard_map/while/body/eval_jaxpr/ppermute | solution.py:13
  548.0 10.6 %collective-permute-start.1 = (bf16[32,7168]{1,0:T(8,128)(2,1)S(1)}, bf16[32,7168]{1,0:T(8,128)(2,1)S(1)}, u32[]{:S(2)}, u32[]{:S(2)}) collective-permute-start(bf16[32,7168]{1,0:T(8,128)(2,1)S(1)} %fusion.113), channel_id=1, source_target_pairs={{16,0},{32,16},{48,32},{64,48},{80,64},{96,80},{112,96},{128,112},... | collective-permute-start | bytes 1376264 | tf_op jit(solution)/shard_map/while/body/eval_jaxpr/ppermute | solution.py:13
  565.0 11.3 %collective-permute-start.1 = (bf16[32,7168]{1,0:T(8,128)(2,1)S(1)}, bf16[32,7168]{1,0:T(8,128)(2,1)S(1)}, u32[]{:S(2)}, u32[]{:S(2)}) collective-permute-start(bf16[32,7168]{1,0:T(8,128)(2,1)S(1)} %fusion.113), channel_id=1, source_target_pairs={{16,0},{32,16},{48,32},{64,48},{80,64},{96,80},{112,96},{128,112},... | collective-permute-start | bytes 1376264 | tf_op jit(solution)/shard_map/while/body/eval_jaxpr/ppermute | solution.py:13
  582.7 11.3 %collective-permute-start.1 = (bf16[32,7168]{1,0:T(8,128)(2,1)S(1)}, bf16[32,7168]{1,0:T(8,128)(2,1)S(1)}, u32[]{:S(2)}, u32[]{:S(2)}) collective-permute-start(bf16[32,7168]{1,0:T(8,128)(2,1)S(1)} %fusion.113), channel_id=1, source_target_pairs={{16,0},{32,16},{48,32},{64,48},{80,64},{96,80},{112,96},{128,112},... | collective-permute-start | bytes 1376264 | tf_op jit(solution)/shard_map/while/body/eval_jaxpr/ppermute | solution.py:13
  600.4 11.3 %collective-permute-start.1 = (bf16[32,7168]{1,0:T(8,128)(2,1)S(1)}, bf16[32,7168]{1,0:T(8,128)(2,1)S(1)}, u32[]{:S(2)}, u32[]{:S(2)}) collective-permute-start(bf16[32,7168]{1,0:T(8,128)(2,1)S(1)} %fusion.113), channel_id=1, source_target_pairs={{16,0},{32,16},{48,32},{64,48},{80,64},{96,80},{112,96},{128,112},... | collective-permute-start | bytes 1376264 | tf_op jit(solution)/shard_map/while/body/eval_jaxpr/ppermute | solution.py:13
  618.0 12.3 %collective-permute-start.1 = (bf16[32,7168]{1,0:T(8,128)(2,1)S(1)}, bf16[32,7168]{1,0:T(8,128)(2,1)S(1)}, u32[]{:S(2)}, u32[]{:S(2)}) collective-permute-start(bf16[32,7168]{1,0:T(8,128)(2,1)S(1)} %fusion.113), channel_id=1, source_target_pairs={{16,0},{32,16},{48,32},{64,48},{80,64},{96,80},{112,96},{128,112},... | collective-permute-start | bytes 1376264 | tf_op jit(solution)/shard_map/while/body/eval_jaxpr/ppermute | solution.py:13
  636.6 13.8 %collective-permute-start.1 = (bf16[32,7168]{1,0:T(8,128)(2,1)S(1)}, bf16[32,7168]{1,0:T(8,128)(2,1)S(1)}, u32[]{:S(2)}, u32[]{:S(2)}) collective-permute-start(bf16[32,7168]{1,0:T(8,128)(2,1)S(1)} %fusion.113), channel_id=1, source_target_pairs={{16,0},{32,16},{48,32},{64,48},{80,64},{96,80},{112,96},{128,112},... | collective-permute-start | bytes 1376264 | tf_op jit(solution)/shard_map/while/body/eval_jaxpr/ppermute | solution.py:13
  656.8 15.2 %collective-permute-start.1 = (bf16[32,7168]{1,0:T(8,128)(2,1)S(1)}, bf16[32,7168]{1,0:T(8,128)(2,1)S(1)}, u32[]{:S(2)}, u32[]{:S(2)}) collective-permute-start(bf16[32,7168]{1,0:T(8,128)(2,1)S(1)} %fusion.113), channel_id=1, source_target_pairs={{16,0},{32,16},{48,32},{64,48},{80,64},{96,80},{112,96},{128,112},... | collective-permute-start | bytes 1376264 | tf_op jit(solution)/shard_map/while/body/eval_jaxpr/ppermute | solution.py:13
  678.3 16.5 %collective-permute-start.1 = (bf16[32,7168]{1,0:T(8,128)(2,1)S(1)}, bf16[32,7168]{1,0:T(8,128)(2,1)S(1)}, u32[]{:S(2)}, u32[]{:S(2)}) collective-permute-start(bf16[32,7168]{1,0:T(8,128)(2,1)S(1)} %fusion.113), channel_id=1, source_target_pairs={{16,0},{32,16},{48,32},{64,48},{80,64},{96,80},{112,96},{128,112},... | collective-permute-start | bytes 1376264 | tf_op jit(solution)/shard_map/while/body/eval_jaxpr/ppermute | solution.py:13
  701.2 17.7 %collective-permute-start.1 = (bf16[32,7168]{1,0:T(8,128)(2,1)S(1)}, bf16[32,7168]{1,0:T(8,128)(2,1)S(1)}, u32[]{:S(2)}, u32[]{:S(2)}) collective-permute-start(bf16[32,7168]{1,0:T(8,128)(2,1)S(1)} %fusion.113), channel_id=1, source_target_pairs={{16,0},{32,16},{48,32},{64,48},{80,64},{96,80},{112,96},{128,112},... | collective-permute-start | bytes 1376264 | tf_op jit(solution)/shard_map/while/body/eval_jaxpr/ppermute | solution.py:13
  718.8 3.6 copy-start.5
  936.1 4.8 copy-start.3
  936.1 4.8 copy-start.7
  939.6 42.4 %collective-permute-start.2 = (bf16[7168,128]{1,0:T(8,128)(2,1)}, bf16[7168,128]{1,0:T(8,128)(2,1)}, u32[]{:S(2)}, u32[]{:S(2)}) collective-permute-start(bf16[7168,128]{1,0:T(8,128)(2,1)} %subtract_convert_fusion.1), channel_id=1, source_target_pairs={{16,0},{32,16},{48,32},{64,48},{80,64},{96,80},{112,96},{128,112},... | collective-permute-start | bytes 5505032 | tf_op jit(solution)/shard_map/ppermute | solution.py:13
  940.9 3.2 copy-start.6
  942.7 78.6 %collective-permute-start.3 = (bf16[128,7168]{1,0:T(8,128)(2,1)}, bf16[128,7168]{1,0:T(8,128)(2,1)}, u32[]{:S(2)}, u32[]{:S(2)}) collective-permute-start(bf16[128,7168]{1,0:T(8,128)(2,1)} %subtract_convert_fusion), channel_id=1, source_target_pairs={{16,0},{32,16},{48,32},{64,48},{80,64},{96,80},{112,96},{128,112},... | collective-permute-start | bytes 5505032 | tf_op jit(solution)/shard_map/ppermute | solution.py:13
  1026.4 3.0 copy-start.8
  (56 other events, 120.8 us)
Sparse Core Ops, SparseCore 0:
  724.6 211.5 all-reduce.2
where the time goes:
time: 1040 us
  waiting for transfers between devices  643 us (62%)
  other arithmetic  125 us (12%)
  starting transfers between devices  118 us (11%)
  matrix products  71.1 us (7%)
  local copies, waits for them, and re-layouts  64.2 us (6%)
  between operations  14.1 us (1%)
    ppermute x40, waiting for transfers between devices, shifted(): return lax.ppermute(x, axis, pairs)  433 us
    psum x1, waiting for transfers between devices, per_device(): lax.psum(local_down.astype(jnp.bfloat16), 'dp').astype(jnp.float32)  210 us
    ppermute x40, starting transfers between devices, shifted(): return lax.ppermute(x, axis, pairs)  118 us
    dynamic_update_slice x38, other arithmetic, put_slot(): lax.dynamic_update_index_in_dim(buffer, jnp.where(valid, value, current),...  80.6 us
    dynamic_slice x76, local copies, waits for them, and re-layouts, put_slot(): current = lax.dynamic_index_in_dim(buffer, slot, 0, keepdims=False)  40.2 us
    reduce_sum x40, other arithmetic, normalize(): scaled = lax.rsqrt(jnp.mean(values * values, axis=-1, keepdims=True) + eps)  31.3 us
    dot_general x20, matrix products, layer_apply(): jnp.dot(active, upward, preferred_element_type=jnp.float32)  27.5 us
  transfers between devices with their start and end apart: 41, of which 41 were waited for; matrix products, arithmetic and copies ran while one was open for 1% of the time, Pallas kernels for 0%

commit v1 on v0

v1 whole, which is shorter than its diff:
```python
import functools

import jax
import jax.numpy as jnp
from jax import lax
from jax.experimental import pallas as pl
from jax.experimental.pallas import tpu as pltpu
from jax.sharding import PartitionSpec as P

MESH = pl.DeviceIdType.MESH
eps = 1e-05
learn_rate = 0.05
f32 = jnp.float32
bf16 = jnp.bfloat16


def dot_nn(a, b):
    return jnp.dot(a, b, preferred_element_type=f32)


def dot_tn(a, b):
    return lax.dot_general(a, b, (((0,), (0,)), ((), ())), preferred_element_type=f32)


def dot_nt(a, b):
    return lax.dot_general(a, b, (((1,), (1,)), ((), ())), preferred_element_type=f32)


def gelu_pair(a):
    c = 0.7978845608028654
    inner = c * (a + 0.044715 * a * a * a)
    th = jnp.tanh(inner)
    value = 0.5 * a * (1.0 + th)
    slope = 0.5 * (1.0 + th) + 0.5 * a * (1.0 - th * th) * c * (1.0 + 3 * 0.044715 * a * a)
    return value, slope


def recurrence_kernel(sections, chunks, pyh, n0, mm, gu, x0, up, xout, u_out, q_out, cc, e_out,
                      ul, ql, mb, ys, nl, nsend, pacc, yacc, hacc, slope, act, rinv, ecol,
                      upart, xin, xkeep, xgive,
                      u_send, u_recv, q_send, q_recv, m_send, m_recv, n_sem, w_sem, c_send, c_recv,
                      g_send, g_recv):
    s = lax.axis_index("section")
    rows, width = x0.shape
    rank = up.shape[0]
    half = width // 2
    piece = half // chunks
    z = s // 2
    ylo = lax.rem(s, 2)
    partner = s + 1 - 2 * ylo

    def peer(offset):
        return lax.rem(s + offset, sections)

    barrier = pltpu.get_barrier_semaphore()

    def greet(o, carry):
        pl.semaphore_signal(barrier, inc=1, device_id={"section": peer(o)}, device_id_type=MESH)
        return carry

    lax.fori_loop(1, sections, greet, 0)
    pl.semaphore_wait(barrier, sections - 1)

    eye = (lax.broadcasted_iota(jnp.int32, (rows, rows), 0)
           == lax.broadcasted_iota(jnp.int32, (rows, rows), 1)).astype(f32)

    def to_row(col):
        return jnp.sum(eye * col, axis=0, keepdims=True)

    def to_col(row):
        return jnp.sum(eye * row, axis=1, keepdims=True)

    def columns(base, c):
        return pl.ds(pl.multiple_of(base + c * piece, 128), piece)

    def w_copy():
        return pltpu.make_async_remote_copy(
            src_ref=up.at[:, pl.ds(pl.multiple_of((1 - ylo) * half, 128), half)],
            dst_ref=upart, send_sem=w_sem.at[0], recv_sem=w_sem.at[1],
            device_id={"section": partner}, device_id_type=MESH)

    def u_copy(o):
        return pltpu.make_async_remote_copy(
            src_ref=ul.at[s], dst_ref=ul.at[s], send_sem=u_send.at[o], recv_sem=u_recv.at[s],
            device_id={"section": peer(o)}, device_id_type=MESH)

    def u_arrived(k):
        return pltpu.make_async_remote_copy(
            src_ref=ul.at[k], dst_ref=ul.at[k], send_sem=u_send.at[0], recv_sem=u_recv.at[k],
            device_id={"section": partner}, device_id_type=MESH)

    def q_copy(j):
        return pltpu.make_async_remote_copy(
            src_ref=ql.at[s], dst_ref=ql.at[s], send_sem=q_send.at[j], recv_sem=q_recv.at[s],
            device_id={"section": j}, device_id_type=MESH)

    def q_arrived(k):
        return pltpu.make_async_remote_copy(
            src_ref=ql.at[k], dst_ref=ql.at[k], send_sem=q_send.at[0], recv_sem=q_recv.at[k],
            device_id={"section": partner}, device_id_type=MESH)

    def m_copy(j):
        return pltpu.make_async_remote_copy(
            src_ref=mm.at[j], dst_ref=mb.at[s], send_sem=m_send.at[j], recv_sem=m_recv.at[s],
            device_id={"section": j}, device_id_type=MESH)

    def m_arrived(k):
        return pltpu.make_async_remote_copy(
            src_ref=mb.at[k], dst_ref=mb.at[k], send_sem=m_send.at[0], recv_sem=m_recv.at[k],
            device_id={"section": partner}, device_id_type=MESH)

    def n_copy():
        return pltpu.make_async_remote_copy(
            src_ref=nsend, dst_ref=nl, send_sem=n_sem.at[0], recv_sem=n_sem.at[1],
            device_id={"section": peer(1)}, device_id_type=MESH)

    def x_copy(c):
        return pltpu.make_async_remote_copy(
            src_ref=xkeep.at[:, columns(0, c)], dst_ref=xin.at[:, columns(0, c)],
            send_sem=c_send.at[c], recv_sem=c_recv.at[c],
            device_id={"section": peer(2)}, device_id_type=MESH)

    def give_copy(c):
        return pltpu.make_async_remote_copy(
            src_ref=xgive.at[:, columns(0, c)], dst_ref=xout.at[:, columns(ylo * half, c)],
            send_sem=g_send.at[c], recv_sem=g_recv.at[c],
            device_id={"section": partner}, device_id_type=MESH)

    def give_arrived(c):
        return pltpu.make_async_remote_copy(
            src_ref=xgive.at[:, columns(0, c)], dst_ref=xout.at[:, columns((1 - ylo) * half, c)],
            send_sem=g_send.at[c], recv_sem=g_recv.at[c],
            device_id={"section": partner}, device_id_type=MESH)

    def start_m(j, carry):
        @pl.when(j < s)
        def _():
            m_copy(j).start()
        return carry

    pacc[...] = pyh[0]
    yacc[...] = pyh[1]
    hacc[...] = pyh[2]
    ecol[...] = jnp.zeros_like(ecol)

    def chain(t):
        c = t - (2 * z + 3)

        @pl.when((c >= 0) & (c < chunks))
        def _():
            @pl.when(z > 0)
            def _():
                x_copy(c).wait_recv()

            @pl.when(c == 0)
            def _():
                w_copy().wait_recv()

            here = columns(ylo * half, c)
            start = jnp.where(z > 0, xin[:, columns(0, c)], x0[:, here]).astype(f32)
            mine = up[:, here]
            other = upart[:, columns(0, c)]
            first = ylo == 0
            u_a = ul[2 * z]
            u_b = ul[2 * z + 1]
            x_a = (start + dot_nn(u_a, jnp.where(first, mine, other))).astype(bf16)
            x_b = (x_a.astype(f32) + dot_nn(u_b, jnp.where(first, other, mine))).astype(bf16)
            xkeep[:, columns(0, c)] = x_b

            @pl.when(z < sections // 2 - 1)
            def _():
                x_copy(c).start()

            xgive[:, columns(0, c)] = jnp.where(first, x_b, x_a)
            give_copy(c).start()
            xout[:, here] = jnp.where(first, x_a, x_b)

    def forward_tick(t, carry):
        k = t - 1

        @pl.when((t > 0) & (k != s))
        def _():
            u_arrived(k).wait_recv()

        @pl.when((t > 0) & (k < s))
        def _():
            pacc[...] += dot_nn(ul[k], mm[k])

        @pl.when(t == s)
        def _():
            @pl.when(s > 0)
            def _():
                n_copy().wait_recv()

            norm = jnp.where(s > 0, to_col(nl[0:1, :]), n0[:, 0:1])
            scale = lax.rsqrt(norm * (1.0 / width) + eps)
            pre = pacc[...] * scale
            value, grad = gelu_pair(pre)
            ul[s] = value.astype(bf16)

            def send(o, carry):
                u_copy(o).start()
                return carry

            lax.fori_loop(1, sections, send, 0)
            act[...] = pre
            slope[...] = grad
            rinv[...] = jnp.broadcast_to(scale, rinv.shape)

        @pl.when((t > 0) & (k > s))
        def _():
            ys[k] = yacc[...]

        @pl.when(t > 0)
        def _():
            yacc[...] += dot_nn(ul[k], gu[k])

        @pl.when((t == s) & (s < sections - 1))
        def _():
            mine = ul[s]
            norm = jnp.where(s > 0, to_col(nl[0:1, :]), n0[:, 0:1])
            grown = norm + jnp.sum(
                mine.astype(f32) * (2.0 * yacc[...] + dot_nn(mine, gu[s])), axis=1, keepdims=True)
            nsend[...] = jnp.broadcast_to(to_row(grown), nsend.shape)
            n_copy().start()

        @pl.when(t == 0)
        def _():
            w_copy().start()
            lax.fori_loop(0, sections, start_m, 0)

        chain(t)
        return carry

    lax.fori_loop(0, sections, forward_tick, 0)

    @pl.when(s != sections - 1)
    def _():
        u_arrived(sections - 1).wait_recv()

    def c_of(k):
        return to_col(ql[k, rows:rows + 1, :].astype(f32) + ql[k, rows + 1:rows + 2, :].astype(f32))

    def cross(k, head):
        sum_col = ecol[...]
        cc[k, :, 0:rank] = head.astype(bf16)
        mine = ul[s].astype(f32) * sum_col
        cc[k, :, rank:2 * rank] = (-dot_tn(ul[k], mine.astype(bf16))).astype(bf16)

    def backward_tick(t, carry):
        j = 2 * sections - 1 - t
        k = j + 1
        behind = (k < sections) & (k > s)

        @pl.when(behind)
        def _():
            m_arrived(k).wait_recv()
            q_arrived(k).wait_recv()
            hacc[...] += dot_nt(ql[k, 0:rows, :], mb[k]) - c_of(k) * ys[k]

        @pl.when(s == j)
        def _():
            q = hacc[...] * slope[...]
            scale = rinv[...]
            ql[s, 0:rows, :] = (q * scale).astype(bf16)
            mix = jnp.sum(q * act[...], axis=1, keepdims=True) * (1.0 / width)
            line = to_row(mix * scale[:, 0:1] * scale[:, 0:1])
            high = line.astype(bf16)
            low = (line - high.astype(f32)).astype(bf16)
            spot = lax.broadcasted_iota(jnp.int32, (16, rows), 0)
            ql[s, rows:rows + 16, :] = jnp.where(
                spot == 0, high.astype(f32), jnp.where(spot == 1, low.astype(f32), 0.0)).astype(bf16)

            def send(i, carry):
                q_copy(s - 1 - i).start()
                return carry

            lax.fori_loop(0, s, send, 0)

        @pl.when(behind)
        def _():
            cross(k, dot_tn(ql[k, 0:rows, :], ul[s]))
            ecol[...] += jnp.broadcast_to(c_of(k), ecol.shape)

        chain(t)
        return carry

    lax.fori_loop(sections, 2 * sections, backward_tick, 0)

    def tail(k, carry):
        @pl.when(k <= s)
        def _():
            keep = jnp.where(k < s, 1.0, 0.0)
            cross(k, dot_tn(ul[k], ql[s, 0:rows, :]) * keep)
        return carry

    lax.fori_loop(0, sections, tail, 0)
    u_out[...] = ul[s]
    q_out[...] = ql[s, 0:rows, :]
    e_out[...] = ecol[...]

    def finish(c, carry):
        @pl.when(z < sections // 2 - 1)
        def _():
            x_copy(c).wait_send()
        give_copy(c).wait_send()
        give_arrived(c).wait_recv()
        return carry

    lax.fori_loop(0, chunks, finish, 0)

    def settle(o, carry):
        u_copy(o).wait_send()

        @pl.when(o - 1 < s)
        def _():
            q_copy(o - 1).wait_send()
            m_copy(o - 1).wait_send()
        return carry

    lax.fori_loop(1, sections, settle, 0)
    w_copy().wait_send()

    @pl.when(s < sections - 1)
    def _():
        n_copy().wait_send()


def recurrence(sections, pyh, n0, mm, gu, x0, up):
    rows, width = x0.shape
    rank = up.shape[0]
    half = width // 2
    chunks = 14
    vm = pl.BlockSpec(memory_space=pltpu.VMEM)
    dma = pltpu.SemaphoreType.DMA
    block = (sections, rank, rank)
    sq = (rows, rank)
    return pl.pallas_call(
        functools.partial(recurrence_kernel, sections, chunks),
        out_shape=(
            jax.ShapeDtypeStruct((rows, width), bf16),
            jax.ShapeDtypeStruct(sq, bf16),
            jax.ShapeDtypeStruct(sq, bf16),
            jax.ShapeDtypeStruct((sections, rank, 2 * rank), bf16),
            jax.ShapeDtypeStruct(sq, f32),
        ),
        in_specs=[vm] * 6,
        out_specs=(vm,) * 5,
        scratch_shapes=[
            pltpu.VMEM((sections, rows, rank), bf16),
            pltpu.VMEM((sections, rows + 16, rank), bf16),
            pltpu.VMEM(block, bf16),
            pltpu.VMEM((sections, rows, rank), f32),
            pltpu.VMEM((8, rows), f32),
            pltpu.VMEM((8, rows), f32),
            pltpu.VMEM(sq, f32), pltpu.VMEM(sq, f32), pltpu.VMEM(sq, f32),
            pltpu.VMEM(sq, f32), pltpu.VMEM(sq, f32), pltpu.VMEM(sq, f32), pltpu.VMEM(sq, f32),
            pltpu.VMEM((rank, half), bf16),
            pltpu.VMEM((rows, half), bf16),
            pltpu.VMEM((rows, half), bf16),
            pltpu.VMEM((rows, half), bf16),
            dma((sections,)), dma((sections,)), dma((sections,)), dma((sections,)),
            dma((sections,)), dma((sections,)), dma((2,)), dma((2,)),
            dma((chunks,)), dma((chunks,)), dma((chunks,)), dma((chunks,)),
        ],
        compiler_params=pltpu.CompilerParams(
            collective_id=1, has_side_effects=True, vmem_limit_bytes=40 * 1024 * 1024),
    )(pyh, n0, mm, gu, x0, up)


def per_device(inputs, cotangent, w_down, w_up):
    down = w_down[0]
    upward = w_up[0]
    micro, batch_rows, width = inputs.shape
    rank = down.shape[1]
    rows = micro * batch_rows
    sections = lax.axis_size("section")
    shards = lax.axis_size("dp")
    part = width // shards
    d = lax.axis_index("dp")
    x0 = inputs.reshape(rows, width)
    g16 = cotangent.reshape(rows, width)
    up_t = upward.T

    mine_u = lax.dynamic_slice_in_dim(up_t, d * part, part, 0)
    mine_w = lax.dynamic_slice_in_dim(down, d * part, part, 0)
    all_u = lax.all_gather(mine_u, "section")
    all_w = lax.all_gather(mine_w, "section")
    grams = jnp.einsum("kfr,fc->krc", all_u, jnp.concatenate([mine_w, mine_u], axis=1),
                       preferred_element_type=f32).astype(bf16)
    grams = lax.psum(grams, "dp")
    mm = grams[:, :, :rank]
    gu = grams[:, :, rank:]

    pyh = jnp.stack([dot_nn(x0, down), dot_nt(x0, upward), dot_nt(g16, upward)])
    values = x0.astype(f32)
    n0 = jnp.broadcast_to(jnp.sum(values * values, axis=1, keepdims=True), (rows, rank))

    ahead_in, u_s, q_s, cc, e_s = recurrence(sections, pyh, n0, mm, gu, x0, upward)

    mixed = (g16.astype(f32) - e_s[:, 0:1] * values).astype(bf16)
    g_part = jnp.concatenate([dot_tn(x0, q_s), dot_tn(mixed, u_s)], axis=1).astype(bf16)
    packed = jnp.concatenate([g_part.reshape(shards, part, 2 * rank), cc], axis=1)
    mine = lax.psum_scatter(packed, "dp", scatter_dimension=0, tiled=False)
    all_cc = lax.all_gather(mine[part:], "dp")
    order = lax.broadcasted_iota(jnp.int32, (sections, 1, 1), 0)
    s = lax.axis_index("section")
    head = all_cc[:, :, :rank]
    zero = jnp.zeros_like(head)
    for_u = jnp.concatenate([jnp.where(order < s, head, zero), all_cc[:, :, rank:]], axis=2)
    for_w = jnp.where(order > s, head, zero)
    fix_u = jnp.einsum("kfr,krc->fc", all_u, for_u, preferred_element_type=f32)
    fix_w = jnp.einsum("kfr,krc->fc", all_w, for_w, preferred_element_type=f32)
    g_mine = (mine[:part].astype(f32) + fix_u
              + jnp.pad(fix_w, ((0, 0), (rank, 0)))).astype(bf16)
    pairs = [(i, i - 1) for i in range(1, sections)]
    g_next = lax.ppermute(g_mine, "section", pairs)
    g_own = lax.all_gather(g_mine, "dp").reshape(width, 2 * rank)
    g_nxt = lax.all_gather(g_next, "dp").reshape(width, 2 * rank)
    grad_down = g_own[:, :rank]
    grad_up = g_own[:, rank:].T
    down_next, up_next = lax.ppermute((down, upward), "section", pairs)
    new_down = (down_next.astype(f32) - learn_rate * g_nxt[:, :rank].astype(f32)).astype(bf16)
    new_up = (up_next.astype(f32) - learn_rate * g_nxt[:, rank:].T.astype(f32)).astype(bf16)

    hidden = ahead_in.astype(f32)
    unit = hidden * lax.rsqrt(jnp.mean(hidden * hidden, axis=-1, keepdims=True) + eps)
    pre = dot_nn(unit.astype(bf16), new_down)
    last = s == sections - 1
    bump = dot_nn(jax.nn.gelu(pre).astype(bf16), new_up)
    advance = jnp.where(last, hidden, hidden + bump).astype(bf16)
    return (grad_down[None], grad_up[None], advance.reshape(1, micro, batch_rows, width))


def solution(mesh):
    in_specs = (
        P(None, "dp", None),
        P(None, "dp", None),
        P("section", None, None),
        P("section", None, None),
    )
    out_specs = (P("section", None, None), P("section", None, None), P("section", None, "dp", None))
    return jax.shard_map(
        per_device, mesh=mesh, in_specs=in_specs, out_specs=out_specs, check_vma=False
    )
```

time: 1040 us -> 833 us (0.80)
  Pallas kernels: 0 us -> 128 us
  other arithmetic: 125 us -> 8.38 us
  starting transfers between devices: 118 us -> 4.33 us
  matrix products: 71.1 us -> 22.3 us
  waiting for transfers between devices: 643 us -> 612 us
  local copies, waits for them, and re-layouts: 64.2 us -> 42.1 us
    ppermute x40 -> x3, waiting for transfers between devices: 433 us -> 5.8 us  [the longest x1 5.8 us: per_device(): g_next = lax.ppermute(g_mine, 'section', pairs)]
    all_gather x0 -> x5, waiting for transfers between devices: none -> 355 us  [the longest x1 123 us: per_device(): g_own = lax.all_gather(g_mine, 'dp').reshape(width, 2 * rank)]
    pallas_call x0 -> x1, Pallas kernels: none -> 128 us  [recurrence(): pl.pallas_call(functools.partial(recurrence_kernel, sections, chunks), ou...]
    ppermute x40 -> x3, starting transfers between devices: 118 us -> 4.04 us  [the longest x2 2.75 us: per_device(): down_next, up_next = lax.ppermute((down, upward), 'section', pairs)]
    reduce_scatter x0 -> x1, waiting for transfers between devices: none -> 103 us  [per_device(): mine = lax.psum_scatter(packed, 'dp', scatter_dimension=0, tiled=False)]
    dynamic_update_slice x38 -> x0, other arithmetic: 80.6 us -> none  [put_slot(): lax.dynamic_update_index_in_dim(buffer, jnp.where(valid, value, current),...]
    psum x1, waiting for transfers between devices: 210 us -> 148 us  [per_device(): grams = lax.psum(grams, 'dp')]
    dot_general x79 -> x9, matrix products: 71.1 us -> 22.3 us  [the longest x2 8.3 us: dot_nn(): return jnp.dot(a, b, preferred_element_type=f32)]
  transfers between devices with their start and end apart: 41 -> 10, of which waited for: 41 -> 8; matrix products, arithmetic and copies ran while one was open for 1% -> 4% of each run, Pallas kernels for 0% -> 0%
where the time goes in v1:
time: 833 us; the launch traced here: 832 us
  waiting for transfers between devices  612 us (73%)
  Pallas kernels  128 us (15%)
  local copies, waits for them, and re-layouts  42.1 us (5%)
  matrix products  22.3 us (3%)
  between operations  14.4 us (2%)
  other arithmetic  8.38 us (1%)
    psum x1, waiting for transfers between devices, per_device(): grams = lax.psum(grams, 'dp')  148 us
    pallas_call x1, Pallas kernels, recurrence(): pl.pallas_call(functools.partial(recurrence_kernel, sections, chunks), ou...  128 us
    all_gather x1, waiting for transfers between devices, per_device(): g_own = lax.all_gather(g_mine, 'dp').reshape(width, 2 * rank)  123 us
    reduce_scatter x1, waiting for transfers between devices, per_device(): mine = lax.psum_scatter(packed, 'dp', scatter_dimension=0, tiled=False)  103 us
    all_gather x1, waiting for transfers between devices, per_device(): all_u = lax.all_gather(mine_u, 'section')  66.9 us
    all_gather x1, waiting for transfers between devices, per_device(): all_w = lax.all_gather(mine_w, 'section')  61.9 us
    all_gather x1, waiting for transfers between devices, per_device(): g_nxt = lax.all_gather(g_next, 'dp').reshape(width, 2 * rank)  52.9 us
    all_gather x1, waiting for transfers between devices, per_device(): all_cc = lax.all_gather(mine[part:], 'dp')  50.6 us
  transfers between devices with their start and end apart: 10, of which 8 were waited for; matrix products, arithmetic and copies ran while one was open for 4% of the time, Pallas kernels for 0%

profile of v1, /device:TPU:1, one launch (start us, length us, event | category | flops | bytes accessed | tf_op | source)
XLA Modules:
  0.0 832.1 jit_solution(8873381199407401763)
XLA Ops:
  7.2 1.0 constant_dynamic-slice_fusion.1
  8.2 0.8 copy.30
  9.1 0.9 fusion.71
  10.0 66.9 %all-gather.13.cloned.1.call-done = bf16[7168,128]{1,0:T(8,128)(2,1)} async-done(((bf16[448,128]{1,0:T(8,128)(2,1)}), bf16[7168,128]{1,0:T(8,128)(2,1)}) %all-gather.13.cloned.1.call-update) | async-done | bytes 1835024 | tf_op jit(solution)/shard_map/all_gather | solution.py:387
  76.9 3.4 convolution_convert_fusion.2
  80.4 0.5 multiply_reduce_fusion
  80.8 0.1 broadcast_in_dim.31
  80.9 2.3 convolution_bitcast_fusion.3
  83.2 0.7 fusion.18
  83.9 0.8 copy-done.1
  84.7 0.6 copy-done.6
  85.2 0.6 convolution_bitcast_fusion.2
  85.9 148.3 %all-reduce.3.cloned.1.call-done = bf16[16,128,256]{2,1,0:T(8,128)(2,1)} async-done(((bf16[16,128,256]{2,1,0:T(8,128)(2,1)}), bf16[16,128,256]{2,1,0:T(8,128)(2,1)}) %all-reduce.3.cloned.1.call-update) | async-done | bytes 1048592 | tf_op jit(solution)/shard_map/psum | solution.py:391
  234.2 1.4 fusion.61
  235.7 0.1 broadcast_in_dim.32.n0
  235.7 0.3 copy-done.2
  236.0 128.1 %shard_map.67 = (bf16[128,7168]{1,0:T(8,128)(2,1)S(1)}, bf16[128,128]{1,0:T(8,128)(2,1)S(1)}, bf16[128,128]{1,0:T(8,128)(2,1)S(1)}, bf16[16,128,256]{2,1,0:T(8,128)(2,1)S(1)}, f32[128,128]{1,0:T(8,128)S(1)}) custom-call(f32[3,128,128]{2,1,0:T(8,128)S(1)} %pad_maximum_fusion.1.pyh, f32[128,128]{1,0:T(8,128)S(1)} %broadcast_in_dim.32.n0, ...), custom_call_target="tpu_custom_call" | custom-call | tf_op jit(solution)/shard_map/pallas_call | solution.py:338
  364.1 1.3 copy-done.4
  365.5 0.1 slice_reduce_fusion
  365.6 2.1 fusion.6
  367.7 3.9 copy.32
  371.6 1.9 fusion.2
  373.4 3.3 copy.31
  376.7 2.1 convolution_convert_fusion.1
  378.9 2.4 pad_maximum_fusion
  381.4 102.9 %reduce-scatter.2.cloned.1.call-done = bf16[1,576,256]{2,1,0:T(8,128)(2,1)} async-done(((bf16[16,576,256]{2,1,0:T(8,128)(2,1)}), bf16[1,576,256]{2,1,0:T(8,128)(2,1)}) %reduce-scatter.2.cloned.1.call-update) | async-done | bytes 294928 | tf_op jit(solution)/shard_map/reduce_scatter | solution.py:404
  484.3 1.5 slice.49
  485.8 1.6 constant_dynamic-slice_fusion
  487.5 50.6 %all-gather.9.cloned.1.call-done = bf16[16,128,256]{2,1,0:T(8,128)(2,1)} async-done(((bf16[1,128,256]{2,1,0:T(8,128)(2,1)}), bf16[16,128,256]{2,1,0:T(8,128)(2,1)}) %all-gather.9.cloned.1.call-update) | async-done | bytes 1048592 | tf_op jit(solution)/shard_map/all_gather | solution.py:405
  538.1 1.4 broadcast_select_fusion
  539.5 61.9 %all-gather.11.cloned.1.call-done = bf16[16,448,128]{2,1,0:T(8,128)(2,1)} async-done(((bf16[1,448,128]{2,1,0:T(8,128)(2,1)}), bf16[16,448,128]{2,1,0:T(8,128)(2,1)}) %all-gather.11.cloned.1.call-update) | async-done | bytes 1835024 | tf_op jit(solution)/shard_map/all_gather | solution.py:388
  601.4 2.3 convolution_bitcast_fusion.1
  603.8 1.3 fusion.17
  605.2 1.3 collective-permute-start.1
  606.5 5.8 collective-permute-done.1
  612.3 0.7 copy-done.10
  613.0 1.3 collective-permute-start.2
  614.3 3.9 copy.29
  618.3 1.5 collective-permute-start
  619.7 1.9 fusion.3
  621.7 123.1 %all-gather.15.cloned.1.call-done = bf16[7168,256]{1,0:T(8,128)(2,1)} async-done(((bf16[448,256]{1,0:T(8,128)(2,1)}), bf16[7168,256]{1,0:T(8,128)(2,1)}) %all-gather.15.cloned.1.call-update) | async-done | bytes 3670032 | tf_op jit(solution)/shard_map/all_gather | solution.py:418
  744.8 4.1 slice_bitcast_fusion
  748.9 3.9 copy.35
  752.8 52.9 %all-gather.17.cloned.1.call-done = bf16[7168,256]{1,0:T(8,128)(2,1)} async-done(((bf16[448,256]{1,0:T(8,128)(2,1)}), bf16[7168,256]{1,0:T(8,128)(2,1)}) %all-gather.17.cloned.1.call-update) | async-done | bytes 3670032 | tf_op jit(solution)/shard_map/all_gather | solution.py:419
  805.7 4.1 fusion.60
  809.8 3.9 copy.36
  813.7 3.9 copy.37
  817.6 7.6 fusion.1
  (39 shorter events, 0.5 us)
Async XLA Ops:
  7.2 69.7 %all-gather.13.cloned.1.call-start = ((), (), s32[]{:S(2)}) async-start(), calls=%async_computation.5 | async-start | bytes 1949696 | tf_op jit(solution)/shard_map/all_gather | solution.py:387
  9.0 225.2 %all-reduce.3.cloned.1.call-start = ((), (), s32[]{:S(2)}) async-start(), calls=%async_computation.1 | async-start | bytes 2097152 | tf_op jit(solution)/shard_map/psum | solution.py:391
  76.9 3.5 copy-start
  80.3 404.0 %reduce-scatter.2.cloned.1.call-start = ((), (), s32[]{:S(2)}) async-start(), calls=%async_computation.2 | async-start | bytes 5013504 | tf_op jit(solution)/shard_map/reduce_scatter | solution.py:404
  80.9 2.3 copy-start.5
  83.2 1.5 copy-start.1
  83.2 2.0 copy-start.6
  234.2 1.8 copy-start.2
  236.0 129.6 %copy-start.7 = (bf16[4,32,7168]{2,1,0:T(8,128)(2,1)S(1)}, bf16[4,32,7168]{2,1,0:T(8,128)(2,1)}, u32[]{:S(2)}) copy-start(bf16[4,32,7168]{2,1,0:T(8,128)(2,1)} %param.5) | copy-start | bytes 5505028
  364.1 1.3 copy-start.4
  381.3 156.8 %all-gather.9.cloned.1.call-start = ((), (), s32[]{:S(2)}) async-start(), calls=%async_computation.3 | async-start | bytes 1114112 | tf_op jit(solution)/shard_map/all_gather | solution.py:405
  485.8 115.6 %all-gather.11.cloned.1.call-start = ((), (), s32[]{:S(2)}) async-start(), calls=%async_computation.4 | async-start | bytes 1949696 | tf_op jit(solution)/shard_map/all_gather | solution.py:388
  487.4 257.4 %all-gather.15.cloned.1.call-start = ((), (), s32[]{:S(2)}) async-start(), calls=%async_computation.6 | async-start | bytes 3899392 | tf_op jit(solution)/shard_map/all_gather | solution.py:418
  538.1 63.3 %copy-start.9 = (bf16[16,128,256]{2,1,0:T(8,128)(2,1)S(1)}, bf16[16,128,256]{2,1,0:T(8,128)(2,1)}, u32[]{:S(2)}) copy-start(bf16[16,128,256]{2,1,0:T(8,128)(2,1)} %all-gather.9.cloned.1.call-done) | copy-start | bytes 3145732
  539.5 64.3 %copy-start.11 = (bf16[1,576,256]{2,1,0:T(8,128)(2,1)S(1)}, bf16[1,576,256]{2,1,0:T(8,128)(2,1)}, u32[]{:S(2)}) copy-start(bf16[1,576,256]{2,1,0:T(8,128)(2,1)} %reduce-scatter.2.cloned.1.call-done) | copy-start | bytes 884740
  601.4 2.4 copy-start.8
  603.8 9.2 %copy-start.3 = (bf16[1,128,7168]{2,1,0:T(8,128)(2,1)S(1)}, bf16[1,128,7168]{2,1,0:T(8,128)(2,1)}, u32[]{:S(2)}) copy-start(bf16[1,128,7168]{2,1,0:T(8,128)(2,1)} %param.7) | copy-start | bytes 5505028
  605.2 200.5 %all-gather.17.cloned.1.call-start = ((), (), s32[]{:S(2)}) async-start(), calls=%async_computation.7 | async-start | bytes 3899392 | tf_op jit(solution)/shard_map/all_gather | solution.py:419
  605.2 7.1 collective-permute-start.1
  612.3 0.7 copy-start.10
  613.0 204.6 %collective-permute-start.2 = (bf16[128,7168]{1,0:T(8,128)(2,1)S(1)}, bf16[128,7168]{1,0:T(8,128)(2,1)}, u32[]{:S(2)}, u32[]{:S(2)}) collective-permute-start(bf16[128,7168]{1,0:T(8,128)(2,1)S(1)} %bitcast.80), channel_id=1, source_target_pairs={{16,0},{32,16},{48,32},{64,48},{80,64},{96,80},{112,96},{128,112},... | collective-permute-start | bytes 5505032 | tf_op jit(solution)/shard_map/ppermute | solution.py:422
  618.3 199.4 %collective-permute-start = (bf16[7168,128]{0,1:T(8,128)(2,1)}, bf16[7168,128]{0,1:T(8,128)(2,1)}, u32[]{:S(2)}, u32[]{:S(2)}) collective-permute-start(bf16[7168,128]{0,1:T(8,128)(2,1)} %bitcast.84), channel_id=1, source_target_pairs={{16,0},{32,16},{48,32},{64,48},{80,64},{96,80},{112,96},{128,112},... | collective-permute-start | bytes 5505032 | tf_op jit(solution)/shard_map/ppermute | solution.py:422
Sparse Core Ops, SparseCore 0:
  10.4 66.4 all-gather.12
  80.4 153.7 all-reduce.2
  381.4 102.8 reduce-scatter.1
  487.5 50.5 all-gather.8
  540.3 61.0 all-gather.10
  605.3 139.4 all-gather.14
  747.5 58.0 all-gather.16

commit v2 on v1

--- a/solution.py
+++ b/solution.py
@@ -35,11 +35,13 @@
     return value, slope
 
 
-def recurrence_kernel(sections, chunks, pyh, n0, mm, gu, x0, up, xout, u_out, q_out, cc, e_out,
-                      ul, ql, mb, ys, nl, nsend, pacc, yacc, hacc, slope, act, rinv, ecol,
-                      upart, xin, xkeep, xgive,
-                      u_send, u_recv, q_send, q_recv, m_send, m_recv, n_sem, w_sem, c_send, c_recv,
-                      g_send, g_recv):
+def recurrence_kernel(sections, chunks, pyh, n0, mm, gu, x0, g16, up, wd,
+                      xout, gout, u_out, q_out,
+                      ul, ql, mb, ys, nl, nsend, pacc, yacc, hacc, slope, act, rinv, cpair,
+                      upart, wpart, xin, xkeep, xgive, gin, gkeep, ggive,
+                      u_send, u_recv, q_send, q_recv, m_send, m_recv, n_sem,
+                      up_send, up_recv, wp_send, wp_recv, c_send, c_recv, g_send, g_recv,
+                      b_send, b_recv, h_send, h_recv):
     s = lax.axis_index("section")
     rows, width = x0.shape
     rank = up.shape[0]
@@ -73,10 +75,34 @@
     def columns(base, c):
         return pl.ds(pl.multiple_of(base + c * piece, 128), piece)
 
-    def w_copy():
-        return pltpu.make_async_remote_copy(
-            src_ref=up.at[:, pl.ds(pl.multiple_of((1 - ylo) * half, 128), half)],
-            dst_ref=upart, send_sem=w_sem.at[0], recv_sem=w_sem.at[1],
+    def up_copy(c):
+        return pltpu.make_async_remote_copy(
+            src_ref=up.at[:, columns((1 - ylo) * half, c)], dst_ref=upart.at[:, columns(0, c)],
+            send_sem=up_send.at[c], recv_sem=up_recv.at[c],
+            device_id={"section": partner}, device_id_type=MESH)
+
+    def wp_copy(c):
+        return pltpu.make_async_remote_copy(
+            src_ref=wd.at[columns((1 - ylo) * half, c), :], dst_ref=wpart.at[columns(0, c), :],
+            send_sem=wp_send.at[c], recv_sem=wp_recv.at[c],
+            device_id={"section": partner}, device_id_type=MESH)
+
+    def b_copy(c):
+        return pltpu.make_async_remote_copy(
+            src_ref=gkeep.at[:, columns(0, c)], dst_ref=gin.at[:, columns(0, c)],
+            send_sem=b_send.at[c], recv_sem=b_recv.at[c],
+            device_id={"section": peer(sections - 2)}, device_id_type=MESH)
+
+    def h_copy(c):
+        return pltpu.make_async_remote_copy(
+            src_ref=ggive.at[:, columns(0, c)], dst_ref=gout.at[:, columns(ylo * half, c)],
+            send_sem=h_send.at[c], recv_sem=h_recv.at[c],
+            device_id={"section": partner}, device_id_type=MESH)
+
+    def h_arrived(c):
+        return pltpu.make_async_remote_copy(
+            src_ref=ggive.at[:, columns(0, c)], dst_ref=gout.at[:, columns((1 - ylo) * half, c)],
+            send_sem=h_send.at[c], recv_sem=h_recv.at[c],
             device_id={"section": partner}, device_id_type=MESH)
 
     def u_copy(o):
@@ -141,7 +167,6 @@
     pacc[...] = pyh[0]
     yacc[...] = pyh[1]
     hacc[...] = pyh[2]
-    ecol[...] = jnp.zeros_like(ecol)
 
     def chain(t):
         c = t - (2 * z + 3)
@@ -152,10 +177,7 @@
             def _():
                 x_copy(c).wait_recv()
 
-            @pl.when(c == 0)
-            def _():
-                w_copy().wait_recv()
-
+            up_copy(c).wait_recv()
             here = columns(ylo * half, c)
             start = jnp.where(z > 0, xin[:, columns(0, c)], x0[:, here]).astype(f32)
             mine = up[:, here]
@@ -175,6 +197,51 @@
             give_copy(c).start()
             xout[:, here] = jnp.where(first, x_a, x_b)
 
+    def c_of(k):
+        return to_col(ql[k, rows:rows + 1, :].astype(f32) + ql[k, rows + 1:rows + 2, :].astype(f32))
+
+    def chain_back(t):
+        c = t - (sections + 2 + 2 * (sections // 2 - 1 - z))
+
+        @pl.when((c >= 0) & (c < chunks))
+        def _():
+            @pl.when(z < sections // 2 - 1)
+            def _():
+                b_copy(c).wait_recv()
+
+            @pl.when(c == 0)
+            def _():
+                @pl.when(ylo == 1)
+                def _():
+                    q_arrived(2 * z).wait_recv()
+                cpair[0] = jnp.broadcast_to(c_of(2 * z), (rows, rank))
+                cpair[1] = jnp.broadcast_to(c_of(2 * z + 1), (rows, rank))
+
+            wp_copy(c).wait_recv()
+            here = columns(ylo * half, c)
+            there = columns(0, c)
+            first = ylo == 0
+            mine = wd[here, :]
+            other = wpart[there, :]
+            g_b = jnp.where(z < sections // 2 - 1, gin[:, there], g16[:, here])
+            x_a = jnp.where(z > 0, xin[:, there], x0[:, here]).astype(f32)
+            x_b = jnp.where(first, xout[:, here], xgive[:, there]).astype(f32)
+            q_a = ql[2 * z, 0:rows, :]
+            q_b = ql[2 * z + 1, 0:rows, :]
+            g_a = (g_b.astype(f32) + dot_nt(q_b, jnp.where(first, other, mine))
+                   - cpair[1, :, 0:1] * x_b).astype(bf16)
+            g_0 = (g_a.astype(f32) + dot_nt(q_a, jnp.where(first, mine, other))
+                   - cpair[0, :, 0:1] * x_a).astype(bf16)
+
+            @pl.when(z > 0)
+            def _():
+                gkeep[:, there] = g_0
+                b_copy(c).start()
+
+            ggive[:, there] = jnp.where(first, g_b, g_a)
+            h_copy(c).start()
+            gout[:, here] = jnp.where(first, g_a, g_b)
+
     def forward_tick(t, carry):
         k = t - 1
 
@@ -226,8 +293,15 @@
 
         @pl.when(t == 0)
         def _():
-            w_copy().start()
             lax.fori_loop(0, sections, start_m, 0)
+
+        @pl.when(t < chunks)
+        def _():
+            up_copy(t).start()
+
+        @pl.when((t >= 2) & (t < chunks + 2))
+        def _():
+            wp_copy(t - 2).start()
 
         chain(t)
         return carry
@@ -237,15 +311,6 @@
     @pl.when(s != sections - 1)
     def _():
         u_arrived(sections - 1).wait_recv()
-
-    def c_of(k):
-        return to_col(ql[k, rows:rows + 1, :].astype(f32) + ql[k, rows + 1:rows + 2, :].astype(f32))
-
-    def cross(k, head):
-        sum_col = ecol[...]
-        cc[k, :, 0:rank] = head.astype(bf16)
-        mine = ul[s].astype(f32) * sum_col
-        cc[k, :, rank:2 * rank] = (-dot_tn(ul[k], mine.astype(bf16))).astype(bf16)
 
     def backward_tick(t, carry):
         j = 2 * sections - 1 - t
@@ -275,29 +340,29 @@
                 q_copy(s - 1 - i).start()
                 return carry
 
-            lax.fori_loop(0, s, send, 0)
-
-        @pl.when(behind)
-        def _():
-            cross(k, dot_tn(ql[k, 0:rows, :], ul[s]))
-            ecol[...] += jnp.broadcast_to(c_of(k), ecol.shape)
+            @pl.when(s > 0)
+            def _():
+                q_copy(s - 1).start()
+
+            @pl.when(ylo == 0)
+            def _():
+                q_copy(s + 1).start()
+
+            lax.fori_loop(1, s, send, 0)
 
         chain(t)
+        chain_back(t)
         return carry
 
     lax.fori_loop(sections, 2 * sections, backward_tick, 0)
 
-    def tail(k, carry):
-        @pl.when(k <= s)
-        def _():
-            keep = jnp.where(k < s, 1.0, 0.0)
-            cross(k, dot_tn(ul[k], ql[s, 0:rows, :]) * keep)
-        return carry
-
-    lax.fori_loop(0, sections, tail, 0)
+    def drain_tick(t, carry):
+        chain_back(t)
+        return carry
+
+    lax.fori_loop(2 * sections, 2 * sections + chunks, drain_tick, 0)
     u_out[...] = ul[s]
     q_out[...] = ql[s, 0:rows, :]
-    e_out[...] = ecol[...]
 
     def finish(c, carry):
         @pl.when(z < sections // 2 - 1)
@@ -305,6 +370,14 @@
             x_copy(c).wait_send()
         give_copy(c).wait_send()
         give_arrived(c).wait_recv()
+
+        @pl.when(z > 0)
+        def _():
+            b_copy(c).wait_send()
+        h_copy(c).wait_send()
+        h_arrived(c).wait_recv()
+        up_copy(c).wait_send()
+        wp_copy(c).wait_send()
         return carry
 
     lax.fori_loop(0, chunks, finish, 0)
@@ -319,53 +392,311 @@
         return carry
 
     lax.fori_loop(1, sections, settle, 0)
-    w_copy().wait_send()
+
+    @pl.when(ylo == 0)
+    def _():
+        q_copy(s + 1).wait_send()
 
     @pl.when(s < sections - 1)
     def _():
         n_copy().wait_send()
 
 
-def recurrence(sections, pyh, n0, mm, gu, x0, up):
+def recurrence(sections, pyh, n0, mm, gu, x0, g16, up, wd):
     rows, width = x0.shape
     rank = up.shape[0]
     half = width // 2
     chunks = 14
     vm = pl.BlockSpec(memory_space=pltpu.VMEM)
     dma = pltpu.SemaphoreType.DMA
-    block = (sections, rank, rank)
     sq = (rows, rank)
+    wide = jax.ShapeDtypeStruct((rows, width), bf16)
+    strip = pltpu.VMEM((rows, half), bf16)
     return pl.pallas_call(
         functools.partial(recurrence_kernel, sections, chunks),
-        out_shape=(
-            jax.ShapeDtypeStruct((rows, width), bf16),
-            jax.ShapeDtypeStruct(sq, bf16),
-            jax.ShapeDtypeStruct(sq, bf16),
-            jax.ShapeDtypeStruct((sections, rank, 2 * rank), bf16),
-            jax.ShapeDtypeStruct(sq, f32),
-        ),
-        in_specs=[vm] * 6,
-        out_specs=(vm,) * 5,
+        out_shape=(wide, wide, jax.ShapeDtypeStruct(sq, bf16), jax.ShapeDtypeStruct(sq, bf16)),
+        in_specs=[vm] * 8,
+        out_specs=(vm,) * 4,
         scratch_shapes=[
             pltpu.VMEM((sections, rows, rank), bf16),
             pltpu.VMEM((sections, rows + 16, rank), bf16),
-            pltpu.VMEM(block, bf16),
+            pltpu.VMEM((sections, rank, rank), bf16),
             pltpu.VMEM((sections, rows, rank), f32),
             pltpu.VMEM((8, rows), f32),
             pltpu.VMEM((8, rows), f32),
             pltpu.VMEM(sq, f32), pltpu.VMEM(sq, f32), pltpu.VMEM(sq, f32),
-            pltpu.VMEM(sq, f32), pltpu.VMEM(sq, f32), pltpu.VMEM(sq, f32), pltpu.VMEM(sq, f32),
+            pltpu.VMEM(sq, f32), pltpu.VMEM(sq, f32), pltpu.VMEM(sq, f32),
+            pltpu.VMEM((2,) + sq, f32),
             pltpu.VMEM((rank, half), bf16),
-            pltpu.VMEM((rows, half), bf16),
-            pltpu.VMEM((rows, half), bf16),
-            pltpu.VMEM((rows, half), bf16),
-            dma((sections,)), dma((sections,)), dma((sections,)), dma((sections,)),
-            dma((sections,)), dma((sections,)), dma((2,)), dma((2,)),
-            dma((chunks,)), dma((chunks,)), dma((chunks,)), dma((chunks,)),
+            pltpu.VMEM((half, rank), bf16),
+            strip, strip, strip, strip, strip, strip,
+        ] + [dma((sections,))] * 6 + [dma((2,))] + [dma((chunks,))] * 12,
+        compiler_params=pltpu.CompilerParams(
+            collective_id=1, has_side_effects=True, vmem_limit_bytes=48 * 1024 * 1024),
+    )(pyh, n0, mm, gu, x0, g16, up, wd)
+
+
+def reduce_kernel(yh_n, x_n, sections, x1, g1, u_s, q_s, up, base, own, nxt,
+                  part, rc, sums, rax, rby, sa, ray, sb, rbx, gs, nw,
+                  c_send, c_recv, ax_send, ax_recv, s_sem, bx_send, bx_recv,
+                  own_send, own_recv, oc_send, oc_recv, nx_send, nx_recv, ny_send, ny_recv,
+                  nc_send, nc_recv):
+    d = lax.axis_index("dp")
+    s = lax.axis_index("section")
+    yh = d // (2 * x_n)
+    x = lax.rem(d // 2, x_n)
+    core = lax.rem(d, 2)
+    rows = base.shape[0]
+    cut = rows // 2
+
+    def place(y_, x_, c_):
+        return {"dp": (y_ * x_n + x_) * 2 + c_}
+
+    def xp(i):
+        return lax.rem(x + i, x_n)
+
+    other_core = place(yh, x, 1 - core)
+    other_y = place(1 - yh, x, core)
+    up_section = lax.rem(s + 1, sections)
+    down_section = lax.rem(s + sections - 1, sections)
+
+    def copy(src, dst, send, recv, where):
+        return pltpu.make_async_remote_copy(src_ref=src, dst_ref=dst, send_sem=send, recv_sem=recv,
+                                            device_id=where, device_id_type=MESH)
+
+    barrier = pltpu.get_barrier_semaphore()
+    peers = [other_core, other_y, {"section": up_section}, {"section": down_section}]
+    peers += [place(yh, xp(i), core) for i in range(1, x_n)]
+    for where in peers:
+        pl.semaphore_signal(barrier, inc=1, device_id=where, device_id_type=MESH)
+    pl.semaphore_wait(barrier, len(peers))
+
+    def core_copy(b):
+        return copy(part.at[b, 1 - core], rc.at[b], c_send.at[b], c_recv.at[b], other_core)
+
+    def terms(b, carry):
+        cols = pl.ds(pl.multiple_of(b * 2 * rows, 128), 2 * rows)
+        u = u_s[...]
+        before = (x1[:, cols].astype(f32) - dot_nn(u, up[:, cols])).astype(bf16)
+        g_down = dot_tn(before, q_s[...]).astype(bf16)
+        g_up = dot_tn(g1[:, cols], u).astype(bf16)
+        rank = u.shape[1]
+        for half in range(2):
+            part[b, half, :, 0:rank] = g_down[half * rows:(half + 1) * rows]
+            part[b, half, :, rank:2 * rank] = g_up[half * rows:(half + 1) * rows]
+        core_copy(b).start()
+        return carry
+
+    blocks = yh_n * x_n
+    lax.fori_loop(0, blocks, terms, 0)
+
+    def first_sum(b, carry):
+        core_copy(b).wait_recv()
+        y_ = b // x_n
+        x_ = lax.rem(b, x_n)
+        sums[y_, x_] = (part[b, core].astype(f32) + rc[b].astype(f32)).astype(bf16)
+        return carry
+
+    lax.fori_loop(0, blocks, first_sum, 0)
+
+    def ax_copy(i):
+        return copy(sums.at[:, xp(i), 0:cut], rax.at[i - 1], ax_send.at[i - 1], ax_recv.at[i - 1],
+                    place(yh, xp(i), core))
+
+    by_copy = copy(sums.at[1 - yh, :, cut:rows], rby, s_sem.at[0], s_sem.at[1], other_y)
+    ay_copy = copy(sa.at[1 - yh], ray, s_sem.at[2], s_sem.at[3], other_y)
+
+    def bx_copy(i):
+        return copy(sb.at[xp(i)], rbx.at[i - 1], bx_send.at[i - 1], bx_recv.at[i - 1],
+                    place(yh, xp(i), core))
+
+    by_copy.start()
+    for i in range(1, x_n):
+        ax_copy(i).start()
+    for i in range(1, x_n):
+        ax_copy(i).wait_recv()
+    for y_ in range(yh_n):
+        total = sums[y_, x, 0:cut].astype(f32)
+        for i in range(1, x_n):
+            total = total + rax[i - 1, y_].astype(f32)
+        sa[y_] = total.astype(bf16)
+    ay_copy.start()
+    by_copy.wait_recv()
+    for x_ in range(x_n):
+        sb[x_] = (sums[yh, x_, cut:rows].astype(f32) + rby[x_].astype(f32)).astype(bf16)
+    for i in range(1, x_n):
+        bx_copy(i).start()
+    ay_copy.wait_recv()
+    total_a = sa[yh].astype(f32) + ray[...].astype(f32)
+    for i in range(1, x_n):
+        bx_copy(i).wait_recv()
+    total_b = sb[x].astype(f32)
+    for i in range(1, x_n):
+        total_b = total_b + rbx[i - 1].astype(f32)
+    gs[0:cut] = total_a.astype(bf16)
+    gs[cut:rows] = total_b.astype(bf16)
+    nw[...] = (base[...].astype(f32) - learn_rate * gs[...].astype(f32)).astype(bf16)
+
+    has_next = s < sections - 1
+    next_copy = copy(nw, nxt.at[yh, x, core], s_sem.at[4], s_sem.at[5], {"section": down_section})
+    own_y = copy(gs, own.at[yh, x, core], s_sem.at[6], s_sem.at[7], other_y)
+    own_y.start()
+
+    @pl.when(s > 0)
+    def _():
+        next_copy.start()
+
+    own[yh, x, core] = gs[...]
+
+    def own_x(i):
+        return copy(own.at[:, x, core], own.at[:, x, core], own_send.at[i - 1], own_recv.at[i - 1],
+                    place(yh, xp(i), core))
+
+    def own_c(i):
+        spot = own.at[:, xp(i), core]
+        return copy(spot, spot, oc_send.at[i], oc_recv.at[i], other_core)
+
+    own_y.wait_recv()
+    for i in range(1, x_n):
+        own_x(i).start()
+    own_c(0).start()
+
+    def nxt_x(i):
+        spot = nxt.at[yh, x, core]
+        return copy(spot, spot, nx_send.at[i - 1], nx_recv.at[i - 1], place(yh, xp(i), core))
+
+    def nxt_y(i):
+        spot = nxt.at[yh, xp(i), core]
+        return copy(spot, spot, ny_send.at[i], ny_recv.at[i], other_y)
+
+    def nxt_c(i):
+        spot = nxt.at[:, xp(i), core]
+        return copy(spot, spot, nc_send.at[i], nc_recv.at[i], other_core)
+
+    @pl.when(has_next)
+    def _():
+        next_copy.wait_recv()
+        for i in range(1, x_n):
+            nxt_x(i).start()
+        nxt_y(0).start()
+
+    for i in range(1, x_n):
+        own_x(x_n - i).wait_recv()
+        own_c(i).start()
+
+    @pl.when(has_next)
+    def _():
+        for i in range(1, x_n):
+            nxt_x(x_n - i).wait_recv()
+            nxt_y(i).start()
+        for i in range(x_n):
+            nxt_y(i).wait_recv()
+            nxt_c(i).start()
+        for i in range(x_n):
+            nxt_c(i).wait()
+            nxt_y(i).wait_send()
+        for i in range(1, x_n):
+            nxt_x(i).wait_send()
+
+    for i in range(x_n):
+        own_c(i).wait()
+    for i in range(1, x_n):
+        own_x(i).wait_send()
+        ax_copy(i).wait_send()
+        bx_copy(i).wait_send()
+    by_copy.wait_send()
+    ay_copy.wait_send()
+    own_y.wait_send()
+
+    @pl.when(s > 0)
+    def _():
+        next_copy.wait_send()
+
+    def settle(b, carry):
+        core_copy(b).wait_send()
+        return carry
+
+    lax.fori_loop(0, blocks, settle, 0)
+
+
+def reduce_gather(sections, shards, x1, g1, u_s, q_s, up, base):
+    x_n = 4
+    yh_n = shards // (2 * x_n)
+    rows, cols = base.shape
+    cut = rows // 2
+    vm = pl.BlockSpec(memory_space=pltpu.VMEM)
+    dma = pltpu.SemaphoreType.DMA
+    full = jax.ShapeDtypeStruct((yh_n, x_n, 2, rows, cols), bf16)
+
+    def buf(*lead):
+        return pltpu.VMEM(lead + (cols,), bf16)
+
+    return pl.pallas_call(
+        functools.partial(reduce_kernel, yh_n, x_n, sections),
+        out_shape=(full, full),
+        in_specs=[vm] * 6,
+        out_specs=(vm, vm),
+        scratch_shapes=[
+            buf(yh_n * x_n, 2, rows), buf(yh_n * x_n, rows), buf(yh_n, x_n, rows),
+            buf(x_n - 1, yh_n, cut), buf(x_n, cut), buf(yh_n, cut), buf(cut),
+            buf(x_n, cut), buf(x_n - 1, cut), buf(rows), buf(rows),
+            dma((yh_n * x_n,)), dma((yh_n * x_n,)), dma((x_n - 1,)), dma((x_n - 1,)), dma((8,)),
+            dma((x_n - 1,)), dma((x_n - 1,)), dma((x_n - 1,)), dma((x_n - 1,)),
+            dma((x_n,)), dma((x_n,)), dma((x_n - 1,)), dma((x_n - 1,)), dma((x_n,)), dma((x_n,)),
+            dma((x_n,)), dma((x_n,)),
         ],
         compiler_params=pltpu.CompilerParams(
-            collective_id=1, has_side_effects=True, vmem_limit_bytes=40 * 1024 * 1024),
-    )(pyh, n0, mm, gu, x0, up)
+            collective_id=2, has_side_effects=True, vmem_limit_bytes=52 * 1024 * 1024),
+    )(x1, g1, u_s, q_s, up, base)
+
+
+def finish_kernel(sections, own, nxt, x1, grad_down, grad_up, advance):
+    last = lax.axis_index("section") == sections - 1
+    rows, width = x1.shape
+    rank = grad_down.shape[1]
+    step = 896
+    count = width // step
+
+    def first(b, carry):
+        pre, norm = carry
+        here = pl.ds(pl.multiple_of(b * step, 128), step)
+        block = own[here, :]
+        grad_down[here, :] = block[:, 0:rank]
+        grad_up[:, here] = block[:, rank:2 * rank].astype(f32).T.astype(bf16)
+        x = x1[:, here]
+        values = x.astype(f32)
+        pre = pre + dot_nn(x, nxt[here, 0:rank])
+        return pre, norm + jnp.sum(values * values, axis=1, keepdims=True)
+
+    pre, norm = lax.fori_loop(
+        0, count, first, (jnp.zeros((rows, rank), f32), jnp.zeros((rows, 1), f32)))
+    value, unused = gelu_pair(pre * lax.rsqrt(norm * (1.0 / width) + eps))
+    value = value.astype(bf16)
+
+    def second(b, carry):
+        here = pl.ds(pl.multiple_of(b * step, 128), step)
+        bump = dot_nt(value, nxt[here, rank:2 * rank])
+        advance[:, here] = (x1[:, here].astype(f32) + jnp.where(last, 0.0, bump)).astype(bf16)
+        return carry
+
+    lax.fori_loop(0, count, second, 0)
+
+
+def finish(sections, own, nxt, x1):
+    rows, width = x1.shape
+    rank = own.shape[1] // 2
+    vm = pl.BlockSpec(memory_space=pltpu.VMEM)
+    return pl.pallas_call(
+        functools.partial(finish_kernel, sections),
+        out_shape=(
+            jax.ShapeDtypeStruct((width, rank), bf16),
+            jax.ShapeDtypeStruct((rank, width), bf16),
+            jax.ShapeDtypeStruct((rows, width), bf16),
+        ),
+        in_specs=[vm] * 3,
+        out_specs=(vm,) * 3,
+        compiler_params=pltpu.CompilerParams(vmem_limit_bytes=48 * 1024 * 1024),
+    )(own, nxt, x1)
 
 
 def per_device(inputs, cotangent, w_down, w_up):
@@ -385,8 +716,8 @@
     mine_u = lax.dynamic_slice_in_dim(up_t, d * part, part, 0)
     mine_w = lax.dynamic_slice_in_dim(down, d * part, part, 0)
     all_u = lax.all_gather(mine_u, "section")
-    all_w = lax.all_gather(mine_w, "section")
-    grams = jnp.einsum("kfr,fc->krc", all_u, jnp.concatenate([mine_w, mine_u], axis=1),
+    base = jnp.concatenate([mine_w, mine_u], axis=1)
+    grams = jnp.einsum("kfr,fc->krc", all_u, base,
                        preferred_element_type=f32).astype(bf16)
     grams = lax.psum(grams, "dp")
     mm = grams[:, :, :rank]
@@ -396,39 +727,10 @@
     values = x0.astype(f32)
     n0 = jnp.broadcast_to(jnp.sum(values * values, axis=1, keepdims=True), (rows, rank))
 
-    ahead_in, u_s, q_s, cc, e_s = recurrence(sections, pyh, n0, mm, gu, x0, upward)
-
-    mixed = (g16.astype(f32) - e_s[:, 0:1] * values).astype(bf16)
-    g_part = jnp.concatenate([dot_tn(x0, q_s), dot_tn(mixed, u_s)], axis=1).astype(bf16)
-    packed = jnp.concatenate([g_part.reshape(shards, part, 2 * rank), cc], axis=1)
-    mine = lax.psum_scatter(packed, "dp", scatter_dimension=0, tiled=False)
-    all_cc = lax.all_gather(mine[part:], "dp")
-    order = lax.broadcasted_iota(jnp.int32, (sections, 1, 1), 0)
-    s = lax.axis_index("section")
-    head = all_cc[:, :, :rank]
-    zero = jnp.zeros_like(head)
-    for_u = jnp.concatenate([jnp.where(order < s, head, zero), all_cc[:, :, rank:]], axis=2)
-    for_w = jnp.where(order > s, head, zero)
-    fix_u = jnp.einsum("kfr,krc->fc", all_u, for_u, preferred_element_type=f32)
-    fix_w = jnp.einsum("kfr,krc->fc", all_w, for_w, preferred_element_type=f32)
-    g_mine = (mine[:part].astype(f32) + fix_u
-              + jnp.pad(fix_w, ((0, 0), (rank, 0)))).astype(bf16)
-    pairs = [(i, i - 1) for i in range(1, sections)]
-    g_next = lax.ppermute(g_mine, "section", pairs)
-    g_own = lax.all_gather(g_mine, "dp").reshape(width, 2 * rank)
-    g_nxt = lax.all_gather(g_next, "dp").reshape(width, 2 * rank)
-    grad_down = g_own[:, :rank]
-    grad_up = g_own[:, rank:].T
-    down_next, up_next = lax.ppermute((down, upward), "section", pairs)
-    new_down = (down_next.astype(f32) - learn_rate * g_nxt[:, :rank].astype(f32)).astype(bf16)
-    new_up = (up_next.astype(f32) - learn_rate * g_nxt[:, rank:].T.astype(f32)).astype(bf16)
-
-    hidden = ahead_in.astype(f32)
-    unit = hidden * lax.rsqrt(jnp.mean(hidden * hidden, axis=-1, keepdims=True) + eps)
-    pre = dot_nn(unit.astype(bf16), new_down)
-    last = s == sections - 1
-    bump = dot_nn(jax.nn.gelu(pre).astype(bf16), new_up)
-    advance = jnp.where(last, hidden, hidden + bump).astype(bf16)
+    x1, g1, u_s, q_s = recurrence(sections, pyh, n0, mm, gu, x0, g16, upward, down)
+    own, nxt = reduce_gather(sections, shards, x1, g1, u_s, q_s, upward, base)
+    wide = (width, 2 * rank)
+    grad_down, grad_up, advance = finish(sections, own.reshape(wide), nxt.reshape(wide), x1)
     return (grad_down[None], grad_up[None], advance.reshape(1, micro, batch_rows, width))
 
 

time: 833 us -> 514 us (0.62)
  waiting for transfers between devices: 612 us -> 214 us
  Pallas kernels: 128 us -> 267 us
  local copies, waits for them, and re-layouts: 42.1 us -> 9.8 us
  matrix products: 22.3 us -> 6.96 us
    all_gather x4 -> x0, waiting for transfers between devices: 288 us -> none  [the longest x1 123 us: per_device(): g_own = lax.all_gather(g_mine, 'dp').reshape(width, 2 * rank)]
    pallas_call x0 -> x2, Pallas kernels: none -> 122 us  [the longest x1 114 us: reduce_gather(): pl.pallas_call(functools.partial(reduce_kernel, yh_n, x_n, sections), out...]
    reduce_scatter x1 -> x0, waiting for transfers between devices: 103 us -> none  [per_device(): mine = lax.psum_scatter(packed, 'dp', scatter_dimension=0, tiled=False)]
    pallas_call x1, Pallas kernels: 128 us -> 145 us  [recurrence(): pl.pallas_call(functools.partial(recurrence_kernel, sections, chunks), ou...]
    unnamed x28 -> x18, local copies, waits for them, and re-layouts: 19.3 us -> 5.65 us
  transfers between devices with their start and end apart: 10 -> 2, of which waited for: 8 -> 2; matrix products, arithmetic and copies ran while one was open for 4% -> 1% of each run, Pallas kernels for 0% -> 0%
where the time goes in v2:
time: 514 us
  Pallas kernels  267 us (52%)
  waiting for transfers between devices  214 us (42%)
  between operations  14.2 us (3%)
  local copies, waits for them, and re-layouts  9.8 us (2%)
  matrix products  6.96 us (1%)
    psum x1, waiting for transfers between devices, per_device(): grams = lax.psum(grams, 'dp')  149 us
    pallas_call x1, Pallas kernels, recurrence(): pl.pallas_call(functools.partial(recurrence_kernel, sections, chunks), ou...  145 us
    pallas_call x1, Pallas kernels, reduce_gather(): pl.pallas_call(functools.partial(reduce_kernel, yh_n, x_n, sections), out...  114 us
    all_gather x1, waiting for transfers between devices, per_device(): all_u = lax.all_gather(mine_u, 'section')  64.9 us
  transfers between devices with their start and end apart: 2, of which 2 were waited for; matrix products, arithmetic and copies ran while one was open for 1% of the time, Pallas kernels for 0%

profile of v2, /device:TPU:1, one launch (start us, length us, event | category | flops | bytes accessed | tf_op | source)
XLA Modules:
  0.0 514.1 jit_solution(16322054086073518739)
XLA Ops:
  7.2 0.0 all-gather.3.cloned.1.call-start
  7.2 1.0 constant_dynamic-slice_fusion
  8.2 0.8 copy.7
  9.0 0.0 copy-start.8
  9.0 0.0 all-gather.3.cloned.1.call-update
  9.0 0.0 all-reduce.2.cloned.1.call-start
  9.1 2.0 multiply_reduce_fusion
  11.1 0.1 broadcast_in_dim.14
  11.1 0.9 dynamic-slice_bitcast_fusion
  12.0 64.9 %all-gather.3.cloned.1.call-done = bf16[7168,128]{1,0:T(8,128)(2,1)} async-done(((bf16[448,128]{1,0:T(8,128)(2,1)}), bf16[7168,128]{1,0:T(8,128)(2,1)}) %all-gather.3.cloned.1.call-update) | async-done | bytes 1835024 | tf_op jit(solution)/shard_map/all_gather | solution.py:718
  76.9 0.0 copy-done.8
  76.9 0.0 copy-start.4
  76.9 3.4 convolution_convert_fusion
  80.3 0.0 all-reduce.2.cloned.1.call-update
  80.3 0.0 copy-done.4
  80.4 0.0 copy-start.5
  80.4 0.0 copy-start.6
  80.4 2.3 convolution_bitcast_fusion.1
  82.7 0.0 copy-done.5
  82.7 0.3 copy-done.6
  83.0 0.0 copy-start.7
  83.0 0.6 convolution_bitcast_fusion.2
  83.6 0.9 copy-done.7
  84.5 0.6 convolution_bitcast_fusion
  85.2 149.1 %all-reduce.2.cloned.1.call-done = bf16[16,128,256]{2,1,0:T(8,128)(2,1)} async-done(((bf16[16,128,256]{2,1,0:T(8,128)(2,1)}), bf16[16,128,256]{2,1,0:T(8,128)(2,1)}) %all-reduce.2.cloned.1.call-update) | async-done | bytes 1048592 | tf_op jit(solution)/shard_map/psum | solution.py:722
  234.3 1.3 fusion.4
  235.6 0.1 broadcast_in_dim.15.n0
  235.6 145.3 %shard_map.67 = (bf16[128,7168]{1,0:T(8,128)(2,1)S(1)}, bf16[128,7168]{1,0:T(8,128)(2,1)S(1)}, bf16[128,128]{1,0:T(8,128)(2,1)S(1)}, bf16[128,128]{1,0:T(8,128)(2,1)S(1)}) custom-call(f32[3,128,128]{2,1,0:T(8,128)S(1)} %pad_maximum_fusion.1.pyh, f32[128,128]{1,0:T(8,128)S(1)} %broadcast_in_dim.15.n0, bf16[16,128,128]{2,1,0:T(8,128)(2,1)S(1)} %get-tuple-element.22.mm, ...), custom_call_target="tpu_custom_call" | custom-call | tf_op jit(solution)/shard_map/pallas_call | solution.py:415
  381.0 0.0 copy-start
  381.0 1.2 copy-done
  382.2 0.0 copy-start.3
  382.2 1.2 copy-done.3
  383.4 0.0 copy-start.1
  383.4 113.7 %shard_map.68 = (bf16[2,4,2,448,256]{4,3,2,1,0:T(8,128)(2,1)}, bf16[2,4,2,448,256]{4,3,2,1,0:T(8,128)(2,1)}) custom-call(bf16[128,7168]{1,0:T(8,128)(2,1)} %copy-done, bf16[128,7168]{1,0:T(8,128)(2,1)} %copy-done.3, bf16[128,128]{1,0:T(8,128)(2,1)S(1)} %get-tuple-element.14.u_s, bf16[128,128]{1,0:T(8,128)(2,1)S(1)} %get-tuple-element.15.q_s, ...), custom_call_target="tpu_custom_call" | custom-call | tf_op jit(solution)/shard_map/pallas_call | solution.py:634
  497.1 0.0 copy-done.1
  497.1 0.0 copy-start.2
  497.1 2.0 copy-done.2
  499.2 8.1 %shard_map.69 = (bf16[7168,128]{1,0:T(8,128)(2,1)}, bf16[128,7168]{1,0:T(8,128)(2,1)}, bf16[128,7168]{1,0:T(8,128)(2,1)}) custom-call(bf16[7168,256]{1,0:T(8,128)(2,1)S(1)} %bitcast.34, bf16[7168,256]{1,0:T(8,128)(2,1)} %bitcast.43, bf16[128,7168]{1,0:T(8,128)(2,1)S(1)} %copy-done.1), custom_call_target="tpu_custom_call" | custom-call | tf_op jit(solution)/shard_map/pallas_call | solution.py:689
  (2 shorter events, 0.0 us)
Async XLA Ops:
  7.2 69.8 %all-gather.3.cloned.1.call-start = ((), (), s32[]{:S(2)}) async-start(), calls=%async_computation.1 | async-start | bytes 1949696 | tf_op jit(solution)/shard_map/all_gather | solution.py:718
  9.0 67.9 %copy-start.8 = (bf16[1,128,448]{1,2,0:T(8,128)(2,1)S(1)}, bf16[1,128,448]{1,2,0:T(8,128)(2,1)}, u32[]{:S(2)}) copy-start(bf16[1,128,448]{1,2,0:T(8,128)(2,1)} %copy.7) | copy-start | bytes 344068
  9.0 225.2 %all-reduce.2.cloned.1.call-start = ((), (), s32[]{:S(2)}) async-start(), calls=%async_computation | async-start | bytes 2097152 | tf_op jit(solution)/shard_map/psum | solution.py:722
  76.9 3.4 copy-start.4
  80.4 2.3 copy-start.5
  80.4 2.6 copy-start.6
  83.0 1.5 copy-start.7
  381.0 1.2 copy-start
  382.2 1.2 copy-start.3
  383.4 113.7 %copy-start.1 = (bf16[128,7168]{1,0:T(8,128)(2,1)S(1)}, bf16[128,7168]{1,0:T(8,128)(2,1)}, u32[]{:S(2)}) copy-start(bf16[128,7168]{1,0:T(8,128)(2,1)} %copy-done) | copy-start | bytes 5505028
  497.1 2.0 copy-start.2
Sparse Core Ops, SparseCore 0:
  10.4 66.5 all-gather.2
  80.5 153.7 all-reduce.1

commit v3 on v2

--- a/solution.py
+++ b/solution.py
@@ -436,6 +436,277 @@
     )(pyh, n0, mm, gu, x0, g16, up, wd)
 
 
+def dp_place(x_n):
+    d = lax.axis_index("dp")
+    return d // (2 * x_n), lax.rem(d // 2, x_n), lax.rem(d, 2)
+
+
+def remote(src, dst, send, recv, where):
+    return pltpu.make_async_remote_copy(src_ref=src, dst_ref=dst, send_sem=send, recv_sem=recv,
+                                        device_id=where, device_id_type=MESH)
+
+
+def scatter_sum(yh_n, x_n, core_copy, part, rc, sums, rax, rby, sa, ray, sb, rbx,
+                ax_send, ax_recv, s_sem, bx_send, bx_recv):
+    yh, x, core = dp_place(x_n)
+    rows = sums.shape[2]
+    cut = rows // 2
+    blocks = yh_n * x_n
+
+    def place(y_, x_, c_):
+        return {"dp": (y_ * x_n + x_) * 2 + c_}
+
+    def xp(i):
+        return lax.rem(x + i, x_n)
+
+    other_y = place(1 - yh, x, core)
+    copy = remote
+
+    def first_sum(b, carry):
+        core_copy(b).wait_recv()
+        y_ = b // x_n
+        x_ = lax.rem(b, x_n)
+        sums[y_, x_] = (part[b, core].astype(f32) + rc[b].astype(f32)).astype(bf16)
+        return carry
+
+    lax.fori_loop(0, blocks, first_sum, 0)
+
+    def ax_copy(i):
+        return copy(sums.at[:, xp(i), 0:cut], rax.at[i - 1], ax_send.at[i - 1], ax_recv.at[i - 1],
+                    place(yh, xp(i), core))
+
+    by_copy = copy(sums.at[1 - yh, :, cut:rows], rby, s_sem.at[0], s_sem.at[1], other_y)
+    ay_copy = copy(sa.at[1 - yh], ray, s_sem.at[2], s_sem.at[3], other_y)
+
+    def bx_copy(i):
+        return copy(sb.at[xp(i)], rbx.at[i - 1], bx_send.at[i - 1], bx_recv.at[i - 1],
+                    place(yh, xp(i), core))
+
+    by_copy.start()
+    for i in range(1, x_n):
+        ax_copy(i).start()
+    for i in range(1, x_n):
+        ax_copy(i).wait_recv()
+    for y_ in range(yh_n):
+        total = sums[y_, x, 0:cut].astype(f32)
+        for i in range(1, x_n):
+            total = total + rax[i - 1, y_].astype(f32)
+        sa[y_] = total.astype(bf16)
+    ay_copy.start()
+    by_copy.wait_recv()
+    for x_ in range(x_n):
+        sb[x_] = (sums[yh, x_, cut:rows].astype(f32) + rby[x_].astype(f32)).astype(bf16)
+    for i in range(1, x_n):
+        bx_copy(i).start()
+    ay_copy.wait_recv()
+    total_a = sa[yh].astype(f32) + ray[...].astype(f32)
+    for i in range(1, x_n):
+        bx_copy(i).wait_recv()
+    total_b = sb[x].astype(f32)
+    for i in range(1, x_n):
+        total_b = total_b + rbx[i - 1].astype(f32)
+    for i in range(1, x_n):
+        ax_copy(i).wait_send()
+        bx_copy(i).wait_send()
+    by_copy.wait_send()
+    ay_copy.wait_send()
+    return total_a, total_b
+
+
+def gram_kernel(yh_n, x_n, sections, x0, g16, down, up, mine_u, base, pyh, n0, out,
+                allu, part, rc, sums, rax, rby, sa, ray, sb, rbx, gs,
+                z_sem, f_send, f_recv, r_send, r_recv,
+                c_send, c_recv, ax_send, ax_recv, s_sem, bx_send, bx_recv,
+                ga_send, ga_recv, gb_send, gb_recv, gc_send, gc_recv):
+    yh, x, core = dp_place(x_n)
+    s = lax.axis_index("section")
+    z_n = sections // 2
+    z = s // 2
+    ylo = lax.rem(s, 2)
+    rank = up.shape[0]
+    rows = rank
+    cut = rows // 2
+
+    def place(y_, x_, c_):
+        return {"dp": (y_ * x_n + x_) * 2 + c_}
+
+    def xp(i):
+        return lax.rem(x + i, x_n)
+
+    def zp(i):
+        return lax.rem(z + i, z_n)
+
+    other_core = place(yh, x, 1 - core)
+    other_y = place(1 - yh, x, core)
+    partner = {"section": s + 1 - 2 * ylo}
+    after = {"section": 2 * zp(1) + ylo}
+    before = {"section": 2 * zp(z_n - 1) + ylo}
+
+    barrier = pltpu.get_barrier_semaphore()
+    peers = [other_core, other_y, partner, after, before]
+    peers += [place(yh, xp(i), core) for i in range(1, x_n)]
+    for where in peers:
+        pl.semaphore_signal(barrier, inc=1, device_id=where, device_id_type=MESH)
+    pl.semaphore_wait(barrier, len(peers))
+
+    pair = remote(mine_u, allu.at[z, ylo], z_sem.at[0], z_sem.at[1], partner)
+    pair.start()
+    allu[z, ylo] = mine_u[...]
+
+    def products(z_):
+        for y_ in range(2):
+            part[z_, y_] = dot_tn(allu[z_, y_], base[...]).astype(bf16)
+
+    def core_copy(b):
+        return remote(part.at[b, 1 - core], rc.at[b], c_send.at[b], c_recv.at[b], other_core)
+
+    hops = z_n // 2
+
+    def ring_f(i):
+        if i < hops:
+            spot = allu.at[zp(z_n + 1 - i)]
+        else:
+            spot = allu.at[zp(z_n + 1 - i), 0]
+        return remote(spot, spot, f_send.at[i - 1], f_recv.at[i - 1], after)
+
+    def ring_r(i):
+        if i < hops:
+            spot = allu.at[zp(i - 1)]
+        else:
+            spot = allu.at[zp(i - 1), 1]
+        return remote(spot, spot, r_send.at[i - 1], r_recv.at[i - 1], before)
+
+    pair.wait_recv()
+    ring_f(1).start()
+    ring_r(1).start()
+
+    u = up[...]
+    w = down[...]
+    values = x0[...]
+    pyh[0] = dot_nn(values, w)
+    pyh[1] = dot_nt(values, u)
+    pyh[2] = dot_nt(g16[...], u)
+    wide = values.astype(f32)
+    n0[...] = jnp.broadcast_to(jnp.sum(wide * wide, axis=1, keepdims=True), n0.shape)
+    products(z)
+    core_copy(z).start()
+    for i in range(1, hops + 1):
+        ring_f(i).wait_recv()
+        if i < hops:
+            ring_f(i + 1).start()
+        ring_r(i).wait_recv()
+        if i < hops:
+            ring_r(i + 1).start()
+        products(zp(z_n - i))
+        core_copy(zp(z_n - i)).start()
+        if i < hops:
+            products(zp(i))
+            core_copy(zp(i)).start()
+
+    total_a, total_b = scatter_sum(yh_n, x_n, core_copy, part, rc, sums, rax, rby, sa, ray, sb, rbx,
+                                   ax_send, ax_recv, s_sem, bx_send, bx_recv)
+    gs[0:cut] = total_a.astype(bf16)
+    gs[cut:rows] = total_b.astype(bf16)
+    out[yh, x, core] = gs[...]
+
+    low = pl.ds(0, cut)
+    high = pl.ds(cut, cut)
+
+    def spread(src, spot, sems, i, where):
+        return remote(src, spot, sems[0].at[i], sems[1].at[i], where)
+
+    ga = (ga_send, ga_recv)
+    gb = (gb_send, gb_recv)
+    a_y = spread(gs.at[low], out.at[yh, x, core, low], ga, 0, other_y)
+
+    def a_x(i):
+        spot = out.at[:, x, core, low]
+        return spread(spot, spot, ga, i, place(yh, xp(i), core))
+
+    def b_x(i):
+        return spread(gs.at[high], out.at[yh, x, core, high], gb, i - 1, place(yh, xp(i), core))
+
+    def b_y(i):
+        spot = out.at[yh, xp(i), core, high]
+        return spread(spot, spot, gb, x_n - 1 + i, other_y)
+
+    def all_c(i):
+        spot = out.at[:, xp(i), core]
+        return remote(spot, spot, gc_send.at[i], gc_recv.at[i], other_core)
+
+    a_y.start()
+    for i in range(1, x_n):
+        b_x(i).start()
+    b_y(0).start()
+    a_y.wait_recv()
+    for i in range(1, x_n):
+        a_x(i).start()
+    for i in range(1, x_n):
+        b_x(x_n - i).wait_recv()
+        b_y(i).start()
+    b_y(0).wait_recv()
+    all_c(0).start()
+    for i in range(1, x_n):
+        a_x(x_n - i).wait_recv()
+        b_y(i).wait_recv()
+        all_c(i).start()
+    for i in range(x_n):
+        all_c(i).wait()
+        b_y(i).wait_send()
+    for i in range(1, x_n):
+        a_x(i).wait_send()
+        b_x(i).wait_send()
+    a_y.wait_send()
+    pair.wait_send()
+    for i in range(1, hops + 1):
+        ring_f(i).wait_send()
+        ring_r(i).wait_send()
+
+    def settle(b, carry):
+        core_copy(b).wait_send()
+        return carry
+
+    lax.fori_loop(0, yh_n * x_n, settle, 0)
+
+
+def grams_of(sections, shards, x0, g16, down, up, mine_u, base):
+    x_n = 4
+    yh_n = shards // (2 * x_n)
+    rows, width = x0.shape
+    rank = up.shape[0]
+    height = mine_u.shape[0]
+    cut = rank // 2
+    vm = pl.BlockSpec(memory_space=pltpu.VMEM)
+    dma = pltpu.SemaphoreType.DMA
+
+    def buf(*lead):
+        return pltpu.VMEM(lead + (2 * rank,), bf16)
+
+    return pl.pallas_call(
+        functools.partial(gram_kernel, yh_n, x_n, sections),
+        out_shape=(
+            jax.ShapeDtypeStruct((3, rows, rank), f32),
+            jax.ShapeDtypeStruct((rows, rank), f32),
+            jax.ShapeDtypeStruct((yh_n, x_n, 2, rank, 2 * rank), bf16),
+        ),
+        in_specs=[vm] * 6,
+        out_specs=(vm, vm, vm),
+        scratch_shapes=[
+            pltpu.VMEM((sections // 2, 2, height, rank), bf16),
+            buf(yh_n * x_n, 2, rank), buf(yh_n * x_n, rank), buf(yh_n, x_n, rank),
+            buf(x_n - 1, yh_n, cut), buf(x_n, cut), buf(yh_n, cut), buf(cut),
+            buf(x_n, cut), buf(x_n - 1, cut), buf(rank),
+            dma((2,)), dma((sections // 4,)), dma((sections // 4,)),
+            dma((sections // 4,)), dma((sections // 4,)),
+            dma((yh_n * x_n,)), dma((yh_n * x_n,)), dma((x_n - 1,)), dma((x_n - 1,)), dma((4,)),
+            dma((x_n - 1,)), dma((x_n - 1,)),
+            dma((x_n,)), dma((x_n,)), dma((2 * x_n,)), dma((2 * x_n,)), dma((x_n,)), dma((x_n,)),
+        ],
+        compiler_params=pltpu.CompilerParams(
+            collective_id=3, has_side_effects=True, vmem_limit_bytes=48 * 1024 * 1024),
+    )(x0, g16, down, up, mine_u, base)
+
+
 def reduce_kernel(yh_n, x_n, sections, x1, g1, u_s, q_s, up, base, own, nxt,
                   part, rc, sums, rax, rby, sa, ray, sb, rbx, gs, nw,
                   c_send, c_recv, ax_send, ax_recv, s_sem, bx_send, bx_recv,
@@ -490,49 +761,8 @@
     blocks = yh_n * x_n
     lax.fori_loop(0, blocks, terms, 0)
 
-    def first_sum(b, carry):
-        core_copy(b).wait_recv()
-        y_ = b // x_n
-        x_ = lax.rem(b, x_n)
-        sums[y_, x_] = (part[b, core].astype(f32) + rc[b].astype(f32)).astype(bf16)
-        return carry
-
-    lax.fori_loop(0, blocks, first_sum, 0)
-
-    def ax_copy(i):
-        return copy(sums.at[:, xp(i), 0:cut], rax.at[i - 1], ax_send.at[i - 1], ax_recv.at[i - 1],
-                    place(yh, xp(i), core))
-
-    by_copy = copy(sums.at[1 - yh, :, cut:rows], rby, s_sem.at[0], s_sem.at[1], other_y)
-    ay_copy = copy(sa.at[1 - yh], ray, s_sem.at[2], s_sem.at[3], other_y)
-
-    def bx_copy(i):
-        return copy(sb.at[xp(i)], rbx.at[i - 1], bx_send.at[i - 1], bx_recv.at[i - 1],
-                    place(yh, xp(i), core))
-
-    by_copy.start()
-    for i in range(1, x_n):
-        ax_copy(i).start()
-    for i in range(1, x_n):
-        ax_copy(i).wait_recv()
-    for y_ in range(yh_n):
-        total = sums[y_, x, 0:cut].astype(f32)
-        for i in range(1, x_n):
-            total = total + rax[i - 1, y_].astype(f32)
-        sa[y_] = total.astype(bf16)
-    ay_copy.start()
-    by_copy.wait_recv()
-    for x_ in range(x_n):
-        sb[x_] = (sums[yh, x_, cut:rows].astype(f32) + rby[x_].astype(f32)).astype(bf16)
-    for i in range(1, x_n):
-        bx_copy(i).start()
-    ay_copy.wait_recv()
-    total_a = sa[yh].astype(f32) + ray[...].astype(f32)
-    for i in range(1, x_n):
-        bx_copy(i).wait_recv()
-    total_b = sb[x].astype(f32)
-    for i in range(1, x_n):
-        total_b = total_b + rbx[i - 1].astype(f32)
+    total_a, total_b = scatter_sum(yh_n, x_n, core_copy, part, rc, sums, rax, rby, sa, ray, sb, rbx,
+                                   ax_send, ax_recv, s_sem, bx_send, bx_recv)
     gs[0:cut] = total_a.astype(bf16)
     gs[cut:rows] = total_b.astype(bf16)
     nw[...] = (base[...].astype(f32) - learn_rate * gs[...].astype(f32)).astype(bf16)
@@ -602,10 +832,6 @@
         own_c(i).wait()
     for i in range(1, x_n):
         own_x(i).wait_send()
-        ax_copy(i).wait_send()
-        bx_copy(i).wait_send()
-    by_copy.wait_send()
-    ay_copy.wait_send()
     own_y.wait_send()
 
     @pl.when(s > 0)
@@ -715,17 +941,11 @@
 
     mine_u = lax.dynamic_slice_in_dim(up_t, d * part, part, 0)
     mine_w = lax.dynamic_slice_in_dim(down, d * part, part, 0)
-    all_u = lax.all_gather(mine_u, "section")
     base = jnp.concatenate([mine_w, mine_u], axis=1)
-    grams = jnp.einsum("kfr,fc->krc", all_u, base,
-                       preferred_element_type=f32).astype(bf16)
-    grams = lax.psum(grams, "dp")
+    pyh, n0, grams = grams_of(sections, shards, x0, g16, down, upward, mine_u, base)
+    grams = grams.reshape(sections, rank, 2 * rank)
     mm = grams[:, :, :rank]
     gu = grams[:, :, rank:]
-
-    pyh = jnp.stack([dot_nn(x0, down), dot_nt(x0, upward), dot_nt(g16, upward)])
-    values = x0.astype(f32)
-    n0 = jnp.broadcast_to(jnp.sum(values * values, axis=1, keepdims=True), (rows, rank))
 
     x1, g1, u_s, q_s = recurrence(sections, pyh, n0, mm, gu, x0, g16, upward, down)
     own, nxt = reduce_gather(sections, shards, x1, g1, u_s, q_s, upward, base)

time: 514 us -> 335 us (0.65)
  waiting for transfers between devices: 214 us -> 0 us
  Pallas kernels: 267 us -> 325 us
  between operations: 14.2 us -> 0.72 us
  matrix products: 6.96 us -> 0 us
    psum x1 -> x0, waiting for transfers between devices: 149 us -> none  [per_device(): grams = lax.psum(grams, 'dp')]
    all_gather x1 -> x0, waiting for transfers between devices: 64.9 us -> none  [per_device(): all_u = lax.all_gather(mine_u, 'section')]
    pallas_call x0 -> x1, Pallas kernels: none -> 59.2 us  [grams_of(): pl.pallas_call(functools.partial(gram_kernel, yh_n, x_n, sections), out_s...]
    dot_general x4 -> x0, matrix products: 6.96 us -> none  [the longest x1 3.4 us: per_device(): jnp.einsum('kfr,fc->krc', all_u, base, preferred_element_type=f32)]
  transfers between devices with their start and end apart: 2 -> 0, of which waited for: 2 -> 0; matrix products, arithmetic and copies ran while one was open for 1% -> 0% of each run, Pallas kernels for 0% -> 0%
where the time goes in v3:
time: 335 us
  Pallas kernels  325 us (97%)
  local copies, waits for them, and re-layouts  9.83 us (3%)
    pallas_call x1, Pallas kernels, recurrence(): pl.pallas_call(functools.partial(recurrence_kernel, sections, chunks), ou...  142 us
    pallas_call x1, Pallas kernels, reduce_gather(): pl.pallas_call(functools.partial(reduce_kernel, yh_n, x_n, sections), out...  115 us
    pallas_call x1, Pallas kernels, grams_of(): pl.pallas_call(functools.partial(gram_kernel, yh_n, x_n, sections), out_s...  59.2 us
    pallas_call x1, Pallas kernels, finish(): pl.pallas_call(functools.partial(finish_kernel, sections), out_shape=(jax...  8.08 us
    unnamed x12, local copies, waits for them, and re-layouts  7.48 us

profile of v3, /device:TPU:1, one launch (start us, length us, event | category | flops | bytes accessed | tf_op | source)
XLA Modules:
  0.0 335.2 jit_solution(12869296776906792524)
XLA Ops:
  0.6 0.9 dynamic-slice_bitcast_fusion
  1.5 1.0 constant_dynamic-slice_fusion
  2.6 0.1 copy.7
  2.7 0.0 copy-start
  2.8 1.5 copy-done
  4.2 0.0 copy-start.1
  4.2 1.5 copy-done.1
  5.7 59.2 %shard_map.67 = (f32[3,128,128]{2,1,0:T(8,128)S(1)}, f32[128,128]{1,0:T(8,128)S(1)}, bf16[2,4,2,128,256]{4,3,2,1,0:T(8,128)(2,1)S(1)}) custom-call(bf16[128,7168]{1,0:T(8,128)(2,1)S(1)} %bitcast.16, bf16[128,7168]{1,0:T(8,128)(2,1)S(1)} %bitcast.18, bf16[7168,128]{1,0:T(8,128)(2,1)} %bitcast.26, bf16[128,7168]{1,0:T(8,128)(2,1)} %bitcast.23, ...), custom_call_target="tpu_custom_call" | custom-call | tf_op jit(solution)/shard_map/pallas_call | solution.py:685
  65.0 0.3 fusion
  65.3 142.3 %shard_map.68 = (bf16[128,7168]{1,0:T(8,128)(2,1)S(1)}, bf16[128,7168]{1,0:T(8,128)(2,1)S(1)}, bf16[128,128]{1,0:T(8,128)(2,1)S(1)}, bf16[128,128]{1,0:T(8,128)(2,1)S(1)}) custom-call(f32[3,128,128]{2,1,0:T(8,128)S(1)} %get-tuple-element.15.pyh, f32[128,128]{1,0:T(8,128)S(1)} %get-tuple-element.16.n0, bf16[16,128,128]{2,1,0:T(8,128)(2,1)S(1)} %get-tuple-element.28.mm, ...), custom_call_target="tpu_custom_call" | custom-call | tf_op jit(solution)/shard_map/pallas_call | solution.py:415
  207.6 0.0 copy-start.2
  207.6 1.2 copy-done.2
  208.9 0.0 copy-start.5
  208.9 1.2 copy-done.5
  210.1 0.0 copy-start.3
  210.1 115.0 %shard_map.69 = (bf16[2,4,2,448,256]{4,3,2,1,0:T(8,128)(2,1)}, bf16[2,4,2,448,256]{4,3,2,1,0:T(8,128)(2,1)}) custom-call(bf16[128,7168]{1,0:T(8,128)(2,1)} %copy-done.2, bf16[128,7168]{1,0:T(8,128)(2,1)} %copy-done.5, bf16[128,128]{1,0:T(8,128)(2,1)S(1)} %get-tuple-element.20.u_s, bf16[128,128]{1,0:T(8,128)(2,1)S(1)} %get-tuple-element.21.q_s, ...), custom_call_target="tpu_custom_call" | custom-call | tf_op jit(solution)/shard_map/pallas_call | solution.py:860
  325.1 0.0 copy-done.3
  325.1 0.0 copy-start.4
  325.1 2.0 copy-done.4
  327.1 8.1 %shard_map.70 = (bf16[7168,128]{1,0:T(8,128)(2,1)}, bf16[128,7168]{1,0:T(8,128)(2,1)}, bf16[128,7168]{1,0:T(8,128)(2,1)}) custom-call(bf16[7168,256]{1,0:T(8,128)(2,1)S(1)} %bitcast.19, bf16[7168,256]{1,0:T(8,128)(2,1)} %bitcast.28, bf16[128,7168]{1,0:T(8,128)(2,1)S(1)} %copy-done.3), custom_call_target="tpu_custom_call" | custom-call | tf_op jit(solution)/shard_map/pallas_call | solution.py:915
  (1 shorter events, 0.0 us)
Async XLA Ops:
  2.7 1.5 copy-start
  4.2 1.5 copy-start.1
  207.6 1.2 copy-start.2
  208.9 1.2 copy-start.5
  210.1 115.0 %copy-start.3 = (bf16[128,7168]{1,0:T(8,128)(2,1)S(1)}, bf16[128,7168]{1,0:T(8,128)(2,1)}, u32[]{:S(2)}) copy-start(bf16[128,7168]{1,0:T(8,128)(2,1)} %copy-done.2) | copy-start | bytes 5505028
  325.1 2.0 copy-start.4

commit v4 on v3

--- a/solution.py
+++ b/solution.py
@@ -35,36 +35,43 @@
     return value, slope
 
 
-def recurrence_kernel(sections, chunks, pyh, n0, mm, gu, x0, g16, up, wd,
+def recurrence_kernel(sections, chunks, pyh, n0, nn, x0, g16, up, wd,
                       xout, gout, u_out, q_out,
-                      ul, ql, mb, ys, nl, nsend, pacc, yacc, hacc, slope, act, rinv, cpair,
+                      ul, ql, qp, mb, ys, nl, nsend, acc, hacc, slope, act, rinv, uf, qs, cpair,
                       upart, wpart, xin, xkeep, xgive, gin, gkeep, ggive,
-                      u_send, u_recv, q_send, q_recv, m_send, m_recv, n_sem,
+                      u_send, u_recv, q_send, q_recv, m_send, m_recv, e_sem,
                       up_send, up_recv, wp_send, wp_recv, c_send, c_recv, g_send, g_recv,
                       b_send, b_recv, h_send, h_recv):
     s = lax.axis_index("section")
+    planes = sections // 2
     rows, width = x0.shape
+    some = rows // 2
     rank = up.shape[0]
     half = width // 2
     piece = half // chunks
     z = s // 2
     ylo = lax.rem(s, 2)
-    partner = s + 1 - 2 * ylo
+    first = ylo == 0
+    partner = {"section": s + 1 - 2 * ylo}
+    head = slice(0, rank)
+    tail = slice(rank, 2 * rank)
+    mine = pl.ds(ylo * some, some)
+    theirs = pl.ds((1 - ylo) * some, some)
+
+    def plane(i):
+        return {"section": 2 * i + ylo}
 
     def peer(offset):
-        return lax.rem(s + offset, sections)
+        return lax.rem(z + offset, planes)
 
     barrier = pltpu.get_barrier_semaphore()
-
-    def greet(o, carry):
-        pl.semaphore_signal(barrier, inc=1, device_id={"section": peer(o)}, device_id_type=MESH)
-        return carry
-
-    lax.fori_loop(1, sections, greet, 0)
-    pl.semaphore_wait(barrier, sections - 1)
-
-    eye = (lax.broadcasted_iota(jnp.int32, (rows, rows), 0)
-           == lax.broadcasted_iota(jnp.int32, (rows, rows), 1)).astype(f32)
+    for o in range(1, planes):
+        pl.semaphore_signal(barrier, inc=1, device_id=plane(peer(o)), device_id_type=MESH)
+    pl.semaphore_signal(barrier, inc=1, device_id=partner, device_id_type=MESH)
+    pl.semaphore_wait(barrier, planes)
+
+    eye = (lax.broadcasted_iota(jnp.int32, (some, rank), 0)
+           == lax.broadcasted_iota(jnp.int32, (some, rank), 1)).astype(f32)
 
     def to_row(col):
         return jnp.sum(eye * col, axis=0, keepdims=True)
@@ -76,296 +83,312 @@
         return pl.ds(pl.multiple_of(base + c * piece, 128), piece)
 
     def up_copy(c):
-        return pltpu.make_async_remote_copy(
-            src_ref=up.at[:, columns((1 - ylo) * half, c)], dst_ref=upart.at[:, columns(0, c)],
-            send_sem=up_send.at[c], recv_sem=up_recv.at[c],
-            device_id={"section": partner}, device_id_type=MESH)
+        return remote(up.at[:, columns((1 - ylo) * half, c)], upart.at[:, columns(0, c)],
+                      up_send.at[c], up_recv.at[c], partner)
 
     def wp_copy(c):
-        return pltpu.make_async_remote_copy(
-            src_ref=wd.at[columns((1 - ylo) * half, c), :], dst_ref=wpart.at[columns(0, c), :],
-            send_sem=wp_send.at[c], recv_sem=wp_recv.at[c],
-            device_id={"section": partner}, device_id_type=MESH)
+        return remote(wd.at[columns((1 - ylo) * half, c), :], wpart.at[columns(0, c), :],
+                      wp_send.at[c], wp_recv.at[c], partner)
+
+    def x_copy(c):
+        return remote(xkeep.at[:, columns(0, c)], xin.at[:, columns(0, c)],
+                      c_send.at[c], c_recv.at[c], plane(peer(1)))
 
     def b_copy(c):
-        return pltpu.make_async_remote_copy(
-            src_ref=gkeep.at[:, columns(0, c)], dst_ref=gin.at[:, columns(0, c)],
-            send_sem=b_send.at[c], recv_sem=b_recv.at[c],
-            device_id={"section": peer(sections - 2)}, device_id_type=MESH)
+        return remote(gkeep.at[:, columns(0, c)], gin.at[:, columns(0, c)],
+                      b_send.at[c], b_recv.at[c], plane(peer(planes - 1)))
+
+    def give_copy(c):
+        return remote(xgive.at[:, columns(0, c)], xout.at[:, columns(ylo * half, c)],
+                      g_send.at[c], g_recv.at[c], partner)
+
+    def give_arrived(c):
+        return remote(xgive.at[:, columns(0, c)], xout.at[:, columns((1 - ylo) * half, c)],
+                      g_send.at[c], g_recv.at[c], partner)
 
     def h_copy(c):
-        return pltpu.make_async_remote_copy(
-            src_ref=ggive.at[:, columns(0, c)], dst_ref=gout.at[:, columns(ylo * half, c)],
-            send_sem=h_send.at[c], recv_sem=h_recv.at[c],
-            device_id={"section": partner}, device_id_type=MESH)
+        return remote(ggive.at[:, columns(0, c)], gout.at[:, columns(ylo * half, c)],
+                      h_send.at[c], h_recv.at[c], partner)
 
     def h_arrived(c):
-        return pltpu.make_async_remote_copy(
-            src_ref=ggive.at[:, columns(0, c)], dst_ref=gout.at[:, columns((1 - ylo) * half, c)],
-            send_sem=h_send.at[c], recv_sem=h_recv.at[c],
-            device_id={"section": partner}, device_id_type=MESH)
+        return remote(ggive.at[:, columns(0, c)], gout.at[:, columns((1 - ylo) * half, c)],
+                      h_send.at[c], h_recv.at[c], partner)
+
+    def near_copy(k, part, sem):
+        spot = ul.at[k, :, part]
+        return remote(spot, spot, e_sem.at[2 * sem], e_sem.at[2 * sem + 1], plane(peer(1)))
+
+    def n_copy():
+        return remote(nsend, nl, e_sem.at[4], e_sem.at[5], plane(peer(1)))
+
+    def uf_copy():
+        return remote(ul.at[z], uf.at[mine], e_sem.at[6], e_sem.at[7], partner)
+
+    def uf_arrived():
+        return remote(ul.at[z], uf.at[theirs], e_sem.at[6], e_sem.at[7], partner)
+
+    def qp_copy():
+        return remote(ql.at[z], qp, e_sem.at[8], e_sem.at[9], partner)
 
     def u_copy(o):
-        return pltpu.make_async_remote_copy(
-            src_ref=ul.at[s], dst_ref=ul.at[s], send_sem=u_send.at[o], recv_sem=u_recv.at[s],
-            device_id={"section": peer(o)}, device_id_type=MESH)
+        return remote(ul.at[z], ul.at[z], u_send.at[o], u_recv.at[z], plane(peer(o)))
 
     def u_arrived(k):
-        return pltpu.make_async_remote_copy(
-            src_ref=ul.at[k], dst_ref=ul.at[k], send_sem=u_send.at[0], recv_sem=u_recv.at[k],
-            device_id={"section": partner}, device_id_type=MESH)
+        return remote(ul.at[k], ul.at[k], u_send.at[0], u_recv.at[k], plane(peer(1)))
 
     def q_copy(j):
-        return pltpu.make_async_remote_copy(
-            src_ref=ql.at[s], dst_ref=ql.at[s], send_sem=q_send.at[j], recv_sem=q_recv.at[s],
-            device_id={"section": j}, device_id_type=MESH)
+        return remote(ql.at[z], ql.at[z], q_send.at[j], q_recv.at[z], plane(j))
 
     def q_arrived(k):
-        return pltpu.make_async_remote_copy(
-            src_ref=ql.at[k], dst_ref=ql.at[k], send_sem=q_send.at[0], recv_sem=q_recv.at[k],
-            device_id={"section": partner}, device_id_type=MESH)
+        return remote(ql.at[k], ql.at[k], q_send.at[0], q_recv.at[k], plane(peer(1)))
 
     def m_copy(j):
-        return pltpu.make_async_remote_copy(
-            src_ref=mm.at[j], dst_ref=mb.at[s], send_sem=m_send.at[j], recv_sem=m_recv.at[s],
-            device_id={"section": j}, device_id_type=MESH)
+        return remote(nn.at[j, :, 0:2 * rank], mb.at[z], m_send.at[j], m_recv.at[z], plane(j))
 
     def m_arrived(k):
-        return pltpu.make_async_remote_copy(
-            src_ref=mb.at[k], dst_ref=mb.at[k], send_sem=m_send.at[0], recv_sem=m_recv.at[k],
-            device_id={"section": partner}, device_id_type=MESH)
-
-    def n_copy():
-        return pltpu.make_async_remote_copy(
-            src_ref=nsend, dst_ref=nl, send_sem=n_sem.at[0], recv_sem=n_sem.at[1],
-            device_id={"section": peer(1)}, device_id_type=MESH)
-
-    def x_copy(c):
-        return pltpu.make_async_remote_copy(
-            src_ref=xkeep.at[:, columns(0, c)], dst_ref=xin.at[:, columns(0, c)],
-            send_sem=c_send.at[c], recv_sem=c_recv.at[c],
-            device_id={"section": peer(2)}, device_id_type=MESH)
-
-    def give_copy(c):
-        return pltpu.make_async_remote_copy(
-            src_ref=xgive.at[:, columns(0, c)], dst_ref=xout.at[:, columns(ylo * half, c)],
-            send_sem=g_send.at[c], recv_sem=g_recv.at[c],
-            device_id={"section": partner}, device_id_type=MESH)
-
-    def give_arrived(c):
-        return pltpu.make_async_remote_copy(
-            src_ref=xgive.at[:, columns(0, c)], dst_ref=xout.at[:, columns((1 - ylo) * half, c)],
-            send_sem=g_send.at[c], recv_sem=g_recv.at[c],
-            device_id={"section": partner}, device_id_type=MESH)
+        return remote(mb.at[k], mb.at[k], m_send.at[0], m_recv.at[k], plane(peer(1)))
+
+    acc[:, 0:2 * rank] = pyh[0]
+    acc[:, 2 * rank:4 * rank] = pyh[1]
+    hacc[...] = pyh[2]
+
+    def start_up(c, carry):
+        up_copy(c).start()
+        return carry
+
+    lax.fori_loop(0, chunks, start_up, 0)
 
     def start_m(j, carry):
-        @pl.when(j < s)
-        def _():
-            m_copy(j).start()
+        m_copy(j).start()
         return carry
 
-    pacc[...] = pyh[0]
-    yacc[...] = pyh[1]
-    hacc[...] = pyh[2]
-
-    def chain(t):
-        c = t - (2 * z + 3)
-
-        @pl.when((c >= 0) & (c < chunks))
-        def _():
-            @pl.when(z > 0)
+    lax.fori_loop(0, z, start_m, 0)
+
+    def chain(c):
+        @pl.when(z > 0)
+        def _():
+            x_copy(c).wait_recv()
+
+        up_copy(c).wait_recv()
+        here = columns(ylo * half, c)
+        there = columns(0, c)
+        start = jnp.where(z > 0, xin[:, there], x0[:, here]).astype(f32)
+        ours = up[:, here]
+        other = upart[:, there]
+        x_a = (start + dot_nn(uf[:, head], jnp.where(first, ours, other))).astype(bf16)
+        x_b = (x_a.astype(f32) + dot_nn(uf[:, tail], jnp.where(first, other, ours))).astype(bf16)
+        xkeep[:, there] = x_b
+
+        @pl.when(z < planes - 1)
+        def _():
+            x_copy(c).start()
+
+        xgive[:, there] = jnp.where(first, x_b, x_a)
+        give_copy(c).start()
+        xout[:, here] = jnp.where(first, x_a, x_b)
+
+    def chain_back(c):
+        @pl.when(z < planes - 1)
+        def _():
+            b_copy(c).wait_recv()
+
+        wp_copy(c).wait_recv()
+        here = columns(ylo * half, c)
+        there = columns(0, c)
+        ours = wd[here, :]
+        other = wpart[there, :]
+        g_b = jnp.where(z < planes - 1, gin[:, there], g16[:, here])
+        x_a = jnp.where(z > 0, xin[:, there], x0[:, here]).astype(f32)
+        x_b = jnp.where(first, xout[:, here], xgive[:, there]).astype(f32)
+        g_a = (g_b.astype(f32) + dot_nt(qs[:, tail], jnp.where(first, other, ours))
+               - cpair[1, :, 0:1] * x_b).astype(bf16)
+        g_0 = (g_a.astype(f32) + dot_nt(qs[:, head], jnp.where(first, ours, other))
+               - cpair[0, :, 0:1] * x_a).astype(bf16)
+
+        @pl.when(z > 0)
+        def _():
+            gkeep[:, there] = g_0
+            b_copy(c).start()
+
+        ggive[:, there] = jnp.where(first, g_b, g_a)
+        h_copy(c).start()
+        gout[:, here] = jnp.where(first, g_a, g_b)
+
+    def forward_own():
+        @pl.when(z > 0)
+        def _():
+            n_copy().wait_recv()
+
+        norm_a = jnp.where(z > 0, to_col(nl[0:1, :]), n0[:, 0:1])
+        scale_a = lax.rsqrt(norm_a * (1.0 / width) + eps)
+        pre_a = acc[:, 0:rank] * scale_a
+        value_a, slope_a = gelu_pair(pre_a)
+        u_a = value_a.astype(bf16)
+        ul[z, :, head] = u_a
+
+        @pl.when(z < planes - 1)
+        def _():
+            near_copy(z, head, 0).start()
+
+        step = dot_nn(u_a, nn[z, 0:rank, rank:4 * rank])
+        y_a = acc[:, 2 * rank:3 * rank]
+        norm_b = norm_a + jnp.sum(u_a.astype(f32) * (2.0 * y_a + step[:, rank:2 * rank]),
+                                  axis=1, keepdims=True)
+        scale_b = lax.rsqrt(norm_b * (1.0 / width) + eps)
+        pre_b = (acc[:, rank:2 * rank] + step[:, 0:rank]) * scale_b
+        value_b, slope_b = gelu_pair(pre_b)
+        u_b = value_b.astype(bf16)
+        ul[z, :, tail] = u_b
+
+        @pl.when(z < planes - 1)
+        def _():
+            near_copy(z, tail, 1).start()
+
+        y_b = acc[:, 2 * rank:4 * rank] + step[:, rank:3 * rank]
+        more = dot_nn(u_b, nn[z, rank:2 * rank, 2 * rank:4 * rank])
+        norm_c = norm_b + jnp.sum(
+            u_b.astype(f32) * (2.0 * y_b[:, rank:2 * rank] + more[:, rank:2 * rank]),
+            axis=1, keepdims=True)
+
+        @pl.when(z < planes - 1)
+        def _():
+            nsend[...] = jnp.broadcast_to(to_row(norm_c), nsend.shape)
+            n_copy().start()
+
+        uf_copy().start()
+        for o in range(2, planes):
+            u_copy(o).start()
+
+        @pl.when(z == planes - 1)
+        def _():
+            u_copy(1).start()
+
+        uf[mine, :] = ul[z]
+        ys[2 * z + 1] = y_b
+        acc[:, 2 * rank:4 * rank] = y_b + more
+        act[:, head] = pre_a
+        act[:, tail] = pre_b
+        slope[:, head] = slope_a
+        slope[:, tail] = slope_b
+        rinv[0] = jnp.broadcast_to(scale_a, (some, rank))
+        rinv[1] = jnp.broadcast_to(scale_b, (some, rank))
+
+    def c_of(stat):
+        line = stat[0:1, :].astype(f32) + stat[1:2, :].astype(f32)
+        return to_col(line[:, head]), to_col(line[:, tail])
+
+    def backward_own():
+        scale_b = rinv[1]
+        q_b = hacc[:, tail] * slope[:, tail]
+        low_b = (q_b * scale_b).astype(bf16)
+        mix_b = jnp.sum(q_b * act[:, tail], axis=1, keepdims=True) * (1.0 / width)
+        c_b = mix_b * scale_b[:, 0:1] * scale_b[:, 0:1]
+        h_a = hacc[:, head] + dot_nt(low_b, nn[z, 0:rank, rank:2 * rank]) - c_b * ys[2 * z + 1, :, head]
+        scale_a = rinv[0]
+        q_a = h_a * slope[:, head]
+        mix_a = jnp.sum(q_a * act[:, head], axis=1, keepdims=True) * (1.0 / width)
+        c_a = mix_a * scale_a[:, 0:1] * scale_a[:, 0:1]
+        ql[z, 0:some, head] = (q_a * scale_a).astype(bf16)
+        ql[z, 0:some, tail] = low_b
+        spot = lax.broadcasted_iota(jnp.int32, (16, rank), 0)
+        for part, col in ((head, c_a), (tail, c_b)):
+            line = to_row(col)
+            high = line.astype(bf16).astype(f32)
+            ql[z, some:some + 16, part] = jnp.where(
+                spot == 0, high, jnp.where(spot == 1, line - high, 0.0)).astype(bf16)
+
+        def send(i, carry):
+            q_copy(z - 1 - i).start()
+            return carry
+
+        lax.fori_loop(0, z, send, 0)
+        qp_copy().start()
+
+    def tick(t, carry):
+        k = t - 1
+        sent = (k >= 0) & (k < planes)
+        near = sent & (k == z - 1)
+
+        @pl.when(sent & (k != z) & (k != z - 1))
+        def _():
+            u_arrived(k).wait_recv()
+
+        @pl.when(near)
+        def _():
+            near_copy(k, head, 0).wait_recv()
+            acc[...] += dot_nn(ul[k, :, head], nn[k, 0:rank, :])
+            near_copy(k, tail, 1).wait_recv()
+            acc[...] += dot_nn(ul[k, :, tail], nn[k, rank:2 * rank, :])
+
+        @pl.when(sent & (k < z - 1))
+        def _():
+            acc[...] += dot_nn(ul[k], nn[k])
+
+        @pl.when(t == z)
+        def _():
+            forward_own()
+
+        @pl.when(sent & (k > z))
+        def _():
+            before = acc[:, 2 * rank:4 * rank]
+            ys[2 * k] = before
+            between = before + dot_nn(ul[k, :, head], nn[k, 0:rank, 2 * rank:4 * rank])
+            ys[2 * k + 1] = between
+            acc[:, 2 * rank:4 * rank] = between + dot_nn(
+                ul[k, :, tail], nn[k, rank:2 * rank, 2 * rank:4 * rank])
+
+        r = 2 * planes - t
+
+        @pl.when((r < planes) & (r > z))
+        def _():
+            m_arrived(r).wait_recv()
+            q_arrived(r).wait_recv()
+            c_a, c_b = c_of(ql[r, some:some + 16, :])
+            hacc[...] += (dot_nt(ql[r, 0:some, :], mb[r]) - c_a * ys[2 * r] - c_b * ys[2 * r + 1])
+
+        @pl.when(t == 2 * planes - 1 - z)
+        def _():
+            backward_own()
+
+        p = t - (z + 1)
+
+        @pl.when((p >= 0) & (p < chunks // 2))
+        def _():
+            @pl.when(p == 0)
             def _():
-                x_copy(c).wait_recv()
-
-            up_copy(c).wait_recv()
-            here = columns(ylo * half, c)
-            start = jnp.where(z > 0, xin[:, columns(0, c)], x0[:, here]).astype(f32)
-            mine = up[:, here]
-            other = upart[:, columns(0, c)]
-            first = ylo == 0
-            u_a = ul[2 * z]
-            u_b = ul[2 * z + 1]
-            x_a = (start + dot_nn(u_a, jnp.where(first, mine, other))).astype(bf16)
-            x_b = (x_a.astype(f32) + dot_nn(u_b, jnp.where(first, other, mine))).astype(bf16)
-            xkeep[:, columns(0, c)] = x_b
-
-            @pl.when(z < sections // 2 - 1)
+                uf_arrived().wait_recv()
+            for j in range(2):
+                chain(2 * p + j)
+
+        @pl.when((t >= 2) & (t < 2 + chunks // 2))
+        def _():
+            for j in range(2):
+                wp_copy(2 * (t - 2) + j).start()
+
+        b = t - (2 * planes - z)
+
+        @pl.when((b >= 0) & (b < chunks // 2))
+        def _():
+            @pl.when(b == 0)
             def _():
-                x_copy(c).start()
-
-            xgive[:, columns(0, c)] = jnp.where(first, x_b, x_a)
-            give_copy(c).start()
-            xout[:, here] = jnp.where(first, x_a, x_b)
-
-    def c_of(k):
-        return to_col(ql[k, rows:rows + 1, :].astype(f32) + ql[k, rows + 1:rows + 2, :].astype(f32))
-
-    def chain_back(t):
-        c = t - (sections + 2 + 2 * (sections // 2 - 1 - z))
-
-        @pl.when((c >= 0) & (c < chunks))
-        def _():
-            @pl.when(z < sections // 2 - 1)
-            def _():
-                b_copy(c).wait_recv()
-
-            @pl.when(c == 0)
-            def _():
-                @pl.when(ylo == 1)
-                def _():
-                    q_arrived(2 * z).wait_recv()
-                cpair[0] = jnp.broadcast_to(c_of(2 * z), (rows, rank))
-                cpair[1] = jnp.broadcast_to(c_of(2 * z + 1), (rows, rank))
-
-            wp_copy(c).wait_recv()
-            here = columns(ylo * half, c)
-            there = columns(0, c)
-            first = ylo == 0
-            mine = wd[here, :]
-            other = wpart[there, :]
-            g_b = jnp.where(z < sections // 2 - 1, gin[:, there], g16[:, here])
-            x_a = jnp.where(z > 0, xin[:, there], x0[:, here]).astype(f32)
-            x_b = jnp.where(first, xout[:, here], xgive[:, there]).astype(f32)
-            q_a = ql[2 * z, 0:rows, :]
-            q_b = ql[2 * z + 1, 0:rows, :]
-            g_a = (g_b.astype(f32) + dot_nt(q_b, jnp.where(first, other, mine))
-                   - cpair[1, :, 0:1] * x_b).astype(bf16)
-            g_0 = (g_a.astype(f32) + dot_nt(q_a, jnp.where(first, mine, other))
-                   - cpair[0, :, 0:1] * x_a).astype(bf16)
-
-            @pl.when(z > 0)
-            def _():
-                gkeep[:, there] = g_0
-                b_copy(c).start()
-
-            ggive[:, there] = jnp.where(first, g_b, g_a)
-            h_copy(c).start()
-            gout[:, here] = jnp.where(first, g_a, g_b)
-
-    def forward_tick(t, carry):
-        k = t - 1
-
-        @pl.when((t > 0) & (k != s))
-        def _():
-            u_arrived(k).wait_recv()
-
-        @pl.when((t > 0) & (k < s))
-        def _():
-            pacc[...] += dot_nn(ul[k], mm[k])
-
-        @pl.when(t == s)
-        def _():
-            @pl.when(s > 0)
-            def _():
-                n_copy().wait_recv()
-
-            norm = jnp.where(s > 0, to_col(nl[0:1, :]), n0[:, 0:1])
-            scale = lax.rsqrt(norm * (1.0 / width) + eps)
-            pre = pacc[...] * scale
-            value, grad = gelu_pair(pre)
-            ul[s] = value.astype(bf16)
-
-            def send(o, carry):
-                u_copy(o).start()
-                return carry
-
-            lax.fori_loop(1, sections, send, 0)
-            act[...] = pre
-            slope[...] = grad
-            rinv[...] = jnp.broadcast_to(scale, rinv.shape)
-
-        @pl.when((t > 0) & (k > s))
-        def _():
-            ys[k] = yacc[...]
-
-        @pl.when(t > 0)
-        def _():
-            yacc[...] += dot_nn(ul[k], gu[k])
-
-        @pl.when((t == s) & (s < sections - 1))
-        def _():
-            mine = ul[s]
-            norm = jnp.where(s > 0, to_col(nl[0:1, :]), n0[:, 0:1])
-            grown = norm + jnp.sum(
-                mine.astype(f32) * (2.0 * yacc[...] + dot_nn(mine, gu[s])), axis=1, keepdims=True)
-            nsend[...] = jnp.broadcast_to(to_row(grown), nsend.shape)
-            n_copy().start()
-
-        @pl.when(t == 0)
-        def _():
-            lax.fori_loop(0, sections, start_m, 0)
-
-        @pl.when(t < chunks)
-        def _():
-            up_copy(t).start()
-
-        @pl.when((t >= 2) & (t < chunks + 2))
-        def _():
-            wp_copy(t - 2).start()
-
-        chain(t)
+                qp_copy().wait_recv()
+                qs[mine, :] = ql[z, 0:some, :]
+                qs[theirs, :] = qp[0:some, :]
+                for where, stat in ((mine, ql[z, some:some + 16, :]), (theirs, qp[some:some + 16, :])):
+                    c_a, c_b = c_of(stat)
+                    cpair[0, where, :] = jnp.broadcast_to(c_a, (some, rank))
+                    cpair[1, where, :] = jnp.broadcast_to(c_b, (some, rank))
+            for j in range(2):
+                chain_back(2 * b + j)
+
         return carry
 
-    lax.fori_loop(0, sections, forward_tick, 0)
-
-    @pl.when(s != sections - 1)
-    def _():
-        u_arrived(sections - 1).wait_recv()
-
-    def backward_tick(t, carry):
-        j = 2 * sections - 1 - t
-        k = j + 1
-        behind = (k < sections) & (k > s)
-
-        @pl.when(behind)
-        def _():
-            m_arrived(k).wait_recv()
-            q_arrived(k).wait_recv()
-            hacc[...] += dot_nt(ql[k, 0:rows, :], mb[k]) - c_of(k) * ys[k]
-
-        @pl.when(s == j)
-        def _():
-            q = hacc[...] * slope[...]
-            scale = rinv[...]
-            ql[s, 0:rows, :] = (q * scale).astype(bf16)
-            mix = jnp.sum(q * act[...], axis=1, keepdims=True) * (1.0 / width)
-            line = to_row(mix * scale[:, 0:1] * scale[:, 0:1])
-            high = line.astype(bf16)
-            low = (line - high.astype(f32)).astype(bf16)
-            spot = lax.broadcasted_iota(jnp.int32, (16, rows), 0)
-            ql[s, rows:rows + 16, :] = jnp.where(
-                spot == 0, high.astype(f32), jnp.where(spot == 1, low.astype(f32), 0.0)).astype(bf16)
-
-            def send(i, carry):
-                q_copy(s - 1 - i).start()
-                return carry
-
-            @pl.when(s > 0)
-            def _():
-                q_copy(s - 1).start()
-
-            @pl.when(ylo == 0)
-            def _():
-                q_copy(s + 1).start()
-
-            lax.fori_loop(1, s, send, 0)
-
-        chain(t)
-        chain_back(t)
-        return carry
-
-    lax.fori_loop(sections, 2 * sections, backward_tick, 0)
-
-    def drain_tick(t, carry):
-        chain_back(t)
-        return carry
-
-    lax.fori_loop(2 * sections, 2 * sections + chunks, drain_tick, 0)
-    u_out[...] = ul[s]
-    q_out[...] = ql[s, 0:rows, :]
+    lax.fori_loop(0, 2 * planes + chunks // 2, tick, 0)
+    u_out[...] = jnp.where(first, uf[:, head], uf[:, tail])
+    q_out[...] = jnp.where(first, qs[:, head], qs[:, tail])
 
     def finish(c, carry):
-        @pl.when(z < sections // 2 - 1)
+        @pl.when(z < planes - 1)
         def _():
             x_copy(c).wait_send()
         give_copy(c).wait_send()
@@ -381,59 +404,68 @@
         return carry
 
     lax.fori_loop(0, chunks, finish, 0)
-
-    def settle(o, carry):
+    for o in range(2, planes):
         u_copy(o).wait_send()
 
-        @pl.when(o - 1 < s)
-        def _():
-            q_copy(o - 1).wait_send()
-            m_copy(o - 1).wait_send()
+    @pl.when(z == planes - 1)
+    def _():
+        u_copy(1).wait_send()
+
+    @pl.when(z < planes - 1)
+    def _():
+        near_copy(z, head, 0).wait_send()
+        near_copy(z, tail, 1).wait_send()
+        n_copy().wait_send()
+
+    def settle(j, carry):
+        q_copy(j).wait_send()
+        m_copy(j).wait_send()
         return carry
 
-    lax.fori_loop(1, sections, settle, 0)
-
-    @pl.when(ylo == 0)
-    def _():
-        q_copy(s + 1).wait_send()
-
-    @pl.when(s < sections - 1)
-    def _():
-        n_copy().wait_send()
-
-
-def recurrence(sections, pyh, n0, mm, gu, x0, g16, up, wd):
+    lax.fori_loop(0, z, settle, 0)
+    uf_copy().wait_send()
+    qp_copy().wait_send()
+
+
+def recurrence(sections, pyh, n0, nn, x0, g16, up, wd):
     rows, width = x0.shape
     rank = up.shape[0]
     half = width // 2
+    some = rows // 2
+    planes = sections // 2
     chunks = 14
     vm = pl.BlockSpec(memory_space=pltpu.VMEM)
     dma = pltpu.SemaphoreType.DMA
     sq = (rows, rank)
+    two = (some, 2 * rank)
     wide = jax.ShapeDtypeStruct((rows, width), bf16)
     strip = pltpu.VMEM((rows, half), bf16)
     return pl.pallas_call(
         functools.partial(recurrence_kernel, sections, chunks),
         out_shape=(wide, wide, jax.ShapeDtypeStruct(sq, bf16), jax.ShapeDtypeStruct(sq, bf16)),
-        in_specs=[vm] * 8,
+        in_specs=[vm] * 7,
         out_specs=(vm,) * 4,
         scratch_shapes=[
-            pltpu.VMEM((sections, rows, rank), bf16),
-            pltpu.VMEM((sections, rows + 16, rank), bf16),
-            pltpu.VMEM((sections, rank, rank), bf16),
-            pltpu.VMEM((sections, rows, rank), f32),
-            pltpu.VMEM((8, rows), f32),
-            pltpu.VMEM((8, rows), f32),
-            pltpu.VMEM(sq, f32), pltpu.VMEM(sq, f32), pltpu.VMEM(sq, f32),
-            pltpu.VMEM(sq, f32), pltpu.VMEM(sq, f32), pltpu.VMEM(sq, f32),
+            pltpu.VMEM((planes,) + two, bf16),
+            pltpu.VMEM((planes, some + 16, 2 * rank), bf16),
+            pltpu.VMEM((some + 16, 2 * rank), bf16),
+            pltpu.VMEM((planes, 2 * rank, 2 * rank), bf16),
+            pltpu.VMEM((sections,) + two, f32),
+            pltpu.VMEM((8, rank), f32),
+            pltpu.VMEM((8, rank), f32),
+            pltpu.VMEM((some, 4 * rank), f32),
+            pltpu.VMEM(two, f32), pltpu.VMEM(two, f32), pltpu.VMEM(two, f32),
+            pltpu.VMEM((2, some, rank), f32),
+            pltpu.VMEM((rows, 2 * rank), bf16),
+            pltpu.VMEM((rows, 2 * rank), bf16),
             pltpu.VMEM((2,) + sq, f32),
             pltpu.VMEM((rank, half), bf16),
             pltpu.VMEM((half, rank), bf16),
             strip, strip, strip, strip, strip, strip,
-        ] + [dma((sections,))] * 6 + [dma((2,))] + [dma((chunks,))] * 12,
+        ] + [dma((planes,))] * 6 + [dma((10,))] + [dma((chunks,))] * 12,
         compiler_params=pltpu.CompilerParams(
             collective_id=1, has_side_effects=True, vmem_limit_bytes=48 * 1024 * 1024),
-    )(pyh, n0, mm, gu, x0, g16, up, wd)
+    )(pyh, n0, nn, x0, g16, up, wd)
 
 
 def dp_place(x_n):
@@ -514,7 +546,7 @@
 
 
 def gram_kernel(yh_n, x_n, sections, x0, g16, down, up, mine_u, base, pyh, n0, out,
-                allu, part, rc, sums, rax, rby, sa, ray, sb, rbx, gs,
+                allu, part, rc, sums, rax, rby, sa, ray, sb, rbx, gs, gp, two, mine3, theirs3,
                 z_sem, f_send, f_recv, r_send, r_recv,
                 c_send, c_recv, ax_send, ax_recv, s_sem, bx_send, bx_recv,
                 ga_send, ga_recv, gb_send, gb_recv, gc_send, gc_recv):
@@ -583,10 +615,15 @@
     u = up[...]
     w = down[...]
     values = x0[...]
-    pyh[0] = dot_nn(values, w)
-    pyh[1] = dot_nt(values, u)
-    pyh[2] = dot_nt(g16[...], u)
-    wide = values.astype(f32)
+    token_half = x0.shape[0] // 2
+    keep = pl.ds(ylo * token_half, token_half)
+    give = pl.ds((1 - ylo) * token_half, token_half)
+    mine3[0] = dot_nn(values, w)
+    mine3[1] = dot_nt(values, u)
+    mine3[2] = dot_nt(g16[...], u)
+    swap3 = remote(mine3.at[:, give], theirs3, z_sem.at[2], z_sem.at[3], partner)
+    swap3.start()
+    wide = x0[keep, :].astype(f32)
     n0[...] = jnp.broadcast_to(jnp.sum(wide * wide, axis=1, keepdims=True), n0.shape)
     products(z)
     core_copy(z).start()
@@ -607,7 +644,21 @@
                                    ax_send, ax_recv, s_sem, bx_send, bx_recv)
     gs[0:cut] = total_a.astype(bf16)
     gs[cut:rows] = total_b.astype(bf16)
-    out[yh, x, core] = gs[...]
+    swap = remote(gs, gp, z_sem.at[4], z_sem.at[5], partner)
+    swap.start()
+
+    def lanes(base, which):
+        return pl.ds(pl.multiple_of(base + which * rank, 128), rank)
+
+    swap3.wait_recv()
+    pyh[:, :, lanes(0, ylo)] = mine3[:, keep]
+    pyh[:, :, lanes(0, 1 - ylo)] = theirs3[...]
+    two[:, lanes(0, ylo)] = gs[:, 0:rank]
+    two[:, lanes(2 * rank, ylo)] = gs[:, rank:2 * rank]
+    swap.wait_recv()
+    two[:, lanes(0, 1 - ylo)] = gp[:, 0:rank]
+    two[:, lanes(2 * rank, 1 - ylo)] = gp[:, rank:2 * rank]
+    out[yh, x, core] = two[...]
 
     low = pl.ds(0, cut)
     high = pl.ds(cut, cut)
@@ -617,14 +668,14 @@
 
     ga = (ga_send, ga_recv)
     gb = (gb_send, gb_recv)
-    a_y = spread(gs.at[low], out.at[yh, x, core, low], ga, 0, other_y)
+    a_y = spread(two.at[low], out.at[yh, x, core, low], ga, 0, other_y)
 
     def a_x(i):
         spot = out.at[:, x, core, low]
         return spread(spot, spot, ga, i, place(yh, xp(i), core))
 
     def b_x(i):
-        return spread(gs.at[high], out.at[yh, x, core, high], gb, i - 1, place(yh, xp(i), core))
+        return spread(two.at[high], out.at[yh, x, core, high], gb, i - 1, place(yh, xp(i), core))
 
     def b_y(i):
         spot = out.at[yh, xp(i), core, high]
@@ -658,6 +709,8 @@
         b_x(i).wait_send()
     a_y.wait_send()
     pair.wait_send()
+    swap.wait_send()
+    swap3.wait_send()
     for i in range(1, hops + 1):
         ring_f(i).wait_send()
         ring_r(i).wait_send()
@@ -685,9 +738,9 @@
     return pl.pallas_call(
         functools.partial(gram_kernel, yh_n, x_n, sections),
         out_shape=(
-            jax.ShapeDtypeStruct((3, rows, rank), f32),
-            jax.ShapeDtypeStruct((rows, rank), f32),
-            jax.ShapeDtypeStruct((yh_n, x_n, 2, rank, 2 * rank), bf16),
+            jax.ShapeDtypeStruct((3, rows // 2, 2 * rank), f32),
+            jax.ShapeDtypeStruct((rows // 2, rank), f32),
+            jax.ShapeDtypeStruct((yh_n, x_n, 2, rank, 4 * rank), bf16),
         ),
         in_specs=[vm] * 6,
         out_specs=(vm, vm, vm),
@@ -695,8 +748,10 @@
             pltpu.VMEM((sections // 2, 2, height, rank), bf16),
             buf(yh_n * x_n, 2, rank), buf(yh_n * x_n, rank), buf(yh_n, x_n, rank),
             buf(x_n - 1, yh_n, cut), buf(x_n, cut), buf(yh_n, cut), buf(cut),
-            buf(x_n, cut), buf(x_n - 1, cut), buf(rank),
-            dma((2,)), dma((sections // 4,)), dma((sections // 4,)),
+            buf(x_n, cut), buf(x_n - 1, cut), buf(rank), buf(rank),
+            pltpu.VMEM((rank, 4 * rank), bf16),
+            pltpu.VMEM((3, rows, rank), f32), pltpu.VMEM((3, rows // 2, rank), f32),
+            dma((6,)), dma((sections // 4,)), dma((sections // 4,)),
             dma((sections // 4,)), dma((sections // 4,)),
             dma((yh_n * x_n,)), dma((yh_n * x_n,)), dma((x_n - 1,)), dma((x_n - 1,)), dma((4,)),
             dma((x_n - 1,)), dma((x_n - 1,)),
@@ -943,11 +998,8 @@
     mine_w = lax.dynamic_slice_in_dim(down, d * part, part, 0)
     base = jnp.concatenate([mine_w, mine_u], axis=1)
     pyh, n0, grams = grams_of(sections, shards, x0, g16, down, upward, mine_u, base)
-    grams = grams.reshape(sections, rank, 2 * rank)
-    mm = grams[:, :, :rank]
-    gu = grams[:, :, rank:]
-
-    x1, g1, u_s, q_s = recurrence(sections, pyh, n0, mm, gu, x0, g16, upward, down)
+    grams = grams.reshape(sections // 2, 2 * rank, 4 * rank)
+    x1, g1, u_s, q_s = recurrence(sections, pyh, n0, grams, x0, g16, upward, down)
     own, nxt = reduce_gather(sections, shards, x1, g1, u_s, q_s, upward, base)
     wide = (width, 2 * rank)
     grad_down, grad_up, advance = finish(sections, own.reshape(wide), nxt.reshape(wide), x1)

time: 335 us -> 303 us (0.904)
  Pallas kernels: 325 us -> 291 us
    pallas_call x1, Pallas kernels: 142 us -> 114 us  [recurrence(): pl.pallas_call(functools.partial(recurrence_kernel, sections, chunks), ou...]
    pallas_call x1, Pallas kernels: 115 us -> 102 us  [reduce_gather(): pl.pallas_call(functools.partial(reduce_kernel, yh_n, x_n, sections), out...]
    pallas_call x1, Pallas kernels: 59.2 us -> 66.4 us  [grams_of(): pl.pallas_call(functools.partial(gram_kernel, yh_n, x_n, sections), out_s...]
    unnamed x12 -> x14, local copies, waits for them, and re-layouts: 7.48 us -> 8.98 us
where the time goes in v4:
time: 303 us; the launch traced here: 302 us
  Pallas kernels  291 us (96%)
  local copies, waits for them, and re-layouts  11 us (4%)
    pallas_call x1, Pallas kernels, recurrence(): pl.pallas_call(functools.partial(recurrence_kernel, sections, chunks), ou...  114 us
    pallas_call x1, Pallas kernels, reduce_gather(): pl.pallas_call(functools.partial(reduce_kernel, yh_n, x_n, sections), out...  102 us
    pallas_call x1, Pallas kernels, grams_of(): pl.pallas_call(functools.partial(gram_kernel, yh_n, x_n, sections), out_s...  66.4 us
    unnamed x14, local copies, waits for them, and re-layouts  8.98 us
    pallas_call x1, Pallas kernels, finish(): pl.pallas_call(functools.partial(finish_kernel, sections), out_shape=(jax...  8.08 us

profile of v4, /device:TPU:1, one launch (start us, length us, event | category | flops | bytes accessed | tf_op | source)
XLA Modules:
  0.0 302.3 jit_solution(847928634281130926)
XLA Ops:
  0.6 0.9 dynamic-slice_bitcast_fusion
  1.5 1.0 constant_dynamic-slice_fusion
  2.6 0.1 copy.7
  2.7 0.0 copy-start
  2.8 1.5 copy-done
  4.2 0.0 copy-start.1
  4.2 1.5 copy-done.1
  5.7 0.0 copy-start.2
  5.7 1.5 copy-done.2
  7.2 66.4 %shard_map.67 = (f32[3,64,256]{2,1,0:T(8,128)S(1)}, f32[64,128]{1,0:T(8,128)S(1)}, bf16[2,4,2,128,512]{4,3,2,1,0:T(8,128)(2,1)}) custom-call(bf16[128,7168]{1,0:T(8,128)(2,1)S(1)} %bitcast.17, bf16[128,7168]{1,0:T(8,128)(2,1)S(1)} %bitcast.20, bf16[7168,128]{1,0:T(8,128)(2,1)S(1)} %bitcast.16, bf16[128,7168]{1,0:T(8,128)(2,1)} %bitcast.24, ...), custom_call_target="tpu_custom_call" | custom-call | tf_op jit(solution)/shard_map/pallas_call | solution.py:738
  73.6 113.9 %shard_map.68 = (bf16[128,7168]{1,0:T(8,128)(2,1)S(1)}, bf16[128,7168]{1,0:T(8,128)(2,1)S(1)}, bf16[128,128]{1,0:T(8,128)(2,1)S(1)}, bf16[128,128]{1,0:T(8,128)(2,1)S(1)}) custom-call(f32[3,64,256]{2,1,0:T(8,128)S(1)} %get-tuple-element.15.pyh, f32[64,128]{1,0:T(8,128)S(1)} %get-tuple-element.16.n0, bf16[8,256,512]{2,1,0:T(8,128)(2,1)} %bitcast.28, ...), custom_call_target="tpu_custom_call" | custom-call | tf_op jit(solution)/shard_map/pallas_call | solution.py:443
  187.5 0.0 copy-start.3
  187.5 1.2 copy-done.3
  188.7 0.0 copy-start.6
  188.7 1.2 copy-done.6
  190.0 0.0 copy-start.4
  190.0 102.2 %shard_map.69 = (bf16[2,4,2,448,256]{4,3,2,1,0:T(8,128)(2,1)}, bf16[2,4,2,448,256]{4,3,2,1,0:T(8,128)(2,1)}) custom-call(bf16[128,7168]{1,0:T(8,128)(2,1)} %copy-done.3, bf16[128,7168]{1,0:T(8,128)(2,1)} %copy-done.6, bf16[128,128]{1,0:T(8,128)(2,1)S(1)} %get-tuple-element.20.u_s, bf16[128,128]{1,0:T(8,128)(2,1)S(1)} %get-tuple-element.21.q_s, ...), custom_call_target="tpu_custom_call" | custom-call | tf_op jit(solution)/shard_map/pallas_call | solution.py:915
  292.2 0.0 copy-done.4
  292.2 0.0 copy-start.5
  292.2 2.0 copy-done.5
  294.2 8.1 %shard_map.70 = (bf16[7168,128]{1,0:T(8,128)(2,1)}, bf16[128,7168]{1,0:T(8,128)(2,1)}, bf16[128,7168]{1,0:T(8,128)(2,1)}) custom-call(bf16[7168,256]{1,0:T(8,128)(2,1)S(1)} %bitcast.21, bf16[7168,256]{1,0:T(8,128)(2,1)} %bitcast.27, bf16[128,7168]{1,0:T(8,128)(2,1)S(1)} %copy-done.4), custom_call_target="tpu_custom_call" | custom-call | tf_op jit(solution)/shard_map/pallas_call | solution.py:970
  (1 shorter events, 0.0 us)
Async XLA Ops:
  2.7 1.5 copy-start
  4.2 1.5 copy-start.1
  5.7 1.5 copy-start.2
  187.5 1.2 copy-start.3
  188.7 1.2 copy-start.6
  190.0 102.2 %copy-start.4 = (bf16[128,7168]{1,0:T(8,128)(2,1)S(1)}, bf16[128,7168]{1,0:T(8,128)(2,1)}, u32[]{:S(2)}) copy-start(bf16[128,7168]{1,0:T(8,128)(2,1)} %copy-done.3) | copy-start | bytes 5505028
  292.2 2.0 copy-start.5

commit v5 on v4

--- a/solution.py
+++ b/solution.py
@@ -35,12 +35,12 @@
     return value, slope
 
 
-def recurrence_kernel(sections, chunks, pyh, n0, nn, x0, g16, up, wd,
+def recurrence_kernel(sections, chunks, per, pyh, n0, nn, x0, g16, up, wd, upart, wpart,
                       xout, gout, u_out, q_out,
                       ul, ql, qp, mb, ys, nl, nsend, acc, hacc, slope, act, rinv, uf, qs, cpair,
-                      upart, wpart, xin, xkeep, xgive, gin, gkeep, ggive,
+                      xin, xkeep, xgive, gin, gkeep, ggive,
                       u_send, u_recv, q_send, q_recv, m_send, m_recv, e_sem,
-                      up_send, up_recv, wp_send, wp_recv, c_send, c_recv, g_send, g_recv,
+                      c_send, c_recv, g_send, g_recv,
                       b_send, b_recv, h_send, h_recv):
     s = lax.axis_index("section")
     planes = sections // 2
@@ -49,6 +49,7 @@
     rank = up.shape[0]
     half = width // 2
     piece = half // chunks
+    trips = chunks // per
     z = s // 2
     ylo = lax.rem(s, 2)
     first = ylo == 0
@@ -82,14 +83,6 @@
     def columns(base, c):
         return pl.ds(pl.multiple_of(base + c * piece, 128), piece)
 
-    def up_copy(c):
-        return remote(up.at[:, columns((1 - ylo) * half, c)], upart.at[:, columns(0, c)],
-                      up_send.at[c], up_recv.at[c], partner)
-
-    def wp_copy(c):
-        return remote(wd.at[columns((1 - ylo) * half, c), :], wpart.at[columns(0, c), :],
-                      wp_send.at[c], wp_recv.at[c], partner)
-
     def x_copy(c):
         return remote(xkeep.at[:, columns(0, c)], xin.at[:, columns(0, c)],
                       c_send.at[c], c_recv.at[c], plane(peer(1)))
@@ -152,12 +145,6 @@
     acc[:, 2 * rank:4 * rank] = pyh[1]
     hacc[...] = pyh[2]
 
-    def start_up(c, carry):
-        up_copy(c).start()
-        return carry
-
-    lax.fori_loop(0, chunks, start_up, 0)
-
     def start_m(j, carry):
         m_copy(j).start()
         return carry
@@ -169,7 +156,6 @@
         def _():
             x_copy(c).wait_recv()
 
-        up_copy(c).wait_recv()
         here = columns(ylo * half, c)
         there = columns(0, c)
         start = jnp.where(z > 0, xin[:, there], x0[:, here]).astype(f32)
@@ -192,7 +178,6 @@
         def _():
             b_copy(c).wait_recv()
 
-        wp_copy(c).wait_recv()
         here = columns(ylo * half, c)
         there = columns(0, c)
         ours = wd[here, :]
@@ -352,22 +337,17 @@
 
         p = t - (z + 1)
 
-        @pl.when((p >= 0) & (p < chunks // 2))
+        @pl.when((p >= 0) & (p < trips))
         def _():
             @pl.when(p == 0)
             def _():
                 uf_arrived().wait_recv()
-            for j in range(2):
-                chain(2 * p + j)
-
-        @pl.when((t >= 2) & (t < 2 + chunks // 2))
-        def _():
-            for j in range(2):
-                wp_copy(2 * (t - 2) + j).start()
+            for j in range(per):
+                chain(per * p + j)
 
         b = t - (2 * planes - z)
 
-        @pl.when((b >= 0) & (b < chunks // 2))
+        @pl.when((b >= 0) & (b < trips))
         def _():
             @pl.when(b == 0)
             def _():
@@ -378,12 +358,12 @@
                     c_a, c_b = c_of(stat)
                     cpair[0, where, :] = jnp.broadcast_to(c_a, (some, rank))
                     cpair[1, where, :] = jnp.broadcast_to(c_b, (some, rank))
-            for j in range(2):
-                chain_back(2 * b + j)
+            for j in range(per):
+                chain_back(per * b + j)
 
         return carry
 
-    lax.fori_loop(0, 2 * planes + chunks // 2, tick, 0)
+    lax.fori_loop(0, 2 * planes + trips, tick, 0)
     u_out[...] = jnp.where(first, uf[:, head], uf[:, tail])
     q_out[...] = jnp.where(first, qs[:, head], qs[:, tail])
 
@@ -399,8 +379,6 @@
             b_copy(c).wait_send()
         h_copy(c).wait_send()
         h_arrived(c).wait_recv()
-        up_copy(c).wait_send()
-        wp_copy(c).wait_send()
         return carry
 
     lax.fori_loop(0, chunks, finish, 0)
@@ -427,13 +405,14 @@
     qp_copy().wait_send()
 
 
-def recurrence(sections, pyh, n0, nn, x0, g16, up, wd):
+def recurrence(sections, pyh, n0, nn, x0, g16, up, wd, upart, wpart):
     rows, width = x0.shape
     rank = up.shape[0]
     half = width // 2
     some = rows // 2
     planes = sections // 2
-    chunks = 14
+    chunks = 28
+    per = 4
     vm = pl.BlockSpec(memory_space=pltpu.VMEM)
     dma = pltpu.SemaphoreType.DMA
     sq = (rows, rank)
@@ -441,9 +420,9 @@
     wide = jax.ShapeDtypeStruct((rows, width), bf16)
     strip = pltpu.VMEM((rows, half), bf16)
     return pl.pallas_call(
-        functools.partial(recurrence_kernel, sections, chunks),
+        functools.partial(recurrence_kernel, sections, chunks, per),
         out_shape=(wide, wide, jax.ShapeDtypeStruct(sq, bf16), jax.ShapeDtypeStruct(sq, bf16)),
-        in_specs=[vm] * 7,
+        in_specs=[vm] * 9,
         out_specs=(vm,) * 4,
         scratch_shapes=[
             pltpu.VMEM((planes,) + two, bf16),
@@ -459,13 +438,11 @@
             pltpu.VMEM((rows, 2 * rank), bf16),
             pltpu.VMEM((rows, 2 * rank), bf16),
             pltpu.VMEM((2,) + sq, f32),
-            pltpu.VMEM((rank, half), bf16),
-            pltpu.VMEM((half, rank), bf16),
             strip, strip, strip, strip, strip, strip,
-        ] + [dma((planes,))] * 6 + [dma((10,))] + [dma((chunks,))] * 12,
+        ] + [dma((planes,))] * 6 + [dma((10,))] + [dma((chunks,))] * 8,
         compiler_params=pltpu.CompilerParams(
             collective_id=1, has_side_effects=True, vmem_limit_bytes=48 * 1024 * 1024),
-    )(pyh, n0, nn, x0, g16, up, wd)
+    )(pyh, n0, nn, x0, g16, up, wd, upart, wpart)
 
 
 def dp_place(x_n):
@@ -478,12 +455,32 @@
                                         device_id=where, device_id_type=MESH)
 
 
-def scatter_sum(yh_n, x_n, core_copy, part, rc, sums, rax, rby, sa, ray, sb, rbx,
-                ax_send, ax_recv, s_sem, bx_send, bx_recv):
+def block_sum(b, yh_n, x_n, core_copy, part, rc, sums, rax, rby, ax_send, ax_recv, by_send, by_recv):
+    yh, x, core = dp_place(x_n)
+    cut = sums.shape[2] // 2
+    y_ = b // x_n
+    x_ = lax.rem(b, x_n)
+    core_copy(b).wait_recv()
+    sums[y_, x_] = (part[b, core].astype(f32) + rc[b].astype(f32)).astype(bf16)
+    turn = lax.rem(x_ - x + x_n, x_n)
+
+    @pl.when(turn != 0)
+    def _():
+        sem = (turn - 1) * yh_n + y_
+        remote(sums.at[y_, x_, 0:cut], rax.at[turn - 1, y_], ax_send.at[sem], ax_recv.at[sem],
+               {"dp": (yh * x_n + x_) * 2 + core}).start()
+
+    @pl.when(y_ != yh)
+    def _():
+        remote(sums.at[y_, x_, cut:2 * cut], rby.at[x_], by_send.at[x_], by_recv.at[x_],
+               {"dp": (y_ * x_n + x) * 2 + core}).start()
+
+
+def scatter_sum(yh_n, x_n, sums, rax, rby, sa, ray, sb, rbx,
+                ax_send, ax_recv, by_send, by_recv, s_sem, bx_send, bx_recv):
     yh, x, core = dp_place(x_n)
     rows = sums.shape[2]
     cut = rows // 2
-    blocks = yh_n * x_n
 
     def place(y_, x_, c_):
         return {"dp": (y_ * x_n + x_) * 2 + c_}
@@ -492,63 +489,54 @@
         return lax.rem(x + i, x_n)
 
     other_y = place(1 - yh, x, core)
-    copy = remote
-
-    def first_sum(b, carry):
-        core_copy(b).wait_recv()
-        y_ = b // x_n
-        x_ = lax.rem(b, x_n)
-        sums[y_, x_] = (part[b, core].astype(f32) + rc[b].astype(f32)).astype(bf16)
-        return carry
-
-    lax.fori_loop(0, blocks, first_sum, 0)
-
-    def ax_copy(i):
-        return copy(sums.at[:, xp(i), 0:cut], rax.at[i - 1], ax_send.at[i - 1], ax_recv.at[i - 1],
-                    place(yh, xp(i), core))
-
-    by_copy = copy(sums.at[1 - yh, :, cut:rows], rby, s_sem.at[0], s_sem.at[1], other_y)
-    ay_copy = copy(sa.at[1 - yh], ray, s_sem.at[2], s_sem.at[3], other_y)
+
+    def ax_copy(i, y_):
+        sem = (i - 1) * yh_n + y_
+        return remote(sums.at[y_, xp(i), 0:cut], rax.at[i - 1, y_], ax_send.at[sem], ax_recv.at[sem],
+                      place(yh, xp(i), core))
+
+    def by_copy(x_):
+        return remote(sums.at[1 - yh, x_, cut:rows], rby.at[x_], by_send.at[x_], by_recv.at[x_], other_y)
 
     def bx_copy(i):
-        return copy(sb.at[xp(i)], rbx.at[i - 1], bx_send.at[i - 1], bx_recv.at[i - 1],
-                    place(yh, xp(i), core))
-
-    by_copy.start()
-    for i in range(1, x_n):
-        ax_copy(i).start()
-    for i in range(1, x_n):
-        ax_copy(i).wait_recv()
+        return remote(sb.at[xp(i)], rbx.at[i - 1], bx_send.at[i - 1], bx_recv.at[i - 1],
+                      place(yh, xp(i), core))
+
+    ay_copy = remote(sa.at[1 - yh], ray, s_sem.at[0], s_sem.at[1], other_y)
+
+    for i in range(x_n):
+        x_ = xp(i)
+        by_copy(x_).wait_recv()
+        sb[x_] = (sums[yh, x_, cut:rows].astype(f32) + rby[x_].astype(f32)).astype(bf16)
+        if i > 0:
+            bx_copy(i).start()
     for y_ in range(yh_n):
         total = sums[y_, x, 0:cut].astype(f32)
         for i in range(1, x_n):
+            ax_copy(i, y_).wait_recv()
             total = total + rax[i - 1, y_].astype(f32)
         sa[y_] = total.astype(bf16)
     ay_copy.start()
-    by_copy.wait_recv()
-    for x_ in range(x_n):
-        sb[x_] = (sums[yh, x_, cut:rows].astype(f32) + rby[x_].astype(f32)).astype(bf16)
+    total_b = sb[x].astype(f32)
     for i in range(1, x_n):
-        bx_copy(i).start()
+        bx_copy(i).wait_recv()
+        total_b = total_b + rbx[i - 1].astype(f32)
     ay_copy.wait_recv()
     total_a = sa[yh].astype(f32) + ray[...].astype(f32)
     for i in range(1, x_n):
-        bx_copy(i).wait_recv()
-    total_b = sb[x].astype(f32)
-    for i in range(1, x_n):
-        total_b = total_b + rbx[i - 1].astype(f32)
-    for i in range(1, x_n):
-        ax_copy(i).wait_send()
+        for y_ in range(yh_n):
+            ax_copy(i, y_).wait_send()
         bx_copy(i).wait_send()
-    by_copy.wait_send()
+    for x_ in range(x_n):
+        by_copy(x_).wait_send()
     ay_copy.wait_send()
     return total_a, total_b
 
 
-def gram_kernel(yh_n, x_n, sections, x0, g16, down, up, mine_u, base, pyh, n0, out,
+def gram_kernel(yh_n, x_n, sections, x0, g16, down, up, mine_u, base, pyh, n0, out, upart, wpart,
                 allu, part, rc, sums, rax, rby, sa, ray, sb, rbx, gs, gp, two, mine3, theirs3,
                 z_sem, f_send, f_recv, r_send, r_recv,
-                c_send, c_recv, ax_send, ax_recv, s_sem, bx_send, bx_recv,
+                c_send, c_recv, ax_send, ax_recv, by_send, by_recv, s_sem, bx_send, bx_recv,
                 ga_send, ga_recv, gb_send, gb_recv, gc_send, gc_recv):
     yh, x, core = dp_place(x_n)
     s = lax.axis_index("section")
@@ -625,6 +613,17 @@
     swap3.start()
     wide = x0[keep, :].astype(f32)
     n0[...] = jnp.broadcast_to(jnp.sum(wide * wide, axis=1, keepdims=True), n0.shape)
+    half = x0.shape[1] // 2
+    far = pl.ds(pl.multiple_of((1 - ylo) * half, 128), half)
+    swap_u = remote(up.at[:, far], upart, z_sem.at[6], z_sem.at[7], partner)
+    swap_w = remote(down.at[far, :], wpart, z_sem.at[8], z_sem.at[9], partner)
+    swap_u.start()
+    swap_w.start()
+
+    def collect(b):
+        block_sum(b, yh_n, x_n, core_copy, part, rc, sums, rax, rby,
+                  ax_send, ax_recv, by_send, by_recv)
+
     products(z)
     core_copy(z).start()
     for i in range(1, hops + 1):
@@ -636,12 +635,17 @@
             ring_r(i + 1).start()
         products(zp(z_n - i))
         core_copy(zp(z_n - i)).start()
+        if i == 1:
+            collect(z)
+        else:
+            collect(zp(i - 1))
         if i < hops:
             products(zp(i))
             core_copy(zp(i)).start()
-
-    total_a, total_b = scatter_sum(yh_n, x_n, core_copy, part, rc, sums, rax, rby, sa, ray, sb, rbx,
-                                   ax_send, ax_recv, s_sem, bx_send, bx_recv)
+        collect(zp(z_n - i))
+
+    total_a, total_b = scatter_sum(yh_n, x_n, sums, rax, rby, sa, ray, sb, rbx,
+                                   ax_send, ax_recv, by_send, by_recv, s_sem, bx_send, bx_recv)
     gs[0:cut] = total_a.astype(bf16)
     gs[cut:rows] = total_b.astype(bf16)
     swap = remote(gs, gp, z_sem.at[4], z_sem.at[5], partner)
@@ -711,6 +715,8 @@
     pair.wait_send()
     swap.wait_send()
     swap3.wait_send()
+    swap_u.wait()
+    swap_w.wait()
     for i in range(1, hops + 1):
         ring_f(i).wait_send()
         ring_r(i).wait_send()
@@ -741,9 +747,11 @@
             jax.ShapeDtypeStruct((3, rows // 2, 2 * rank), f32),
             jax.ShapeDtypeStruct((rows // 2, rank), f32),
             jax.ShapeDtypeStruct((yh_n, x_n, 2, rank, 4 * rank), bf16),
+            jax.ShapeDtypeStruct((rank, width // 2), bf16),
+            jax.ShapeDtypeStruct((width // 2, rank), bf16),
         ),
         in_specs=[vm] * 6,
-        out_specs=(vm, vm, vm),
+        out_specs=(vm,) * 5,
         scratch_shapes=[
             pltpu.VMEM((sections // 2, 2, height, rank), bf16),
             buf(yh_n * x_n, 2, rank), buf(yh_n * x_n, rank), buf(yh_n, x_n, rank),
@@ -751,9 +759,10 @@
             buf(x_n, cut), buf(x_n - 1, cut), buf(rank), buf(rank),
             pltpu.VMEM((rank, 4 * rank), bf16),
             pltpu.VMEM((3, rows, rank), f32), pltpu.VMEM((3, rows // 2, rank), f32),
-            dma((6,)), dma((sections // 4,)), dma((sections // 4,)),
+            dma((10,)), dma((sections // 4,)), dma((sections // 4,)),
             dma((sections // 4,)), dma((sections // 4,)),
-            dma((yh_n * x_n,)), dma((yh_n * x_n,)), dma((x_n - 1,)), dma((x_n - 1,)), dma((4,)),
+            dma((yh_n * x_n,)), dma((yh_n * x_n,)),
+            dma((yh_n * (x_n - 1),)), dma((yh_n * (x_n - 1),)), dma((x_n,)), dma((x_n,)), dma((4,)),
             dma((x_n - 1,)), dma((x_n - 1,)),
             dma((x_n,)), dma((x_n,)), dma((2 * x_n,)), dma((2 * x_n,)), dma((x_n,)), dma((x_n,)),
         ],
@@ -764,7 +773,7 @@
 
 def reduce_kernel(yh_n, x_n, sections, x1, g1, u_s, q_s, up, base, own, nxt,
                   part, rc, sums, rax, rby, sa, ray, sb, rbx, gs, nw,
-                  c_send, c_recv, ax_send, ax_recv, s_sem, bx_send, bx_recv,
+                  c_send, c_recv, ax_send, ax_recv, by_send, by_recv, s_sem, bx_send, bx_recv,
                   own_send, own_recv, oc_send, oc_recv, nx_send, nx_recv, ny_send, ny_recv,
                   nc_send, nc_recv):
     d = lax.axis_index("dp")
@@ -811,13 +820,22 @@
             part[b, half, :, 0:rank] = g_down[half * rows:(half + 1) * rows]
             part[b, half, :, rank:2 * rank] = g_up[half * rows:(half + 1) * rows]
         core_copy(b).start()
+
+        @pl.when(b > 0)
+        def _():
+            collect(b - 1)
         return carry
+
+    def collect(b):
+        block_sum(b, yh_n, x_n, core_copy, part, rc, sums, rax, rby,
+                  ax_send, ax_recv, by_send, by_recv)
 
     blocks = yh_n * x_n
     lax.fori_loop(0, blocks, terms, 0)
-
-    total_a, total_b = scatter_sum(yh_n, x_n, core_copy, part, rc, sums, rax, rby, sa, ray, sb, rbx,
-                                   ax_send, ax_recv, s_sem, bx_send, bx_recv)
+    collect(blocks - 1)
+
+    total_a, total_b = scatter_sum(yh_n, x_n, sums, rax, rby, sa, ray, sb, rbx,
+                                   ax_send, ax_recv, by_send, by_recv, s_sem, bx_send, bx_recv)
     gs[0:cut] = total_a.astype(bf16)
     gs[cut:rows] = total_b.astype(bf16)
     nw[...] = (base[...].astype(f32) - learn_rate * gs[...].astype(f32)).astype(bf16)
@@ -840,11 +858,6 @@
     def own_c(i):
         spot = own.at[:, xp(i), core]
         return copy(spot, spot, oc_send.at[i], oc_recv.at[i], other_core)
-
-    own_y.wait_recv()
-    for i in range(1, x_n):
-        own_x(i).start()
-    own_c(0).start()
 
     def nxt_x(i):
         spot = nxt.at[yh, x, core]
@@ -865,23 +878,35 @@
             nxt_x(i).start()
         nxt_y(0).start()
 
+    own_y.wait_recv()
+
+    @pl.when(has_next)
+    def _():
+        for i in range(1, x_n):
+            nxt_x(i).wait_send()
+
     for i in range(1, x_n):
-        own_x(x_n - i).wait_recv()
-        own_c(i).start()
+        own_x(i).start()
+    own_c(0).start()
 
     @pl.when(has_next)
     def _():
         for i in range(1, x_n):
             nxt_x(x_n - i).wait_recv()
             nxt_y(i).start()
+
+    for i in range(1, x_n):
+        own_x(x_n - i).wait_recv()
+        own_c(i).start()
+
+    @pl.when(has_next)
+    def _():
         for i in range(x_n):
             nxt_y(i).wait_recv()
             nxt_c(i).start()
         for i in range(x_n):
             nxt_c(i).wait()
             nxt_y(i).wait_send()
-        for i in range(1, x_n):
-            nxt_x(i).wait_send()
 
     for i in range(x_n):
         own_c(i).wait()
@@ -921,7 +946,8 @@
             buf(yh_n * x_n, 2, rows), buf(yh_n * x_n, rows), buf(yh_n, x_n, rows),
             buf(x_n - 1, yh_n, cut), buf(x_n, cut), buf(yh_n, cut), buf(cut),
             buf(x_n, cut), buf(x_n - 1, cut), buf(rows), buf(rows),
-            dma((yh_n * x_n,)), dma((yh_n * x_n,)), dma((x_n - 1,)), dma((x_n - 1,)), dma((8,)),
+            dma((yh_n * x_n,)), dma((yh_n * x_n,)),
+            dma((yh_n * (x_n - 1),)), dma((yh_n * (x_n - 1),)), dma((x_n,)), dma((x_n,)), dma((8,)),
             dma((x_n - 1,)), dma((x_n - 1,)), dma((x_n - 1,)), dma((x_n - 1,)),
             dma((x_n,)), dma((x_n,)), dma((x_n - 1,)), dma((x_n - 1,)), dma((x_n,)), dma((x_n,)),
             dma((x_n,)), dma((x_n,)),
@@ -997,9 +1023,9 @@
     mine_u = lax.dynamic_slice_in_dim(up_t, d * part, part, 0)
     mine_w = lax.dynamic_slice_in_dim(down, d * part, part, 0)
     base = jnp.concatenate([mine_w, mine_u], axis=1)
-    pyh, n0, grams = grams_of(sections, shards, x0, g16, down, upward, mine_u, base)
+    pyh, n0, grams, upart, wpart = grams_of(sections, shards, x0, g16, down, upward, mine_u, base)
     grams = grams.reshape(sections // 2, 2 * rank, 4 * rank)
-    x1, g1, u_s, q_s = recurrence(sections, pyh, n0, grams, x0, g16, upward, down)
+    x1, g1, u_s, q_s = recurrence(sections, pyh, n0, grams, x0, g16, upward, down, upart, wpart)
     own, nxt = reduce_gather(sections, shards, x1, g1, u_s, q_s, upward, base)
     wide = (width, 2 * rank)
     grad_down, grad_up, advance = finish(sections, own.reshape(wide), nxt.reshape(wide), x1)

time: 303 us -> 290 us (0.957)
  Pallas kernels: 291 us -> 279 us
    pallas_call x1, Pallas kernels: 66.4 us -> 85.5 us  [grams_of(): pl.pallas_call(functools.partial(gram_kernel, yh_n, x_n, sections), out_s...]
    pallas_call x1, Pallas kernels: 114 us -> 98.2 us  [recurrence(): pl.pallas_call(functools.partial(recurrence_kernel, sections, chunks, per...]
    pallas_call x1, Pallas kernels: 102 us -> 87.1 us  [reduce_gather(): pl.pallas_call(functools.partial(reduce_kernel, yh_n, x_n, sections), out...]
    unnamed x14 -> x12, local copies, waits for them, and re-layouts: 8.98 us -> 7.48 us
where the time goes in v5:
time: 290 us; the launch traced here: 289 us
  Pallas kernels  279 us (96%)
  local copies, waits for them, and re-layouts  9.54 us (3%)
    pallas_call x1, Pallas kernels, recurrence(): pl.pallas_call(functools.partial(recurrence_kernel, sections, chunks, per...  98.2 us
    pallas_call x1, Pallas kernels, reduce_gather(): pl.pallas_call(functools.partial(reduce_kernel, yh_n, x_n, sections), out...  87.1 us
    pallas_call x1, Pallas kernels, grams_of(): pl.pallas_call(functools.partial(gram_kernel, yh_n, x_n, sections), out_s...  85.5 us
    pallas_call x1, Pallas kernels, finish(): pl.pallas_call(functools.partial(finish_kernel, sections), out_shape=(jax...  8.08 us
    unnamed x12, local copies, waits for them, and re-layouts  7.48 us

profile of v5, /device:TPU:1, one launch (start us, length us, event | category | flops | bytes accessed | tf_op | source)
XLA Modules:
  0.0 289.1 jit_solution(3561458334648496250)
XLA Ops:
  0.6 0.9 dynamic-slice_bitcast_fusion
  1.5 1.0 constant_dynamic-slice_fusion
  2.6 0.1 copy.7
  2.7 0.0 copy-start.2
  2.8 1.5 copy-done.2
  4.2 0.0 copy-start.3
  4.2 1.5 copy-done.3
  5.7 85.5 %shard_map.67 = (f32[3,64,256]{2,1,0:T(8,128)S(1)}, f32[64,128]{1,0:T(8,128)S(1)}, bf16[2,4,2,128,512]{4,3,2,1,0:T(8,128)(2,1)}, bf16[128,3584]{1,0:T(8,128)(2,1)S(1)}, bf16[3584,128]{1,0:T(8,128)(2,1)S(1)}) custom-call(bf16[128,7168]{1,0:T(8,128)(2,1)S(1)} %bitcast.16, bf16[128,7168]{1,0:T(8,128)(2,1)S(1)} %bitcast.18, bf16[7168,128]{1,0:T(8,128)(2,1)} %bitcast.25, ...), custom_call_target="tpu_custom_call" | custom-call | tf_op jit(solution)/shard_map/pallas_call | solution.py:744
  91.3 98.2 %shard_map.68 = (bf16[128,7168]{1,0:T(8,128)(2,1)S(1)}, bf16[128,7168]{1,0:T(8,128)(2,1)S(1)}, bf16[128,128]{1,0:T(8,128)(2,1)S(1)}, bf16[128,128]{1,0:T(8,128)(2,1)S(1)}) custom-call(f32[3,64,256]{2,1,0:T(8,128)S(1)} %get-tuple-element.17.pyh, f32[64,128]{1,0:T(8,128)S(1)} %get-tuple-element.18.n0, bf16[8,256,512]{2,1,0:T(8,128)(2,1)} %bitcast.28, ...), custom_call_target="tpu_custom_call" | custom-call | tf_op jit(solution)/shard_map/pallas_call | solution.py:422
  189.4 0.0 copy-start
  189.4 1.2 copy-done
  190.7 0.0 copy-start.5
  190.7 1.2 copy-done.5
  191.9 0.0 copy-start.1
  191.9 87.1 %shard_map.69 = (bf16[2,4,2,448,256]{4,3,2,1,0:T(8,128)(2,1)}, bf16[2,4,2,448,256]{4,3,2,1,0:T(8,128)(2,1)}) custom-call(bf16[128,7168]{1,0:T(8,128)(2,1)} %copy-done, bf16[128,7168]{1,0:T(8,128)(2,1)} %copy-done.5, bf16[128,128]{1,0:T(8,128)(2,1)S(1)} %get-tuple-element.24.u_s, bf16[128,128]{1,0:T(8,128)(2,1)S(1)} %get-tuple-element.25.q_s, ...), custom_call_target="tpu_custom_call" | custom-call | tf_op jit(solution)/shard_map/pallas_call | solution.py:940
  279.0 0.0 copy-done.1
  279.0 0.0 copy-start.4
  279.0 2.0 copy-done.4
  281.0 8.1 %shard_map.70 = (bf16[7168,128]{1,0:T(8,128)(2,1)}, bf16[128,7168]{1,0:T(8,128)(2,1)}, bf16[128,7168]{1,0:T(8,128)(2,1)}) custom-call(bf16[7168,256]{1,0:T(8,128)(2,1)S(1)} %bitcast.19, bf16[7168,256]{1,0:T(8,128)(2,1)} %bitcast.27, bf16[128,7168]{1,0:T(8,128)(2,1)S(1)} %copy-done.1), custom_call_target="tpu_custom_call" | custom-call | tf_op jit(solution)/shard_map/pallas_call | solution.py:996
  (1 shorter events, 0.0 us)
Async XLA Ops:
  2.7 1.5 copy-start.2
  4.2 1.5 copy-start.3
  189.4 1.2 copy-start
  190.7 1.2 copy-start.5
  191.9 87.1 %copy-start.1 = (bf16[128,7168]{1,0:T(8,128)(2,1)S(1)}, bf16[128,7168]{1,0:T(8,128)(2,1)}, u32[]{:S(2)}) copy-start(bf16[128,7168]{1,0:T(8,128)(2,1)} %copy-done) | copy-start | bytes 5505028
  279.0 2.0 copy-start.4

commit v6 on v5

--- a/solution.py
+++ b/solution.py
@@ -570,8 +570,6 @@
     pl.semaphore_wait(barrier, len(peers))
 
     pair = remote(mine_u, allu.at[z, ylo], z_sem.at[0], z_sem.at[1], partner)
-    pair.start()
-    allu[z, ylo] = mine_u[...]
 
     def products(z_):
         for y_ in range(2):
@@ -582,23 +580,42 @@
 
     hops = z_n // 2
 
-    def ring_f(i):
-        if i < hops:
-            spot = allu.at[zp(z_n + 1 - i)]
-        else:
-            spot = allu.at[zp(z_n + 1 - i), 0]
-        return remote(spot, spot, f_send.at[i - 1], f_recv.at[i - 1], after)
-
-    def ring_r(i):
-        if i < hops:
-            spot = allu.at[zp(i - 1)]
-        else:
-            spot = allu.at[zp(i - 1), 1]
-        return remote(spot, spot, r_send.at[i - 1], r_recv.at[i - 1], before)
-
+    def column(j):
+        return ylo if j == 0 else 1 - ylo
+
+    def ring_f(i, j):
+        spot = allu.at[zp(z_n + 1 - i), column(j)]
+        src = mine_u if (i == 1 and j == 0) else spot
+        sem = 2 * (i - 1) + j
+        return remote(src, spot, f_send.at[sem], f_recv.at[sem], after)
+
+    def ring_r(i, j):
+        spot = allu.at[zp(i - 1), column(j)]
+        src = mine_u if (i == 1 and j == 0) else spot
+        sem = 2 * (i - 1) + j
+        return remote(src, spot, r_send.at[sem], r_recv.at[sem], before)
+
+    used_f = [(i, j) for i in range(1, hops + 1) for j in range(2) if i < hops or j == 0]
+    used_r = [(i, j) for i in range(1, hops + 1) for j in range(2) if i < hops or j == 1]
+
+    pair.start()
+    ring_f(1, 0).start()
+    ring_r(1, 0).start()
+    allu[z, ylo] = mine_u[...]
     pair.wait_recv()
-    ring_f(1).start()
-    ring_r(1).start()
+    ring_f(1, 1).start()
+    ring_r(1, 1).start()
+
+    half = x0.shape[1] // 2
+    quarter = half // 2
+    far = pl.ds(pl.multiple_of((1 - ylo) * half + core * quarter, 128), quarter)
+    near = pl.ds(pl.multiple_of(core * quarter, 128), quarter)
+    swap_u = remote(up.at[:, far], upart.at[:, near], z_sem.at[6], z_sem.at[7], partner)
+    swap_w = remote(down.at[far, :], wpart.at[near, :], z_sem.at[8], z_sem.at[9], partner)
+    share_u = remote(upart.at[:, near], upart.at[:, near], z_sem.at[10], z_sem.at[11], other_core)
+    share_w = remote(wpart.at[near, :], wpart.at[near, :], z_sem.at[12], z_sem.at[13], other_core)
+    swap_u.start()
+    swap_w.start()
 
     u = up[...]
     w = down[...]
@@ -613,12 +630,6 @@
     swap3.start()
     wide = x0[keep, :].astype(f32)
     n0[...] = jnp.broadcast_to(jnp.sum(wide * wide, axis=1, keepdims=True), n0.shape)
-    half = x0.shape[1] // 2
-    far = pl.ds(pl.multiple_of((1 - ylo) * half, 128), half)
-    swap_u = remote(up.at[:, far], upart, z_sem.at[6], z_sem.at[7], partner)
-    swap_w = remote(down.at[far, :], wpart, z_sem.at[8], z_sem.at[9], partner)
-    swap_u.start()
-    swap_w.start()
 
     def collect(b):
         block_sum(b, yh_n, x_n, core_copy, part, rc, sums, rax, rby,
@@ -627,12 +638,15 @@
     products(z)
     core_copy(z).start()
     for i in range(1, hops + 1):
-        ring_f(i).wait_recv()
-        if i < hops:
-            ring_f(i + 1).start()
-        ring_r(i).wait_recv()
-        if i < hops:
-            ring_r(i + 1).start()
+        for j in range(2):
+            if (i, j) in used_f:
+                ring_f(i, j).wait_recv()
+                if (i + 1, j) in used_f:
+                    ring_f(i + 1, j).start()
+            if (i, j) in used_r:
+                ring_r(i, j).wait_recv()
+                if (i + 1, j) in used_r:
+                    ring_r(i + 1, j).start()
         products(zp(z_n - i))
         core_copy(zp(z_n - i)).start()
         if i == 1:
@@ -644,6 +658,10 @@
             core_copy(zp(i)).start()
         collect(zp(z_n - i))
 
+    swap_u.wait_recv()
+    share_u.start()
+    swap_w.wait_recv()
+    share_w.start()
     total_a, total_b = scatter_sum(yh_n, x_n, sums, rax, rby, sa, ray, sb, rbx,
                                    ax_send, ax_recv, by_send, by_recv, s_sem, bx_send, bx_recv)
     gs[0:cut] = total_a.astype(bf16)
@@ -715,11 +733,14 @@
     pair.wait_send()
     swap.wait_send()
     swap3.wait_send()
-    swap_u.wait()
-    swap_w.wait()
-    for i in range(1, hops + 1):
-        ring_f(i).wait_send()
-        ring_r(i).wait_send()
+    swap_u.wait_send()
+    swap_w.wait_send()
+    share_u.wait()
+    share_w.wait()
+    for i, j in used_f:
+        ring_f(i, j).wait_send()
+    for i, j in used_r:
+        ring_r(i, j).wait_send()
 
     def settle(b, carry):
         core_copy(b).wait_send()
@@ -759,8 +780,8 @@
             buf(x_n, cut), buf(x_n - 1, cut), buf(rank), buf(rank),
             pltpu.VMEM((rank, 4 * rank), bf16),
             pltpu.VMEM((3, rows, rank), f32), pltpu.VMEM((3, rows // 2, rank), f32),
-            dma((10,)), dma((sections // 4,)), dma((sections // 4,)),
-            dma((sections // 4,)), dma((sections // 4,)),
+            dma((14,)), dma((sections // 2,)), dma((sections // 2,)),
+            dma((sections // 2,)), dma((sections // 2,)),
             dma((yh_n * x_n,)), dma((yh_n * x_n,)),
             dma((yh_n * (x_n - 1),)), dma((yh_n * (x_n - 1),)), dma((x_n,)), dma((x_n,)), dma((4,)),
             dma((x_n - 1,)), dma((x_n - 1,)),

time: 290 us -> 270 us (0.931)
  Pallas kernels: 279 us -> 259 us
    pallas_call x1, Pallas kernels: 85.5 us -> 64.5 us  [grams_of(): pl.pallas_call(functools.partial(gram_kernel, yh_n, x_n, sections), out_s...]
where the time goes in v6:
time: 270 us
  Pallas kernels  259 us (96%)
  local copies, waits for them, and re-layouts  9.54 us (4%)
    pallas_call x1, Pallas kernels, recurrence(): pl.pallas_call(functools.partial(recurrence_kernel, sections, chunks, per...  99.6 us
    pallas_call x1, Pallas kernels, reduce_gather(): pl.pallas_call(functools.partial(reduce_kernel, yh_n, x_n, sections), out...  87.3 us
    pallas_call x1, Pallas kernels, grams_of(): pl.pallas_call(functools.partial(gram_kernel, yh_n, x_n, sections), out_s...  64.5 us
    pallas_call x1, Pallas kernels, finish(): pl.pallas_call(functools.partial(finish_kernel, sections), out_shape=(jax...  8.08 us
    unnamed x12, local copies, waits for them, and re-layouts  7.48 us

profile of v6, /device:TPU:1, one launch (start us, length us, event | category | flops | bytes accessed | tf_op | source)
XLA Modules:
  0.0 269.7 jit_solution(12532416712901338403)
XLA Ops:
  0.6 0.9 dynamic-slice_bitcast_fusion
  1.5 1.0 constant_dynamic-slice_fusion
  2.6 0.1 copy.7
  2.7 0.0 copy-start.2
  2.8 1.5 copy-done.2
  4.2 0.0 copy-start.3
  4.2 1.5 copy-done.3
  5.7 64.5 %shard_map.67 = (f32[3,64,256]{2,1,0:T(8,128)S(1)}, f32[64,128]{1,0:T(8,128)S(1)}, bf16[2,4,2,128,512]{4,3,2,1,0:T(8,128)(2,1)}, bf16[128,3584]{1,0:T(8,128)(2,1)S(1)}, bf16[3584,128]{1,0:T(8,128)(2,1)S(1)}) custom-call(bf16[128,7168]{1,0:T(8,128)(2,1)S(1)} %bitcast.16, bf16[128,7168]{1,0:T(8,128)(2,1)S(1)} %bitcast.18, bf16[7168,128]{1,0:T(8,128)(2,1)} %bitcast.25, ...), custom_call_target="tpu_custom_call" | custom-call | tf_op jit(solution)/shard_map/pallas_call | solution.py:765
  70.2 99.6 %shard_map.68 = (bf16[128,7168]{1,0:T(8,128)(2,1)S(1)}, bf16[128,7168]{1,0:T(8,128)(2,1)S(1)}, bf16[128,128]{1,0:T(8,128)(2,1)S(1)}, bf16[128,128]{1,0:T(8,128)(2,1)S(1)}) custom-call(f32[3,64,256]{2,1,0:T(8,128)S(1)} %get-tuple-element.17.pyh, f32[64,128]{1,0:T(8,128)S(1)} %get-tuple-element.18.n0, bf16[8,256,512]{2,1,0:T(8,128)(2,1)} %bitcast.28, ...), custom_call_target="tpu_custom_call" | custom-call | tf_op jit(solution)/shard_map/pallas_call | solution.py:422
  169.8 0.0 copy-start
  169.8 1.2 copy-done
  171.1 0.0 copy-start.5
  171.1 1.2 copy-done.5
  172.3 0.0 copy-start.1
  172.3 87.3 %shard_map.69 = (bf16[2,4,2,448,256]{4,3,2,1,0:T(8,128)(2,1)}, bf16[2,4,2,448,256]{4,3,2,1,0:T(8,128)(2,1)}) custom-call(bf16[128,7168]{1,0:T(8,128)(2,1)} %copy-done, bf16[128,7168]{1,0:T(8,128)(2,1)} %copy-done.5, bf16[128,128]{1,0:T(8,128)(2,1)S(1)} %get-tuple-element.24.u_s, bf16[128,128]{1,0:T(8,128)(2,1)S(1)} %get-tuple-element.25.q_s, ...), custom_call_target="tpu_custom_call" | custom-call | tf_op jit(solution)/shard_map/pallas_call | solution.py:961
  259.6 0.0 copy-done.1
  259.6 0.0 copy-start.4
  259.6 2.0 copy-done.4
  261.6 8.1 %shard_map.70 = (bf16[7168,128]{1,0:T(8,128)(2,1)}, bf16[128,7168]{1,0:T(8,128)(2,1)}, bf16[128,7168]{1,0:T(8,128)(2,1)}) custom-call(bf16[7168,256]{1,0:T(8,128)(2,1)S(1)} %bitcast.19, bf16[7168,256]{1,0:T(8,128)(2,1)} %bitcast.27, bf16[128,7168]{1,0:T(8,128)(2,1)S(1)} %copy-done.1), custom_call_target="tpu_custom_call" | custom-call | tf_op jit(solution)/shard_map/pallas_call | solution.py:1017
  (1 shorter events, 0.0 us)
Async XLA Ops:
  2.7 1.5 copy-start.2
  4.2 1.5 copy-start.3
  169.8 1.2 copy-start
  171.1 1.2 copy-start.5
  172.3 87.3 %copy-start.1 = (bf16[128,7168]{1,0:T(8,128)(2,1)S(1)}, bf16[128,7168]{1,0:T(8,128)(2,1)}, u32[]{:S(2)}) copy-start(bf16[128,7168]{1,0:T(8,128)(2,1)} %copy-done) | copy-start | bytes 5505028
  259.6 2.0 copy-start.4

commit v7 on v6

--- a/solution.py
+++ b/solution.py
@@ -35,14 +35,20 @@
     return value, slope
 
 
-def recurrence_kernel(sections, chunks, per, pyh, n0, nn, x0, g16, up, wd, upart, wpart,
-                      xout, gout, u_out, q_out,
+def recurrence_kernel(sections, chunks, per, yh_n, x_n,
+                      pyh, n0, nn, x0, g16, up, wd, upart, wpart, mine_u,
+                      xout, own_w, own_u, nxt_u, bump_u,
                       ul, ql, qp, mb, ys, nl, nsend, acc, hacc, slope, act, rinv, uf, qs, cpair,
-                      xin, xkeep, xgive, gin, gkeep, ggive,
+                      xin, xkeep, xgive, gin, gkeep, ggive, xpass,
+                      gout, us, qv, xb, nacc, part, rc, sums, rax, rby, sa, ray, sb, rbx,
+                      gw, gu, nw, ub,
                       u_send, u_recv, q_send, q_recv, m_send, m_recv, e_sem,
                       c_send, c_recv, g_send, g_recv,
-                      b_send, b_recv, h_send, h_recv):
+                      b_send, b_recv, h_send, h_recv, p_send, p_recv,
+                      k_send, k_recv, ax_send, ax_recv, by_send, by_recv, s_sem, bx_send, bx_recv,
+                      wx_sem, wy_sem, wc_sem, vx_sem, vc_sem, nx_sem, ny_sem, nc_sem):
     s = lax.axis_index("section")
+    yh, x, core = dp_place(x_n)
     planes = sections // 2
     rows, width = x0.shape
     some = rows // 2
@@ -68,8 +74,20 @@
     barrier = pltpu.get_barrier_semaphore()
     for o in range(1, planes):
         pl.semaphore_signal(barrier, inc=1, device_id=plane(peer(o)), device_id_type=MESH)
-    pl.semaphore_signal(barrier, inc=1, device_id=partner, device_id_type=MESH)
-    pl.semaphore_wait(barrier, planes)
+
+    def place(y_, x_, c_):
+        return {"dp": (y_ * x_n + x_) * 2 + c_}
+
+    def xp(i):
+        return lax.rem(x + i, x_n)
+
+    other_core = place(yh, x, 1 - core)
+    other_y = place(1 - yh, x, core)
+    beyond = {"section": lax.rem(s + sections - 1 + 2 * ylo, sections)}
+    others = [partner, beyond, other_core, other_y] + [place(yh, xp(i), core) for i in range(1, x_n)]
+    for where in others:
+        pl.semaphore_signal(barrier, inc=1, device_id=where, device_id_type=MESH)
+    pl.semaphore_wait(barrier, planes - 1 + len(others))
 
     eye = (lax.broadcasted_iota(jnp.int32, (some, rank), 0)
            == lax.broadcasted_iota(jnp.int32, (some, rank), 1)).astype(f32)
@@ -98,6 +116,14 @@
     def give_arrived(c):
         return remote(xgive.at[:, columns(0, c)], xout.at[:, columns((1 - ylo) * half, c)],
                       g_send.at[c], g_recv.at[c], partner)
+
+    def pass_copy(c):
+        return remote(xpass.at[:, columns(0, c)], xb.at[:, columns(ylo * half, c)],
+                      p_send.at[c], p_recv.at[c], partner)
+
+    def pass_arrived(c):
+        return remote(xpass.at[:, columns(0, c)], xb.at[:, columns((1 - ylo) * half, c)],
+                      p_send.at[c], p_recv.at[c], partner)
 
     def h_copy(c):
         return remote(ggive.at[:, columns(0, c)], gout.at[:, columns(ylo * half, c)],
@@ -172,6 +198,10 @@
         xgive[:, there] = jnp.where(first, x_b, x_a)
         give_copy(c).start()
         xout[:, here] = jnp.where(first, x_a, x_b)
+        start = start.astype(bf16)
+        xpass[:, there] = jnp.where(first, x_a, start)
+        pass_copy(c).start()
+        xb[:, here] = jnp.where(first, start, x_a)
 
     def chain_back(c):
         @pl.when(z < planes - 1)
@@ -289,6 +319,29 @@
         lax.fori_loop(0, z, send, 0)
         qp_copy().start()
 
+    shard = mine_u.shape[0]
+    nacc[...] = jnp.zeros_like(nacc)
+
+    def core_copy(b):
+        return remote(part.at[b, 1 - core], rc.at[b], k_send.at[b], k_recv.at[b], other_core)
+
+    def collect(b):
+        block_sum(b, yh_n, x_n, core_copy, part, rc, sums, rax, rby,
+                  ax_send, ax_recv, by_send, by_recv)
+
+    def terms(b):
+        cols = pl.ds(pl.multiple_of(b * 2 * shard, 128), 2 * shard)
+        u = us[...]
+        before = xb[:, cols]
+        wide = before.astype(f32)
+        nacc[...] += jnp.broadcast_to(jnp.sum(wide * wide, axis=1, keepdims=True), nacc.shape)
+        g_down = dot_tn(before, qv[...]).astype(bf16)
+        g_up = dot_tn(gout[:, cols], u).astype(bf16)
+        for i in range(2):
+            part[b, i, :, head] = g_down[i * shard:(i + 1) * shard]
+            part[b, i, :, tail] = g_up[i * shard:(i + 1) * shard]
+        core_copy(b).start()
+
     def tick(t, carry):
         k = t - 1
         sent = (k >= 0) & (k < planes)
@@ -358,27 +411,184 @@
                     c_a, c_b = c_of(stat)
                     cpair[0, where, :] = jnp.broadcast_to(c_a, (some, rank))
                     cpair[1, where, :] = jnp.broadcast_to(c_b, (some, rank))
+                us[...] = jnp.where(first, uf[:, head], uf[:, tail])
+                qv[...] = jnp.where(first, qs[:, head], qs[:, tail])
             for j in range(per):
                 chain_back(per * b + j)
+            terms(ylo * trips + b)
+
+        @pl.when((b >= 1) & (b <= trips))
+        def _():
+            collect(ylo * trips + b - 1)
+
+            def landed(j, carry):
+                c = per * (b - 1) + j
+                give_arrived(c).wait_recv()
+                pass_arrived(c).wait_recv()
+                h_arrived(c).wait_recv()
+                return carry
+
+            lax.fori_loop(0, per, landed, 0)
+            terms((1 - ylo) * trips + b - 1)
+
+        @pl.when((b >= 2) & (b <= trips))
+        def _():
+            collect((1 - ylo) * trips + b - 2)
 
         return carry
 
-    lax.fori_loop(0, 2 * planes + trips, tick, 0)
-    u_out[...] = jnp.where(first, uf[:, head], uf[:, tail])
-    q_out[...] = jnp.where(first, qs[:, head], qs[:, tail])
+    lax.fori_loop(0, 2 * planes + trips + 1, tick, 0)
+    collect((1 - ylo) * trips + trips - 1)
+
+    total_a, total_b = scatter_sum(yh_n, x_n, sums, rax, rby, sa, ray, sb, rbx,
+                                   ax_send, ax_recv, by_send, by_recv, s_sem, bx_send, bx_recv)
+    cut = shard // 2
+    gw[0:cut] = total_a[:, head].astype(bf16)
+    gw[cut:shard] = total_b[:, head].astype(bf16)
+    gu[0:cut] = total_a[:, tail].astype(bf16)
+    gu[cut:shard] = total_b[:, tail].astype(bf16)
+    has_next = s < sections - 1
+    down_section = {"section": lax.rem(s + sections - 1, sections)}
+
+    def pair_of(sems, i):
+        return sems.at[2 * i], sems.at[2 * i + 1]
+
+    def w_x(i):
+        return remote(gw, own_w.at[yh, x, core], *pair_of(wx_sem, i), place(yh, xp(i), core))
+
+    def w_y(i):
+        spot = own_w.at[yh, xp(i), core]
+        return remote(gw if i == 0 else spot, spot, *pair_of(wy_sem, i), other_y)
+
+    def w_c(i):
+        spot = own_w.at[:, xp(i), core]
+        return remote(spot, spot, *pair_of(wc_sem, i), other_core)
+
+    v_y = remote(gu, own_u.at[yh, x, core], *pair_of(vx_sem, 0), other_y)
+
+    def v_x(i):
+        spot = own_u.at[:, x, core]
+        return remote(spot, spot, *pair_of(vx_sem, i), place(yh, xp(i), core))
+
+    def v_c(i):
+        spot = own_u.at[:, xp(i), core]
+        return remote(spot, spot, *pair_of(vc_sem, i), other_core)
+
+    next_copy = remote(nw, nxt_u.at[yh, x, core], *pair_of(nx_sem, 0), down_section)
+    bump_copy = remote(ub, bump_u, *pair_of(nx_sem, x_n), down_section)
+
+    def n_x(i):
+        spot = nxt_u.at[yh, x, core]
+        return remote(spot, spot, *pair_of(nx_sem, i), place(yh, xp(i), core))
+
+    def n_y(i):
+        spot = nxt_u.at[yh, xp(i), core]
+        return remote(spot, spot, *pair_of(ny_sem, i), other_y)
+
+    def n_c(i):
+        spot = nxt_u.at[:, xp(i), core]
+        return remote(spot, spot, *pair_of(nc_sem, i), other_core)
+
+    for i in range(1, x_n):
+        w_x(i).start()
+    v_y.start()
+    w_y(0).start()
+
+    @pl.when(s > 0)
+    def _():
+        nw[...] = (mine_u[...].astype(f32) - learn_rate * gu[...].astype(f32)).astype(bf16)
+        next_copy.start()
+
+    own_w[yh, x, core] = gw[...]
+    own_u[yh, x, core] = gu[...]
+    v_y.wait_recv()
+    for i in range(1, x_n):
+        w_x(x_n - i).wait_recv()
+        w_y(i).start()
+    for i in range(1, x_n):
+        v_x(i).start()
+    v_c(0).start()
+
+    @pl.when(has_next)
+    def _():
+        next_copy.wait_recv()
+        for i in range(1, x_n):
+            n_x(i).start()
+        n_y(0).start()
+
+    for i in range(x_n):
+        w_y(i).wait_recv()
+        w_c(i).start()
+
+    @pl.when(has_next)
+    def _():
+        for i in range(1, x_n):
+            n_x(x_n - i).wait_recv()
+            n_y(i).start()
+
+    for i in range(1, x_n):
+        v_x(x_n - i).wait_recv()
+        v_c(i).start()
+    for i in range(x_n):
+        w_c(i).wait()
+
+    @pl.when(s > 0)
+    def _():
+        def ahead(b, pre):
+            y_ = b // x_n
+            x_ = lax.rem(b, x_n)
+            cols = pl.ds(pl.multiple_of(b * 2 * shard, 128), 2 * shard)
+            both = jnp.concatenate([own_w[y_, x_, 0], own_w[y_, x_, 1]], axis=0)
+            fresh = wd[cols, :].astype(f32) - learn_rate * both.astype(f32)
+            return pre + dot_nn(xb[:, cols], fresh.astype(bf16))
+
+        pre = lax.fori_loop(0, yh_n * x_n, ahead, jnp.zeros((rows, rank), f32))
+        value, unused = gelu_pair(pre * lax.rsqrt(nacc[...] * (1.0 / width) + eps))
+        ub[...] = value.astype(bf16)
+        bump_copy.start()
+
+    @pl.when(has_next)
+    def _():
+        for i in range(x_n):
+            n_y(i).wait_recv()
+            n_c(i).start()
+        for i in range(x_n):
+            n_c(i).wait()
+            n_y(i).wait_send()
+        for i in range(1, x_n):
+            n_x(i).wait_send()
+        bump_copy.wait_recv()
+
+    for i in range(x_n):
+        v_c(i).wait()
+        w_y(i).wait_send()
+    for i in range(1, x_n):
+        w_x(i).wait_send()
+        v_x(i).wait_send()
+    v_y.wait_send()
+
+    @pl.when(s > 0)
+    def _():
+        next_copy.wait_send()
+        bump_copy.wait_send()
+
+    def core_settle(b, carry):
+        core_copy(b).wait_send()
+        return carry
+
+    lax.fori_loop(0, yh_n * x_n, core_settle, 0)
 
     def finish(c, carry):
         @pl.when(z < planes - 1)
         def _():
             x_copy(c).wait_send()
         give_copy(c).wait_send()
-        give_arrived(c).wait_recv()
+        pass_copy(c).wait_send()
 
         @pl.when(z > 0)
         def _():
             b_copy(c).wait_send()
         h_copy(c).wait_send()
-        h_arrived(c).wait_recv()
         return carry
 
     lax.fori_loop(0, chunks, finish, 0)
@@ -405,25 +615,35 @@
     qp_copy().wait_send()
 
 
-def recurrence(sections, pyh, n0, nn, x0, g16, up, wd, upart, wpart):
+def recurrence(sections, shards, pyh, n0, nn, x0, g16, up, wd, upart, wpart, mine_u):
     rows, width = x0.shape
     rank = up.shape[0]
     half = width // 2
     some = rows // 2
     planes = sections // 2
     chunks = 28
-    per = 4
+    per = 7
+    x_n = 4
+    yh_n = shards // (2 * x_n)
+    shard = mine_u.shape[0]
+    cut = shard // 2
+    blocks = yh_n * x_n
     vm = pl.BlockSpec(memory_space=pltpu.VMEM)
     dma = pltpu.SemaphoreType.DMA
     sq = (rows, rank)
     two = (some, 2 * rank)
-    wide = jax.ShapeDtypeStruct((rows, width), bf16)
     strip = pltpu.VMEM((rows, half), bf16)
+    full = jax.ShapeDtypeStruct((yh_n, x_n, 2, shard, rank), bf16)
+
+    def buf(*lead):
+        return pltpu.VMEM(lead + (2 * rank,), bf16)
+
     return pl.pallas_call(
-        functools.partial(recurrence_kernel, sections, chunks, per),
-        out_shape=(wide, wide, jax.ShapeDtypeStruct(sq, bf16), jax.ShapeDtypeStruct(sq, bf16)),
-        in_specs=[vm] * 9,
-        out_specs=(vm,) * 4,
+        functools.partial(recurrence_kernel, sections, chunks, per, yh_n, x_n),
+        out_shape=(jax.ShapeDtypeStruct((rows, width), bf16), full, full, full,
+                   jax.ShapeDtypeStruct(sq, bf16)),
+        in_specs=[vm] * 10,
+        out_specs=(vm,) * 5,
         scratch_shapes=[
             pltpu.VMEM((planes,) + two, bf16),
             pltpu.VMEM((planes, some + 16, 2 * rank), bf16),
@@ -438,11 +658,25 @@
             pltpu.VMEM((rows, 2 * rank), bf16),
             pltpu.VMEM((rows, 2 * rank), bf16),
             pltpu.VMEM((2,) + sq, f32),
-            strip, strip, strip, strip, strip, strip,
-        ] + [dma((planes,))] * 6 + [dma((10,))] + [dma((chunks,))] * 8,
+            strip, strip, strip, strip, strip, strip, strip,
+            pltpu.VMEM((rows, width), bf16),
+            pltpu.VMEM(sq, bf16), pltpu.VMEM(sq, bf16),
+            pltpu.VMEM((rows, width), bf16), pltpu.VMEM(sq, f32),
+            buf(blocks, 2, shard), buf(blocks, shard), buf(yh_n, x_n, shard),
+            buf(x_n - 1, yh_n, cut), buf(x_n, cut), buf(yh_n, cut), buf(cut),
+            buf(x_n, cut), buf(x_n - 1, cut),
+            pltpu.VMEM((shard, rank), bf16), pltpu.VMEM((shard, rank), bf16),
+            pltpu.VMEM((shard, rank), bf16), pltpu.VMEM(sq, bf16),
+        ] + [dma((planes,))] * 6 + [dma((10,))] + [dma((chunks,))] * 10 + [
+            dma((blocks,)), dma((blocks,)),
+            dma((yh_n * (x_n - 1),)), dma((yh_n * (x_n - 1),)), dma((x_n,)), dma((x_n,)), dma((2,)),
+            dma((x_n - 1,)), dma((x_n - 1,)),
+            dma((2 * x_n,)), dma((2 * x_n,)), dma((2 * x_n,)), dma((2 * x_n,)), dma((2 * x_n,)),
+            dma((2 * x_n + 2,)), dma((2 * x_n,)), dma((2 * x_n,)),
+        ],
         compiler_params=pltpu.CompilerParams(
-            collective_id=1, has_side_effects=True, vmem_limit_bytes=48 * 1024 * 1024),
-    )(pyh, n0, nn, x0, g16, up, wd, upart, wpart)
+            collective_id=1, has_side_effects=True, vmem_limit_bytes=56 * 1024 * 1024),
+    )(pyh, n0, nn, x0, g16, up, wd, upart, wpart, mine_u)
 
 
 def dp_place(x_n):
@@ -792,239 +1026,32 @@
     )(x0, g16, down, up, mine_u, base)
 
 
-def reduce_kernel(yh_n, x_n, sections, x1, g1, u_s, q_s, up, base, own, nxt,
-                  part, rc, sums, rax, rby, sa, ray, sb, rbx, gs, nw,
-                  c_send, c_recv, ax_send, ax_recv, by_send, by_recv, s_sem, bx_send, bx_recv,
-                  own_send, own_recv, oc_send, oc_recv, nx_send, nx_recv, ny_send, ny_recv,
-                  nc_send, nc_recv):
-    d = lax.axis_index("dp")
-    s = lax.axis_index("section")
-    yh = d // (2 * x_n)
-    x = lax.rem(d // 2, x_n)
-    core = lax.rem(d, 2)
-    rows = base.shape[0]
-    cut = rows // 2
-
-    def place(y_, x_, c_):
-        return {"dp": (y_ * x_n + x_) * 2 + c_}
-
-    def xp(i):
-        return lax.rem(x + i, x_n)
-
-    other_core = place(yh, x, 1 - core)
-    other_y = place(1 - yh, x, core)
-    up_section = lax.rem(s + 1, sections)
-    down_section = lax.rem(s + sections - 1, sections)
-
-    def copy(src, dst, send, recv, where):
-        return pltpu.make_async_remote_copy(src_ref=src, dst_ref=dst, send_sem=send, recv_sem=recv,
-                                            device_id=where, device_id_type=MESH)
-
-    barrier = pltpu.get_barrier_semaphore()
-    peers = [other_core, other_y, {"section": up_section}, {"section": down_section}]
-    peers += [place(yh, xp(i), core) for i in range(1, x_n)]
-    for where in peers:
-        pl.semaphore_signal(barrier, inc=1, device_id=where, device_id_type=MESH)
-    pl.semaphore_wait(barrier, len(peers))
-
-    def core_copy(b):
-        return copy(part.at[b, 1 - core], rc.at[b], c_send.at[b], c_recv.at[b], other_core)
-
-    def terms(b, carry):
-        cols = pl.ds(pl.multiple_of(b * 2 * rows, 128), 2 * rows)
-        u = u_s[...]
-        before = (x1[:, cols].astype(f32) - dot_nn(u, up[:, cols])).astype(bf16)
-        g_down = dot_tn(before, q_s[...]).astype(bf16)
-        g_up = dot_tn(g1[:, cols], u).astype(bf16)
-        rank = u.shape[1]
-        for half in range(2):
-            part[b, half, :, 0:rank] = g_down[half * rows:(half + 1) * rows]
-            part[b, half, :, rank:2 * rank] = g_up[half * rows:(half + 1) * rows]
-        core_copy(b).start()
-
-        @pl.when(b > 0)
-        def _():
-            collect(b - 1)
-        return carry
-
-    def collect(b):
-        block_sum(b, yh_n, x_n, core_copy, part, rc, sums, rax, rby,
-                  ax_send, ax_recv, by_send, by_recv)
-
-    blocks = yh_n * x_n
-    lax.fori_loop(0, blocks, terms, 0)
-    collect(blocks - 1)
-
-    total_a, total_b = scatter_sum(yh_n, x_n, sums, rax, rby, sa, ray, sb, rbx,
-                                   ax_send, ax_recv, by_send, by_recv, s_sem, bx_send, bx_recv)
-    gs[0:cut] = total_a.astype(bf16)
-    gs[cut:rows] = total_b.astype(bf16)
-    nw[...] = (base[...].astype(f32) - learn_rate * gs[...].astype(f32)).astype(bf16)
-
-    has_next = s < sections - 1
-    next_copy = copy(nw, nxt.at[yh, x, core], s_sem.at[4], s_sem.at[5], {"section": down_section})
-    own_y = copy(gs, own.at[yh, x, core], s_sem.at[6], s_sem.at[7], other_y)
-    own_y.start()
-
-    @pl.when(s > 0)
-    def _():
-        next_copy.start()
-
-    own[yh, x, core] = gs[...]
-
-    def own_x(i):
-        return copy(own.at[:, x, core], own.at[:, x, core], own_send.at[i - 1], own_recv.at[i - 1],
-                    place(yh, xp(i), core))
-
-    def own_c(i):
-        spot = own.at[:, xp(i), core]
-        return copy(spot, spot, oc_send.at[i], oc_recv.at[i], other_core)
-
-    def nxt_x(i):
-        spot = nxt.at[yh, x, core]
-        return copy(spot, spot, nx_send.at[i - 1], nx_recv.at[i - 1], place(yh, xp(i), core))
-
-    def nxt_y(i):
-        spot = nxt.at[yh, xp(i), core]
-        return copy(spot, spot, ny_send.at[i], ny_recv.at[i], other_y)
-
-    def nxt_c(i):
-        spot = nxt.at[:, xp(i), core]
-        return copy(spot, spot, nc_send.at[i], nc_recv.at[i], other_core)
-
-    @pl.when(has_next)
-    def _():
-        next_copy.wait_recv()
-        for i in range(1, x_n):
-            nxt_x(i).start()
-        nxt_y(0).start()
-
-    own_y.wait_recv()
-
-    @pl.when(has_next)
-    def _():
-        for i in range(1, x_n):
-            nxt_x(i).wait_send()
-
-    for i in range(1, x_n):
-        own_x(i).start()
-    own_c(0).start()
-
-    @pl.when(has_next)
-    def _():
-        for i in range(1, x_n):
-            nxt_x(x_n - i).wait_recv()
-            nxt_y(i).start()
-
-    for i in range(1, x_n):
-        own_x(x_n - i).wait_recv()
-        own_c(i).start()
-
-    @pl.when(has_next)
-    def _():
-        for i in range(x_n):
-            nxt_y(i).wait_recv()
-            nxt_c(i).start()
-        for i in range(x_n):
-            nxt_c(i).wait()
-            nxt_y(i).wait_send()
-
-    for i in range(x_n):
-        own_c(i).wait()
-    for i in range(1, x_n):
-        own_x(i).wait_send()
-    own_y.wait_send()
-
-    @pl.when(s > 0)
-    def _():
-        next_copy.wait_send()
-
-    def settle(b, carry):
-        core_copy(b).wait_send()
-        return carry
-
-    lax.fori_loop(0, blocks, settle, 0)
-
-
-def reduce_gather(sections, shards, x1, g1, u_s, q_s, up, base):
-    x_n = 4
-    yh_n = shards // (2 * x_n)
-    rows, cols = base.shape
-    cut = rows // 2
-    vm = pl.BlockSpec(memory_space=pltpu.VMEM)
-    dma = pltpu.SemaphoreType.DMA
-    full = jax.ShapeDtypeStruct((yh_n, x_n, 2, rows, cols), bf16)
-
-    def buf(*lead):
-        return pltpu.VMEM(lead + (cols,), bf16)
-
-    return pl.pallas_call(
-        functools.partial(reduce_kernel, yh_n, x_n, sections),
-        out_shape=(full, full),
-        in_specs=[vm] * 6,
-        out_specs=(vm, vm),
-        scratch_shapes=[
-            buf(yh_n * x_n, 2, rows), buf(yh_n * x_n, rows), buf(yh_n, x_n, rows),
-            buf(x_n - 1, yh_n, cut), buf(x_n, cut), buf(yh_n, cut), buf(cut),
-            buf(x_n, cut), buf(x_n - 1, cut), buf(rows), buf(rows),
-            dma((yh_n * x_n,)), dma((yh_n * x_n,)),
-            dma((yh_n * (x_n - 1),)), dma((yh_n * (x_n - 1),)), dma((x_n,)), dma((x_n,)), dma((8,)),
-            dma((x_n - 1,)), dma((x_n - 1,)), dma((x_n - 1,)), dma((x_n - 1,)),
-            dma((x_n,)), dma((x_n,)), dma((x_n - 1,)), dma((x_n - 1,)), dma((x_n,)), dma((x_n,)),
-            dma((x_n,)), dma((x_n,)),
-        ],
-        compiler_params=pltpu.CompilerParams(
-            collective_id=2, has_side_effects=True, vmem_limit_bytes=52 * 1024 * 1024),
-    )(x1, g1, u_s, q_s, up, base)
-
-
-def finish_kernel(sections, own, nxt, x1, grad_down, grad_up, advance):
+def finish_kernel(sections, own_w, own_u, nxt_u, bump_u, x1, grad_down, grad_up, advance):
     last = lax.axis_index("section") == sections - 1
+    grad_down[...] = own_w[...]
+    grad_up[...] = own_u[...].astype(f32).T.astype(bf16)
+    bump = dot_nt(bump_u[...], nxt_u[...])
+    advance[...] = (x1[...].astype(f32) + jnp.where(last, 0.0, bump)).astype(bf16)
+
+
+def finish(sections, own_w, own_u, nxt_u, bump_u, x1):
     rows, width = x1.shape
-    rank = grad_down.shape[1]
-    step = 896
-    count = width // step
-
-    def first(b, carry):
-        pre, norm = carry
-        here = pl.ds(pl.multiple_of(b * step, 128), step)
-        block = own[here, :]
-        grad_down[here, :] = block[:, 0:rank]
-        grad_up[:, here] = block[:, rank:2 * rank].astype(f32).T.astype(bf16)
-        x = x1[:, here]
-        values = x.astype(f32)
-        pre = pre + dot_nn(x, nxt[here, 0:rank])
-        return pre, norm + jnp.sum(values * values, axis=1, keepdims=True)
-
-    pre, norm = lax.fori_loop(
-        0, count, first, (jnp.zeros((rows, rank), f32), jnp.zeros((rows, 1), f32)))
-    value, unused = gelu_pair(pre * lax.rsqrt(norm * (1.0 / width) + eps))
-    value = value.astype(bf16)
-
-    def second(b, carry):
-        here = pl.ds(pl.multiple_of(b * step, 128), step)
-        bump = dot_nt(value, nxt[here, rank:2 * rank])
-        advance[:, here] = (x1[:, here].astype(f32) + jnp.where(last, 0.0, bump)).astype(bf16)
-        return carry
-
-    lax.fori_loop(0, count, second, 0)
-
-
-def finish(sections, own, nxt, x1):
-    rows, width = x1.shape
-    rank = own.shape[1] // 2
-    vm = pl.BlockSpec(memory_space=pltpu.VMEM)
+    rank = own_w.shape[1]
+    step = width // 4
+    tall = pl.BlockSpec((step, rank), lambda i: (i, 0))
+    flat = pl.BlockSpec((rows, step), lambda i: (0, i))
     return pl.pallas_call(
         functools.partial(finish_kernel, sections),
+        grid=(width // step,),
         out_shape=(
             jax.ShapeDtypeStruct((width, rank), bf16),
             jax.ShapeDtypeStruct((rank, width), bf16),
             jax.ShapeDtypeStruct((rows, width), bf16),
         ),
-        in_specs=[vm] * 3,
-        out_specs=(vm,) * 3,
-        compiler_params=pltpu.CompilerParams(vmem_limit_bytes=48 * 1024 * 1024),
-    )(own, nxt, x1)
+        in_specs=[tall, tall, tall, pl.BlockSpec((rows, rank), lambda i: (0, 0)), flat],
+        out_specs=(tall, flat, flat),
+        compiler_params=pltpu.CompilerParams(vmem_limit_bytes=32 * 1024 * 1024),
+    )(own_w, own_u, nxt_u, bump_u, x1)
 
 
 def per_device(inputs, cotangent, w_down, w_up):
@@ -1046,10 +1073,11 @@
     base = jnp.concatenate([mine_w, mine_u], axis=1)
     pyh, n0, grams, upart, wpart = grams_of(sections, shards, x0, g16, down, upward, mine_u, base)
     grams = grams.reshape(sections // 2, 2 * rank, 4 * rank)
-    x1, g1, u_s, q_s = recurrence(sections, pyh, n0, grams, x0, g16, upward, down, upart, wpart)
-    own, nxt = reduce_gather(sections, shards, x1, g1, u_s, q_s, upward, base)
-    wide = (width, 2 * rank)
-    grad_down, grad_up, advance = finish(sections, own.reshape(wide), nxt.reshape(wide), x1)
+    x1, own_w, own_u, nxt_u, bump_u = recurrence(
+        sections, shards, pyh, n0, grams, x0, g16, upward, down, upart, wpart, mine_u)
+    tall = (width, rank)
+    grad_down, grad_up, advance = finish(
+        sections, own_w.reshape(tall), own_u.reshape(tall), nxt_u.reshape(tall), bump_u, x1)
     return (grad_down[None], grad_up[None], advance.reshape(1, micro, batch_rows, width))
 
 

time: 270 us -> 261 us (0.967)
  Pallas kernels: 259 us -> 245 us
  local copies, waits for them, and re-layouts: 9.54 us -> 14.9 us
    pallas_call x2 -> x1, Pallas kernels: 95.3 us -> 3.28 us  [finish(): pl.pallas_call(functools.partial(finish_kernel, sections), grid=(width //...]
    pallas_call x1, Pallas kernels: 99.6 us -> 177 us  [recurrence(): pl.pallas_call(functools.partial(recurrence_kernel, sections, chunks, per...]
    unnamed x12 -> x24, local copies, waits for them, and re-layouts: 7.48 us -> 12.9 us
where the time goes in v7:
time: 261 us; the launch traced here: 260 us
  Pallas kernels  245 us (94%)
  local copies, waits for them, and re-layouts  14.9 us (6%)
    pallas_call x1, Pallas kernels, recurrence(): pl.pallas_call(functools.partial(recurrence_kernel, sections, chunks, per...  177 us
    pallas_call x1, Pallas kernels, grams_of(): pl.pallas_call(functools.partial(gram_kernel, yh_n, x_n, sections), out_s...  64.5 us
    unnamed x24, local copies, waits for them, and re-layouts  12.9 us

profile of v7, /device:TPU:1, one launch (start us, length us, event | category | flops | bytes accessed | tf_op | source)
XLA Modules:
  0.0 260.3 jit_solution(7761055316351580248)
XLA Ops:
  0.6 0.9 dynamic-slice_bitcast_fusion
  1.5 1.0 constant_dynamic-slice_fusion
  2.6 0.1 copy.7
  2.7 0.0 copy-start.2
  2.8 0.0 copy-start
  2.8 1.5 copy-done
  4.3 0.0 copy-start.1
  4.3 1.5 copy-done.1
  5.8 64.5 %shard_map.67 = (f32[3,64,256]{2,1,0:T(8,128)S(1)}, f32[64,128]{1,0:T(8,128)S(1)}, bf16[2,4,2,128,512]{4,3,2,1,0:T(8,128)(2,1)}, bf16[128,3584]{1,0:T(8,128)(2,1)S(1)}, bf16[3584,128]{1,0:T(8,128)(2,1)S(1)}) custom-call(bf16[128,7168]{1,0:T(8,128)(2,1)S(1)} %bitcast.17, bf16[128,7168]{1,0:T(8,128)(2,1)S(1)} %bitcast.19, bf16[7168,128]{1,0:T(8,128)(2,1)} %bitcast.28, ...), custom_call_target="tpu_custom_call" | custom-call | tf_op jit(solution)/shard_map/pallas_call | solution.py:999
  70.3 0.0 copy-done.2
  70.3 0.0 copy-start.7
  70.3 0.9 copy-done.7
  71.2 0.0 copy-start.8
  71.2 0.9 copy-done.8
  72.1 0.0 copy-start.9
  72.1 0.7 copy-done.9
  72.8 0.0 copy-start.11
  72.8 0.6 copy-done.11
  73.4 176.9 %shard_map.68 = (bf16[128,7168]{1,0:T(8,128)(2,1)}, bf16[2,4,2,448,128]{4,3,2,1,0:T(8,128)(2,1)}, bf16[2,4,2,448,128]{4,3,2,1,0:T(8,128)(2,1)}, bf16[2,4,2,448,128]{4,3,2,1,0:T(8,128)(2,1)}, bf16[128,128]{1,0:T(8,128)(2,1)}) custom-call(f32[3,64,256]{2,1,0:T(8,128)} %copy-done.9, f32[64,128]{1,0:T(8,128)} %copy-done.11, bf16[8,256,512]{2,1,0:T(8,128)(2,1)} %bitcast.30, ...), custom_call_target="tpu_custom_call" | custom-call | tf_op jit(solution)/shard_map/pallas_call | solution.py:641
  250.3 0.0 copy-start.3
  250.3 1.5 copy-done.3
  251.8 0.0 copy-start.4
  251.8 1.5 copy-done.4
  253.3 0.0 copy-start.5
  253.3 1.5 copy-done.5
  254.8 0.0 copy-start.6
  254.8 1.5 copy-done.6
  256.3 0.0 copy-start.10
  256.3 0.8 copy-done.10
  257.0 3.3 %shard_map.69 = (bf16[7168,128]{1,0:T(8,128)(2,1)}, bf16[128,7168]{1,0:T(8,128)(2,1)}, bf16[128,7168]{1,0:T(8,128)(2,1)}) custom-call(bf16[7168,128]{1,0:T(8,128)(2,1)S(1)} %bitcast.23, bf16[7168,128]{1,0:T(8,128)(2,1)S(1)} %bitcast.24, bf16[7168,128]{1,0:T(8,128)(2,1)S(1)} %bitcast.25, bf16[128,128]{1,0:T(8,128)(2,1)S(1)} %copy-done.10, ...), custom_call_target="tpu_custom_call" | custom-call | tf_op jit(solution)/shard_map/pallas_call | solution.py:1043
  (1 shorter events, 0.0 us)
Async XLA Ops:
  2.7 67.6 %copy-start.2 = (bf16[1,128,448]{1,2,0:T(8,128)(2,1)}, bf16[1,128,448]{1,2,0:T(8,128)(2,1)S(1)}, u32[]{:S(2)}) copy-start(bf16[1,128,448]{1,2,0:T(8,128)(2,1)S(1)} %copy.7) | copy-start | bytes 344068
  2.8 1.5 copy-start
  4.3 1.5 copy-start.1
  70.3 0.9 copy-start.7
  71.2 0.9 copy-start.8
  72.1 0.7 copy-start.9
  72.8 0.6 copy-start.11
  250.3 1.5 copy-start.3
  251.8 1.5 copy-start.4
  253.3 1.5 copy-start.5
  254.8 1.5 copy-start.6
  256.3 0.8 copy-start.10

commit v8 on v7

--- a/solution.py
+++ b/solution.py
@@ -38,11 +38,11 @@
 def recurrence_kernel(sections, chunks, per, yh_n, x_n,
                       pyh, n0, nn, x0, g16, up, wd, upart, wpart, mine_u,
                       xout, own_w, own_u, nxt_u, bump_u,
-                      ul, ql, qp, mb, ys, nl, nsend, acc, hacc, slope, act, rinv, uf, qs, cpair,
-                      xin, xkeep, xgive, gin, gkeep, ggive, xpass,
+                      ul, ql, qp, ys, nl, nsend, acc, hacc, slope, act, rinv, uf, qs, cpair,
+                      xin, xkeep, xgive, gin, gkeep, ggive, xpass, delta,
                       gout, us, qv, xb, nacc, part, rc, sums, rax, rby, sa, ray, sb, rbx,
                       gw, gu, nw, ub,
-                      u_send, u_recv, q_send, q_recv, m_send, m_recv, e_sem,
+                      u_send, u_recv, q_send, q_recv, e_sem,
                       c_send, c_recv, g_send, g_recv,
                       b_send, b_recv, h_send, h_recv, p_send, p_recv,
                       k_send, k_recv, ax_send, ax_recv, by_send, by_recv, s_sem, bx_send, bx_recv,
@@ -161,73 +161,78 @@
     def q_arrived(k):
         return remote(ql.at[k], ql.at[k], q_send.at[0], q_recv.at[k], plane(peer(1)))
 
-    def m_copy(j):
-        return remote(nn.at[j, :, 0:2 * rank], mb.at[z], m_send.at[j], m_recv.at[z], plane(j))
-
-    def m_arrived(k):
-        return remote(mb.at[k], mb.at[k], m_send.at[0], m_recv.at[k], plane(peer(1)))
-
     acc[:, 0:2 * rank] = pyh[0]
     acc[:, 2 * rank:4 * rank] = pyh[1]
     hacc[...] = pyh[2]
 
-    def start_m(j, carry):
-        m_copy(j).start()
-        return carry
-
-    lax.fori_loop(0, z, start_m, 0)
-
-    def chain(c):
-        @pl.when(z > 0)
-        def _():
-            x_copy(c).wait_recv()
-
-        here = columns(ylo * half, c)
-        there = columns(0, c)
-        start = jnp.where(z > 0, xin[:, there], x0[:, here]).astype(f32)
-        ours = up[:, here]
-        other = upart[:, there]
-        x_a = (start + dot_nn(uf[:, head], jnp.where(first, ours, other))).astype(bf16)
-        x_b = (x_a.astype(f32) + dot_nn(uf[:, tail], jnp.where(first, other, ours))).astype(bf16)
-        xkeep[:, there] = x_b
-
-        @pl.when(z < planes - 1)
-        def _():
-            x_copy(c).start()
-
-        xgive[:, there] = jnp.where(first, x_b, x_a)
-        give_copy(c).start()
-        xout[:, here] = jnp.where(first, x_a, x_b)
-        start = start.astype(bf16)
-        xpass[:, there] = jnp.where(first, x_a, start)
-        pass_copy(c).start()
-        xb[:, here] = jnp.where(first, start, x_a)
-
-    def chain_back(c):
-        @pl.when(z < planes - 1)
-        def _():
-            b_copy(c).wait_recv()
-
-        here = columns(ylo * half, c)
-        there = columns(0, c)
+    batch = per * piece
+
+    def wide_columns(base, p):
+        return pl.ds(pl.multiple_of(base + p * batch, 128), batch)
+
+    def chain(p):
+        ours = up[:, wide_columns(ylo * half, p)]
+        other = upart[:, wide_columns(0, p)]
+        grow = dot_nn(uf[:, head], jnp.where(first, ours, other))
+        delta[0] = grow
+        delta[1] = grow + dot_nn(uf[:, tail], jnp.where(first, other, ours))
+        for j in range(per):
+            c = per * p + j
+
+            @pl.when(z > 0)
+            def _():
+                x_copy(c).wait_recv()
+
+            here = columns(ylo * half, c)
+            there = columns(0, c)
+            lane = slice(j * piece, (j + 1) * piece)
+            start = jnp.where(z > 0, xin[:, there], x0[:, here])
+            x_a = (start.astype(f32) + delta[0, :, lane]).astype(bf16)
+            x_b = (start.astype(f32) + delta[1, :, lane]).astype(bf16)
+            xkeep[:, there] = x_b
+
+            @pl.when(z < planes - 1)
+            def _():
+                x_copy(c).start()
+
+            xpass[:, there] = jnp.where(first, x_a, start)
+            pass_copy(c).start()
+            xgive[:, there] = jnp.where(first, x_b, x_a)
+            xout[:, here] = jnp.where(first, x_a, x_b)
+            xb[:, here] = jnp.where(first, start, x_a)
+
+    def chain_back(p):
+        here = wide_columns(ylo * half, p)
+        there = wide_columns(0, p)
         ours = wd[here, :]
         other = wpart[there, :]
-        g_b = jnp.where(z < planes - 1, gin[:, there], g16[:, here])
-        x_a = jnp.where(z > 0, xin[:, there], x0[:, here]).astype(f32)
-        x_b = jnp.where(first, xout[:, here], xgive[:, there]).astype(f32)
-        g_a = (g_b.astype(f32) + dot_nt(qs[:, tail], jnp.where(first, other, ours))
-               - cpair[1, :, 0:1] * x_b).astype(bf16)
-        g_0 = (g_a.astype(f32) + dot_nt(qs[:, head], jnp.where(first, ours, other))
-               - cpair[0, :, 0:1] * x_a).astype(bf16)
-
-        @pl.when(z > 0)
-        def _():
-            gkeep[:, there] = g_0
-            b_copy(c).start()
-
-        ggive[:, there] = jnp.where(first, g_b, g_a)
-        h_copy(c).start()
-        gout[:, here] = jnp.where(first, g_a, g_b)
+        x_a = jnp.where(first, xb[:, here], xpass[:, there]).astype(f32)
+        x_b = jnp.where(first, xpass[:, there], xb[:, here]).astype(f32)
+        grow = dot_nt(qs[:, tail], jnp.where(first, other, ours)) - cpair[1, :, 0:1] * x_b
+        delta[0] = grow
+        delta[1] = (grow + dot_nt(qs[:, head], jnp.where(first, ours, other))
+                    - cpair[0, :, 0:1] * x_a)
+        for j in range(per):
+            c = per * p + j
+
+            @pl.when(z < planes - 1)
+            def _():
+                b_copy(c).wait_recv()
+
+            here = columns(ylo * half, c)
+            there = columns(0, c)
+            lane = slice(j * piece, (j + 1) * piece)
+            g_b = jnp.where(z < planes - 1, gin[:, there], g16[:, here])
+            g_a = (g_b.astype(f32) + delta[0, :, lane]).astype(bf16)
+
+            @pl.when(z > 0)
+            def _():
+                gkeep[:, there] = (g_b.astype(f32) + delta[1, :, lane]).astype(bf16)
+                b_copy(c).start()
+
+            ggive[:, there] = jnp.where(first, g_b, g_a)
+            h_copy(c).start()
+            gout[:, here] = jnp.where(first, g_a, g_b)
 
     def forward_own():
         @pl.when(z > 0)
@@ -379,10 +384,9 @@
 
         @pl.when((r < planes) & (r > z))
         def _():
-            m_arrived(r).wait_recv()
             q_arrived(r).wait_recv()
             c_a, c_b = c_of(ql[r, some:some + 16, :])
-            hacc[...] += (dot_nt(ql[r, 0:some, :], mb[r]) - c_a * ys[2 * r] - c_b * ys[2 * r + 1])
+            hacc[...] += (dot_nn(ql[r, 0:some, :], nn[r, :, 0:2 * rank]) - c_a * ys[2 * r] - c_b * ys[2 * r + 1])
 
         @pl.when(t == 2 * planes - 1 - z)
         def _():
@@ -395,8 +399,14 @@
             @pl.when(p == 0)
             def _():
                 uf_arrived().wait_recv()
-            for j in range(per):
-                chain(per * p + j)
+            chain(p)
+
+        q = t - (z + 1 + trips)
+
+        @pl.when((q >= 0) & (q < chunks // 4))
+        def _():
+            for j in range(4):
+                give_copy(4 * q + j).start()
 
         b = t - (2 * planes - z)
 
@@ -413,8 +423,7 @@
                     cpair[1, where, :] = jnp.broadcast_to(c_b, (some, rank))
                 us[...] = jnp.where(first, uf[:, head], uf[:, tail])
                 qv[...] = jnp.where(first, qs[:, head], qs[:, tail])
-            for j in range(per):
-                chain_back(per * b + j)
+            chain_back(b)
             terms(ylo * trips + b)
 
         @pl.when((b >= 1) & (b <= trips))
@@ -423,7 +432,6 @@
 
             def landed(j, carry):
                 c = per * (b - 1) + j
-                give_arrived(c).wait_recv()
                 pass_arrived(c).wait_recv()
                 h_arrived(c).wait_recv()
                 return carry
@@ -583,6 +591,7 @@
         def _():
             x_copy(c).wait_send()
         give_copy(c).wait_send()
+        give_arrived(c).wait_recv()
         pass_copy(c).wait_send()
 
         @pl.when(z > 0)
@@ -607,7 +616,6 @@
 
     def settle(j, carry):
         q_copy(j).wait_send()
-        m_copy(j).wait_send()
         return carry
 
     lax.fori_loop(0, z, settle, 0)
@@ -648,7 +656,6 @@
             pltpu.VMEM((planes,) + two, bf16),
             pltpu.VMEM((planes, some + 16, 2 * rank), bf16),
             pltpu.VMEM((some + 16, 2 * rank), bf16),
-            pltpu.VMEM((planes, 2 * rank, 2 * rank), bf16),
             pltpu.VMEM((sections,) + two, f32),
             pltpu.VMEM((8, rank), f32),
             pltpu.VMEM((8, rank), f32),
@@ -659,6 +666,7 @@
             pltpu.VMEM((rows, 2 * rank), bf16),
             pltpu.VMEM((2,) + sq, f32),
             strip, strip, strip, strip, strip, strip, strip,
+            pltpu.VMEM((2, rows, half * per // chunks), f32),
             pltpu.VMEM((rows, width), bf16),
             pltpu.VMEM(sq, bf16), pltpu.VMEM(sq, bf16),
             pltpu.VMEM((rows, width), bf16), pltpu.VMEM(sq, f32),
@@ -667,7 +675,7 @@
             buf(x_n, cut), buf(x_n - 1, cut),
             pltpu.VMEM((shard, rank), bf16), pltpu.VMEM((shard, rank), bf16),
             pltpu.VMEM((shard, rank), bf16), pltpu.VMEM(sq, bf16),
-        ] + [dma((planes,))] * 6 + [dma((10,))] + [dma((chunks,))] * 10 + [
+        ] + [dma((planes,))] * 4 + [dma((10,))] + [dma((chunks,))] * 10 + [
             dma((blocks,)), dma((blocks,)),
             dma((yh_n * (x_n - 1),)), dma((yh_n * (x_n - 1),)), dma((x_n,)), dma((x_n,)), dma((2,)),
             dma((x_n - 1,)), dma((x_n - 1,)),
@@ -768,10 +776,10 @@
 
 
 def gram_kernel(yh_n, x_n, sections, x0, g16, down, up, mine_u, base, pyh, n0, out, upart, wpart,
-                allu, part, rc, sums, rax, rby, sa, ray, sb, rbx, gs, gp, two, mine3, theirs3,
+                allu, part, rc, sums, rax, rby, sa, ray, sb, rbx, gs, gp, two, mine3, theirs3, flip, turned,
                 z_sem, f_send, f_recv, r_send, r_recv,
                 c_send, c_recv, ax_send, ax_recv, by_send, by_recv, s_sem, bx_send, bx_recv,
-                ga_send, ga_recv, gb_send, gb_recv, gc_send, gc_recv):
+                ga_send, ga_recv, gb_send, gb_recv, gc_send, gc_recv, t_sem):
     yh, x, core = dp_place(x_n)
     s = lax.axis_index("section")
     z_n = sections // 2
@@ -801,7 +809,25 @@
     peers += [place(yh, xp(i), core) for i in range(1, x_n)]
     for where in peers:
         pl.semaphore_signal(barrier, inc=1, device_id=where, device_id_type=MESH)
-    pl.semaphore_wait(barrier, len(peers))
+    d = lax.axis_index("dp")
+    above = d // 2 < z
+    below = d // 2 > z
+    mirror = [{"section": 2 * (d // 2) + i, "dp": s} for i in range(2)]
+
+    @pl.when(below)
+    def _():
+        for i in range(2):
+            pl.semaphore_signal(barrier, inc=1, device_id={"section": d, "dp": 2 * z + i},
+                                device_id_type=MESH)
+
+    pl.semaphore_wait(barrier, len(peers) + 2 * above.astype(jnp.int32))
+
+    def flip_copy(i):
+        k = lax.rem(d, 2)
+        return remote(flip, turned.at[k], t_sem.at[i], t_sem.at[2 + k], mirror[i])
+
+    def flip_arrived(i):
+        return remote(flip, turned.at[i], t_sem.at[0], t_sem.at[2 + i], mirror[0])
 
     pair = remote(mine_u, allu.at[z, ylo], z_sem.at[0], z_sem.at[1], partner)
 
@@ -903,6 +929,12 @@
     swap = remote(gs, gp, z_sem.at[4], z_sem.at[5], partner)
     swap.start()
 
+    @pl.when(above)
+    def _():
+        flip[...] = gs[:, 0:rank].astype(f32).T.astype(bf16)
+        for i in range(2):
+            flip_copy(i).start()
+
     def lanes(base, which):
         return pl.ds(pl.multiple_of(base + which * rank, 128), rank)
 
@@ -914,6 +946,12 @@
     swap.wait_recv()
     two[:, lanes(0, 1 - ylo)] = gp[:, 0:rank]
     two[:, lanes(2 * rank, 1 - ylo)] = gp[:, rank:2 * rank]
+
+    @pl.when(below)
+    def _():
+        for i in range(2):
+            flip_arrived(i).wait_recv()
+            two[:, i * rank:(i + 1) * rank] = turned[i]
     out[yh, x, core] = two[...]
 
     low = pl.ds(0, cut)
@@ -967,6 +1005,11 @@
     pair.wait_send()
     swap.wait_send()
     swap3.wait_send()
+
+    @pl.when(above)
+    def _():
+        for i in range(2):
+            flip_copy(i).wait_send()
     swap_u.wait_send()
     swap_w.wait_send()
     share_u.wait()
@@ -1014,12 +1057,13 @@
             buf(x_n, cut), buf(x_n - 1, cut), buf(rank), buf(rank),
             pltpu.VMEM((rank, 4 * rank), bf16),
             pltpu.VMEM((3, rows, rank), f32), pltpu.VMEM((3, rows // 2, rank), f32),
+            pltpu.VMEM((rank, rank), bf16), pltpu.VMEM((2, rank, rank), bf16),
             dma((14,)), dma((sections // 2,)), dma((sections // 2,)),
             dma((sections // 2,)), dma((sections // 2,)),
             dma((yh_n * x_n,)), dma((yh_n * x_n,)),
             dma((yh_n * (x_n - 1),)), dma((yh_n * (x_n - 1),)), dma((x_n,)), dma((x_n,)), dma((4,)),
             dma((x_n - 1,)), dma((x_n - 1,)),
-            dma((x_n,)), dma((x_n,)), dma((2 * x_n,)), dma((2 * x_n,)), dma((x_n,)), dma((x_n,)),
+            dma((x_n,)), dma((x_n,)), dma((2 * x_n,)), dma((2 * x_n,)), dma((x_n,)), dma((x_n,)), dma((4,)),
         ],
         compiler_params=pltpu.CompilerParams(
             collective_id=3, has_side_effects=True, vmem_limit_bytes=48 * 1024 * 1024),

time: 261 us -> 242 us (0.927)
  Pallas kernels: 245 us -> 226 us
    pallas_call x1, Pallas kernels: 177 us -> 154 us  [recurrence(): pl.pallas_call(functools.partial(recurrence_kernel, sections, chunks, per...]
    pallas_call x1, Pallas kernels: 64.5 us -> 69.1 us  [grams_of(): pl.pallas_call(functools.partial(gram_kernel, yh_n, x_n, sections), out_s...]
where the time goes in v8:
time: 242 us
  Pallas kernels  226 us (93%)
  local copies, waits for them, and re-layouts  14.9 us (6%)
    pallas_call x1, Pallas kernels, recurrence(): pl.pallas_call(functools.partial(recurrence_kernel, sections, chunks, per...  154 us
    pallas_call x1, Pallas kernels, grams_of(): pl.pallas_call(functools.partial(gram_kernel, yh_n, x_n, sections), out_s...  69.1 us
    unnamed x24, local copies, waits for them, and re-layouts  12.9 us

profile of v8, /device:TPU:1, one launch (start us, length us, event | category | flops | bytes accessed | tf_op | source)
XLA Modules:
  0.0 242.1 jit_solution(3983199940020467067)
XLA Ops:
  0.6 0.9 dynamic-slice_bitcast_fusion
  1.5 1.0 constant_dynamic-slice_fusion
  2.6 0.1 copy.7
  2.7 0.0 copy-start.2
  2.8 0.0 copy-start
  2.8 1.5 copy-done
  4.3 0.0 copy-start.1
  4.3 1.5 copy-done.1
  5.8 69.1 %shard_map.67 = (f32[3,64,256]{2,1,0:T(8,128)S(1)}, f32[64,128]{1,0:T(8,128)S(1)}, bf16[2,4,2,128,512]{4,3,2,1,0:T(8,128)(2,1)}, bf16[128,3584]{1,0:T(8,128)(2,1)S(1)}, bf16[3584,128]{1,0:T(8,128)(2,1)S(1)}) custom-call(bf16[128,7168]{1,0:T(8,128)(2,1)S(1)} %bitcast.17, bf16[128,7168]{1,0:T(8,128)(2,1)S(1)} %bitcast.19, bf16[7168,128]{1,0:T(8,128)(2,1)} %bitcast.28, ...), custom_call_target="tpu_custom_call" | custom-call | tf_op jit(solution)/shard_map/pallas_call | solution.py:1042
  74.9 0.0 copy-done.2
  74.9 0.0 copy-start.7
  74.9 0.9 copy-done.7
  75.8 0.0 copy-start.8
  75.8 0.9 copy-done.8
  76.7 0.0 copy-start.9
  76.7 0.7 copy-done.9
  77.4 0.0 copy-start.11
  77.4 0.6 copy-done.11
  78.0 154.0 %shard_map.68 = (bf16[128,7168]{1,0:T(8,128)(2,1)}, bf16[2,4,2,448,128]{4,3,2,1,0:T(8,128)(2,1)}, bf16[2,4,2,448,128]{4,3,2,1,0:T(8,128)(2,1)}, bf16[2,4,2,448,128]{4,3,2,1,0:T(8,128)(2,1)}, bf16[128,128]{1,0:T(8,128)(2,1)}) custom-call(f32[3,64,256]{2,1,0:T(8,128)} %copy-done.9, f32[64,128]{1,0:T(8,128)} %copy-done.11, bf16[8,256,512]{2,1,0:T(8,128)(2,1)} %bitcast.30, ...), custom_call_target="tpu_custom_call" | custom-call | tf_op jit(solution)/shard_map/pallas_call | solution.py:649
  232.0 0.0 copy-start.3
  232.1 1.5 copy-done.3
  233.5 0.0 copy-start.4
  233.5 1.5 copy-done.4
  235.0 0.0 copy-start.5
  235.0 1.5 copy-done.5
  236.5 0.0 copy-start.6
  236.5 1.5 copy-done.6
  238.0 0.0 copy-start.10
  238.0 0.8 copy-done.10
  238.8 3.3 %shard_map.69 = (bf16[7168,128]{1,0:T(8,128)(2,1)}, bf16[128,7168]{1,0:T(8,128)(2,1)}, bf16[128,7168]{1,0:T(8,128)(2,1)}) custom-call(bf16[7168,128]{1,0:T(8,128)(2,1)S(1)} %bitcast.23, bf16[7168,128]{1,0:T(8,128)(2,1)S(1)} %bitcast.24, bf16[7168,128]{1,0:T(8,128)(2,1)S(1)} %bitcast.25, bf16[128,128]{1,0:T(8,128)(2,1)S(1)} %copy-done.10, ...), custom_call_target="tpu_custom_call" | custom-call | tf_op jit(solution)/shard_map/pallas_call | solution.py:1087
  (1 shorter events, 0.0 us)
Async XLA Ops:
  2.7 72.2 %copy-start.2 = (bf16[1,128,448]{1,2,0:T(8,128)(2,1)}, bf16[1,128,448]{1,2,0:T(8,128)(2,1)S(1)}, u32[]{:S(2)}) copy-start(bf16[1,128,448]{1,2,0:T(8,128)(2,1)S(1)} %copy.7) | copy-start | bytes 344068
  2.8 1.5 copy-start
  4.3 1.5 copy-start.1
  74.9 0.9 copy-start.7
  75.8 0.9 copy-start.8
  76.7 0.7 copy-start.9
  77.4 0.6 copy-start.11
  232.0 1.5 copy-start.3
  233.5 1.5 copy-start.4
  235.0 1.5 copy-start.5
  236.5 1.5 copy-start.6
  238.0 0.8 copy-start.10

commit v9 on v8

--- a/solution.py
+++ b/solution.py
@@ -36,17 +36,22 @@
 
 
 def recurrence_kernel(sections, chunks, per, yh_n, x_n,
-                      pyh, n0, nn, x0, g16, up, wd, upart, wpart, mine_u,
+                      pyh, n0, nn, x0_far, g16_far, up_far, wd_far, upart_far, wpart_far, mine_u,
                       xout, own_w, own_u, nxt_u, bump_u,
                       ul, ql, qp, ys, nl, nsend, acc, hacc, slope, act, rinv, uf, qs, cpair,
                       xin, xkeep, xgive, gin, gkeep, ggive, xpass, delta,
                       gout, us, qv, xb, nacc, part, rc, sums, rax, rby, sa, ray, sb, rbx,
-                      gw, gu, nw, ub,
+                      gw, gu, nw, ub, x0, g16, up, wd, upart, wpart, l_sem,
                       u_send, u_recv, q_send, q_recv, e_sem,
                       c_send, c_recv, g_send, g_recv,
                       b_send, b_recv, h_send, h_recv, p_send, p_recv,
                       k_send, k_recv, ax_send, ax_recv, by_send, by_recv, s_sem, bx_send, bx_recv,
                       wx_sem, wy_sem, wc_sem, vx_sem, vc_sem, nx_sem, ny_sem, nc_sem):
+    loads = [pltpu.make_async_copy(far, near, l_sem.at[i]) for i, (far, near) in enumerate((
+        (up_far, up), (upart_far, upart), (x0_far, x0),
+        (wd_far, wd), (wpart_far, wpart), (g16_far, g16)))]
+    for load in loads:
+        load.start()
     s = lax.axis_index("section")
     yh, x, core = dp_place(x_n)
     planes = sections // 2
@@ -398,6 +403,8 @@
         def _():
             @pl.when(p == 0)
             def _():
+                for load in loads[:3]:
+                    load.wait()
                 uf_arrived().wait_recv()
             chain(p)
 
@@ -414,6 +421,8 @@
         def _():
             @pl.when(b == 0)
             def _():
+                for load in loads[3:]:
+                    load.wait()
                 qp_copy().wait_recv()
                 qs[mine, :] = ql[z, 0:some, :]
                 qs[theirs, :] = qp[0:some, :]
@@ -650,7 +659,7 @@
         functools.partial(recurrence_kernel, sections, chunks, per, yh_n, x_n),
         out_shape=(jax.ShapeDtypeStruct((rows, width), bf16), full, full, full,
                    jax.ShapeDtypeStruct(sq, bf16)),
-        in_specs=[vm] * 10,
+        in_specs=[vm] * 3 + [pl.BlockSpec(memory_space=pl.ANY)] * 6 + [vm],
         out_specs=(vm,) * 5,
         scratch_shapes=[
             pltpu.VMEM((planes,) + two, bf16),
@@ -675,6 +684,9 @@
             buf(x_n, cut), buf(x_n - 1, cut),
             pltpu.VMEM((shard, rank), bf16), pltpu.VMEM((shard, rank), bf16),
             pltpu.VMEM((shard, rank), bf16), pltpu.VMEM(sq, bf16),
+            pltpu.VMEM((rows, width), bf16), pltpu.VMEM((rows, width), bf16),
+            pltpu.VMEM((rank, width), bf16), pltpu.VMEM((width, rank), bf16),
+            pltpu.VMEM((rank, half), bf16), pltpu.VMEM((half, rank), bf16), dma((6,)),
         ] + [dma((planes,))] * 4 + [dma((10,))] + [dma((chunks,))] * 10 + [
             dma((blocks,)), dma((blocks,)),
             dma((yh_n * (x_n - 1),)), dma((yh_n * (x_n - 1),)), dma((x_n,)), dma((x_n,)), dma((2,)),
@@ -683,7 +695,7 @@
             dma((2 * x_n + 2,)), dma((2 * x_n,)), dma((2 * x_n,)),
         ],
         compiler_params=pltpu.CompilerParams(
-            collective_id=1, has_side_effects=True, vmem_limit_bytes=56 * 1024 * 1024),
+            collective_id=1, has_side_effects=True, vmem_limit_bytes=60 * 1024 * 1024),
     )(pyh, n0, nn, x0, g16, up, wd, upart, wpart, mine_u)
 
 
@@ -775,11 +787,16 @@
     return total_a, total_b
 
 
-def gram_kernel(yh_n, x_n, sections, x0, g16, down, up, mine_u, base, pyh, n0, out, upart, wpart,
+def gram_kernel(yh_n, x_n, sections, x0_far, g16_far, down_far, up_far, mine_u, base, pyh, n0, out, upart, wpart,
                 allu, part, rc, sums, rax, rby, sa, ray, sb, rbx, gs, gp, two, mine3, theirs3, flip, turned,
+                x0, g16, down, up, l_sem,
                 z_sem, f_send, f_recv, r_send, r_recv,
                 c_send, c_recv, ax_send, ax_recv, by_send, by_recv, s_sem, bx_send, bx_recv,
                 ga_send, ga_recv, gb_send, gb_recv, gc_send, gc_recv, t_sem):
+    loads = [pltpu.make_async_copy(far, near, l_sem.at[i]) for i, (far, near) in enumerate((
+        (up_far, up), (down_far, down), (x0_far, x0), (g16_far, g16)))]
+    for load in loads:
+        load.start()
     yh, x, core = dp_place(x_n)
     s = lax.axis_index("section")
     z_n = sections // 2
@@ -874,6 +891,8 @@
     swap_w = remote(down.at[far, :], wpart.at[near, :], z_sem.at[8], z_sem.at[9], partner)
     share_u = remote(upart.at[:, near], upart.at[:, near], z_sem.at[10], z_sem.at[11], other_core)
     share_w = remote(wpart.at[near, :], wpart.at[near, :], z_sem.at[12], z_sem.at[13], other_core)
+    for load in loads:
+        load.wait()
     swap_u.start()
     swap_w.start()
 
@@ -1048,7 +1067,7 @@
             jax.ShapeDtypeStruct((rank, width // 2), bf16),
             jax.ShapeDtypeStruct((width // 2, rank), bf16),
         ),
-        in_specs=[vm] * 6,
+        in_specs=[pl.BlockSpec(memory_space=pl.ANY)] * 4 + [vm] * 2,
         out_specs=(vm,) * 5,
         scratch_shapes=[
             pltpu.VMEM((sections // 2, 2, height, rank), bf16),
@@ -1058,6 +1077,8 @@
             pltpu.VMEM((rank, 4 * rank), bf16),
             pltpu.VMEM((3, rows, rank), f32), pltpu.VMEM((3, rows // 2, rank), f32),
             pltpu.VMEM((rank, rank), bf16), pltpu.VMEM((2, rank, rank), bf16),
+            pltpu.VMEM((rows, width), bf16), pltpu.VMEM((rows, width), bf16),
+            pltpu.VMEM((width, rank), bf16), pltpu.VMEM((rank, width), bf16), dma((4,)),
             dma((14,)), dma((sections // 2,)), dma((sections // 2,)),
             dma((sections // 2,)), dma((sections // 2,)),
             dma((yh_n * x_n,)), dma((yh_n * x_n,)),
@@ -1066,7 +1087,7 @@
             dma((x_n,)), dma((x_n,)), dma((2 * x_n,)), dma((2 * x_n,)), dma((x_n,)), dma((x_n,)), dma((4,)),
         ],
         compiler_params=pltpu.CompilerParams(
-            collective_id=3, has_side_effects=True, vmem_limit_bytes=48 * 1024 * 1024),
+            collective_id=3, has_side_effects=True, vmem_limit_bytes=60 * 1024 * 1024),
     )(x0, g16, down, up, mine_u, base)
 
 
@@ -1094,7 +1115,7 @@
         ),
         in_specs=[tall, tall, tall, pl.BlockSpec((rows, rank), lambda i: (0, 0)), flat],
         out_specs=(tall, flat, flat),
-        compiler_params=pltpu.CompilerParams(vmem_limit_bytes=32 * 1024 * 1024),
+        compiler_params=pltpu.CompilerParams(vmem_limit_bytes=60 * 1024 * 1024),
     )(own_w, own_u, nxt_u, bump_u, x1)
 
 

time: 242 us -> 231 us (0.955)
  local copies, waits for them, and re-layouts: 14.9 us -> 2.07 us
    unnamed x24 -> x2, local copies, waits for them, and re-layouts: 12.9 us -> 0.01 us
    pallas_call x1, Pallas kernels: 3.27 us -> 6.33 us  [finish(): pl.pallas_call(functools.partial(finish_kernel, sections), grid=(width //...]
where the time goes in v9:
time: 231 us
  Pallas kernels  227 us (98%)
    pallas_call x1, Pallas kernels, recurrence(): pl.pallas_call(functools.partial(recurrence_kernel, sections, chunks, per...  152 us
    pallas_call x1, Pallas kernels, grams_of(): pl.pallas_call(functools.partial(gram_kernel, yh_n, x_n, sections), out_s...  68.7 us
    pallas_call x1, Pallas kernels, finish(): pl.pallas_call(functools.partial(finish_kernel, sections), grid=(width //...  6.33 us

profile of v9, /device:TPU:1, one launch (start us, length us, event | category | flops | bytes accessed | tf_op | source)
XLA Modules:
  0.0 230.5 jit_solution(7964657598022223006)
XLA Ops:
  0.6 0.9 dynamic-slice_bitcast_fusion
  1.5 1.0 constant_dynamic-slice_fusion
  2.6 0.1 copy.7
  2.7 0.0 copy-start
  2.7 0.7 pad_maximum_fusion.base
  3.4 0.0 copy-done
  3.4 68.7 %shard_map.67 = (f32[3,64,256]{2,1,0:T(8,128)}, f32[64,128]{1,0:T(8,128)}, bf16[2,4,2,128,512]{4,3,2,1,0:T(8,128)(2,1)}, bf16[128,3584]{1,0:T(8,128)(2,1)}, bf16[3584,128]{1,0:T(8,128)(2,1)}) custom-call(bf16[128,7168]{1,0:T(8,128)(2,1)} %bitcast.20, bf16[128,7168]{1,0:T(8,128)(2,1)} %bitcast.22, bf16[7168,128]{1,0:T(8,128)(2,1)} %bitcast.18, ...), custom_call_target="tpu_custom_call" | custom-call | tf_op jit(solution)/shard_map/pallas_call | solution.py:1061
  72.1 152.1 %shard_map.68 = (bf16[128,7168]{1,0:T(8,128)(2,1)}, bf16[2,4,2,448,128]{4,3,2,1,0:T(8,128)(2,1)}, bf16[2,4,2,448,128]{4,3,2,1,0:T(8,128)(2,1)}, bf16[2,4,2,448,128]{4,3,2,1,0:T(8,128)(2,1)}, bf16[128,128]{1,0:T(8,128)(2,1)}) custom-call(f32[3,64,256]{2,1,0:T(8,128)} %get-tuple-element.16.pyh, f32[64,128]{1,0:T(8,128)} %get-tuple-element.17.n0, ...), custom_call_target="tpu_custom_call" | custom-call | tf_op jit(solution)/shard_map/pallas_call | solution.py:658
  224.2 6.3 %shard_map.69 = (bf16[7168,128]{1,0:T(8,128)(2,1)}, bf16[128,7168]{1,0:T(8,128)(2,1)}, bf16[128,7168]{1,0:T(8,128)(2,1)}) custom-call(bf16[7168,128]{1,0:T(8,128)(2,1)} %bitcast.28, bf16[7168,128]{1,0:T(8,128)(2,1)} %bitcast.29, bf16[7168,128]{1,0:T(8,128)(2,1)} %bitcast.30, bf16[128,128]{1,0:T(8,128)(2,1)} %get-tuple-element.24.bump_u, ...), custom_call_target="tpu_custom_call" | custom-call | tf_op jit(solution)/shard_map/pallas_call | solution.py:1108
Async XLA Ops:
  2.7 0.7 copy-start

commit v10 on v9

--- a/solution.py
+++ b/solution.py
@@ -37,11 +37,11 @@
 
 def recurrence_kernel(sections, chunks, per, yh_n, x_n,
                       pyh, n0, nn, x0_far, g16_far, up_far, wd_far, upart_far, wpart_far, mine_u,
-                      xout, own_w, own_u, nxt_u, bump_u,
+                      xout_far, own_w_far, own_u, nxt_u, bump_u,
                       ul, ql, qp, ys, nl, nsend, acc, hacc, slope, act, rinv, uf, qs, cpair,
                       xin, xkeep, xgive, gin, gkeep, ggive, xpass, delta,
                       gout, us, qv, xb, nacc, part, rc, sums, rax, rby, sa, ray, sb, rbx,
-                      gw, gu, nw, ub, x0, g16, up, wd, upart, wpart, l_sem,
+                      gw, gu, nw, ub, x0, g16, up, wd, upart, wpart, xout, own_w, l_sem,
                       u_send, u_recv, q_send, q_recv, e_sem,
                       c_send, c_recv, g_send, g_recv,
                       b_send, b_recv, h_send, h_recv, p_send, p_recv,
@@ -457,6 +457,13 @@
     lax.fori_loop(0, 2 * planes + trips + 1, tick, 0)
     collect((1 - ylo) * trips + trips - 1)
 
+    def landed_x(c, carry):
+        give_arrived(c).wait_recv()
+        return carry
+
+    lax.fori_loop(0, chunks, landed_x, 0)
+    save_x = pltpu.make_async_copy(xout, xout_far, l_sem.at[6])
+    save_x.start()
     total_a, total_b = scatter_sum(yh_n, x_n, sums, rax, rby, sa, ray, sb, rbx,
                                    ax_send, ax_recv, by_send, by_recv, s_sem, bx_send, bx_recv)
     cut = shard // 2
@@ -518,20 +525,26 @@
 
     own_w[yh, x, core] = gw[...]
     own_u[yh, x, core] = gu[...]
-    v_y.wait_recv()
+    @pl.when(has_next)
+    def _():
+        next_copy.wait_recv()
+        for i in range(1, x_n):
+            n_x(i).start()
+
     for i in range(1, x_n):
         w_x(x_n - i).wait_recv()
         w_y(i).start()
+
+    @pl.when(has_next)
+    def _():
+        n_y(0).start()
+        for i in range(1, x_n):
+            n_x(i).wait_send()
+
+    v_y.wait_recv()
     for i in range(1, x_n):
         v_x(i).start()
     v_c(0).start()
-
-    @pl.when(has_next)
-    def _():
-        next_copy.wait_recv()
-        for i in range(1, x_n):
-            n_x(i).start()
-        n_y(0).start()
 
     for i in range(x_n):
         w_y(i).wait_recv()
@@ -548,6 +561,8 @@
         v_c(i).start()
     for i in range(x_n):
         w_c(i).wait()
+    save_w = pltpu.make_async_copy(own_w, own_w_far, l_sem.at[7])
+    save_w.start()
 
     @pl.when(s > 0)
     def _():
@@ -572,8 +587,6 @@
         for i in range(x_n):
             n_c(i).wait()
             n_y(i).wait_send()
-        for i in range(1, x_n):
-            n_x(i).wait_send()
         bump_copy.wait_recv()
 
     for i in range(x_n):
@@ -594,13 +607,14 @@
         return carry
 
     lax.fori_loop(0, yh_n * x_n, core_settle, 0)
+    save_x.wait()
+    save_w.wait()
 
     def finish(c, carry):
         @pl.when(z < planes - 1)
         def _():
             x_copy(c).wait_send()
         give_copy(c).wait_send()
-        give_arrived(c).wait_recv()
         pass_copy(c).wait_send()
 
         @pl.when(z > 0)
@@ -660,7 +674,7 @@
         out_shape=(jax.ShapeDtypeStruct((rows, width), bf16), full, full, full,
                    jax.ShapeDtypeStruct(sq, bf16)),
         in_specs=[vm] * 3 + [pl.BlockSpec(memory_space=pl.ANY)] * 6 + [vm],
-        out_specs=(vm,) * 5,
+        out_specs=(pl.BlockSpec(memory_space=pl.ANY),) * 2 + (vm,) * 3,
         scratch_shapes=[
             pltpu.VMEM((planes,) + two, bf16),
             pltpu.VMEM((planes, some + 16, 2 * rank), bf16),
@@ -686,7 +700,8 @@
             pltpu.VMEM((shard, rank), bf16), pltpu.VMEM(sq, bf16),
             pltpu.VMEM((rows, width), bf16), pltpu.VMEM((rows, width), bf16),
             pltpu.VMEM((rank, width), bf16), pltpu.VMEM((width, rank), bf16),
-            pltpu.VMEM((rank, half), bf16), pltpu.VMEM((half, rank), bf16), dma((6,)),
+            pltpu.VMEM((rank, half), bf16), pltpu.VMEM((half, rank), bf16),
+            pltpu.VMEM((rows, width), bf16), pltpu.VMEM((yh_n, x_n, 2, shard, rank), bf16), dma((8,)),
         ] + [dma((planes,))] * 4 + [dma((10,))] + [dma((chunks,))] * 10 + [
             dma((blocks,)), dma((blocks,)),
             dma((yh_n * (x_n - 1),)), dma((yh_n * (x_n - 1),)), dma((x_n,)), dma((x_n,)), dma((2,)),
@@ -1102,7 +1117,7 @@
 def finish(sections, own_w, own_u, nxt_u, bump_u, x1):
     rows, width = x1.shape
     rank = own_w.shape[1]
-    step = width // 4
+    step = width // 8
     tall = pl.BlockSpec((step, rank), lambda i: (i, 0))
     flat = pl.BlockSpec((rows, step), lambda i: (0, i))
     return pl.pallas_call(

time: 231 us -> 226 us (0.978)
  Pallas kernels: 227 us -> 221 us
    pallas_call x1, Pallas kernels: 152 us -> 143 us  [recurrence(): pl.pallas_call(functools.partial(recurrence_kernel, sections, chunks, per...]
where the time goes in v10:
time: 226 us; the launch traced here: 224 us
  Pallas kernels  221 us (98%)
    pallas_call x1, Pallas kernels, recurrence(): pl.pallas_call(functools.partial(recurrence_kernel, sections, chunks, per...  143 us
    pallas_call x1, Pallas kernels, grams_of(): pl.pallas_call(functools.partial(gram_kernel, yh_n, x_n, sections), out_s...  68.7 us
    pallas_call x1, Pallas kernels, finish(): pl.pallas_call(functools.partial(finish_kernel, sections), grid=(width //...  8.39 us

profile of v10, /device:TPU:1, one launch (start us, length us, event | category | flops | bytes accessed | tf_op | source)
XLA Modules:
  0.0 224.0 jit_solution(12935738986848227136)
XLA Ops:
  0.6 0.9 dynamic-slice_bitcast_fusion
  1.5 1.0 constant_dynamic-slice_fusion
  2.6 0.1 copy.7
  2.7 0.0 copy-start
  2.7 0.7 pad_maximum_fusion.base
  3.4 0.0 copy-done
  3.4 68.7 %shard_map.67 = (f32[3,64,256]{2,1,0:T(8,128)}, f32[64,128]{1,0:T(8,128)}, bf16[2,4,2,128,512]{4,3,2,1,0:T(8,128)(2,1)}, bf16[128,3584]{1,0:T(8,128)(2,1)}, bf16[3584,128]{1,0:T(8,128)(2,1)}) custom-call(bf16[128,7168]{1,0:T(8,128)(2,1)} %bitcast.20, bf16[128,7168]{1,0:T(8,128)(2,1)} %bitcast.22, bf16[7168,128]{1,0:T(8,128)(2,1)} %bitcast.18, ...), custom_call_target="tpu_custom_call" | custom-call | tf_op jit(solution)/shard_map/pallas_call | solution.py:1076
  72.1 143.5 %shard_map.68 = (bf16[128,7168]{1,0:T(8,128)(2,1)}, bf16[2,4,2,448,128]{4,3,2,1,0:T(8,128)(2,1)}, bf16[2,4,2,448,128]{4,3,2,1,0:T(8,128)(2,1)}, bf16[2,4,2,448,128]{4,3,2,1,0:T(8,128)(2,1)}, bf16[128,128]{1,0:T(8,128)(2,1)}) custom-call(f32[3,64,256]{2,1,0:T(8,128)} %get-tuple-element.16.pyh, f32[64,128]{1,0:T(8,128)} %get-tuple-element.17.n0, ...), custom_call_target="tpu_custom_call" | custom-call | tf_op jit(solution)/shard_map/pallas_call | solution.py:672
  215.6 8.4 %shard_map.69 = (bf16[7168,128]{1,0:T(8,128)(2,1)}, bf16[128,7168]{1,0:T(8,128)(2,1)}, bf16[128,7168]{1,0:T(8,128)(2,1)}) custom-call(bf16[7168,128]{1,0:T(8,128)(2,1)} %bitcast.28, bf16[7168,128]{1,0:T(8,128)(2,1)} %bitcast.29, bf16[7168,128]{1,0:T(8,128)(2,1)} %bitcast.30, bf16[128,128]{1,0:T(8,128)(2,1)} %get-tuple-element.24.bump_u, ...), custom_call_target="tpu_custom_call" | custom-call | tf_op jit(solution)/shard_map/pallas_call | solution.py:1123
Async XLA Ops:
  2.7 0.7 copy-start

commit v11 on v10

--- a/solution.py
+++ b/solution.py
@@ -802,14 +802,18 @@
     return total_a, total_b
 
 
-def gram_kernel(yh_n, x_n, sections, x0_far, g16_far, down_far, up_far, mine_u, base, pyh, n0, out, upart, wpart,
+def gram_kernel(yh_n, x_n, sections, x0_far, g16_far, down_far, up_far, mine_u, pyh, n0, out, upart, wpart,
                 allu, part, rc, sums, rax, rby, sa, ray, sb, rbx, gs, gp, two, mine3, theirs3, flip, turned,
-                x0, g16, down, up, l_sem,
+                x0, g16, down, up, base, mine_w, l_sem,
                 z_sem, f_send, f_recv, r_send, r_recv,
                 c_send, c_recv, ax_send, ax_recv, by_send, by_recv, s_sem, bx_send, bx_recv,
                 ga_send, ga_recv, gb_send, gb_recv, gc_send, gc_recv, t_sem):
     loads = [pltpu.make_async_copy(far, near, l_sem.at[i]) for i, (far, near) in enumerate((
         (up_far, up), (down_far, down), (x0_far, x0), (g16_far, g16)))]
+    height = mine_u.shape[0]
+    own_rows = pl.ds(pl.multiple_of(lax.axis_index("dp") * height, 64), height)
+    load_w = pltpu.make_async_copy(down_far.at[own_rows, :], mine_w, l_sem.at[4])
+    load_w.start()
     for load in loads:
         load.start()
     yh, x, core = dp_place(x_n)
@@ -906,29 +910,34 @@
     swap_w = remote(down.at[far, :], wpart.at[near, :], z_sem.at[8], z_sem.at[9], partner)
     share_u = remote(upart.at[:, near], upart.at[:, near], z_sem.at[10], z_sem.at[11], other_core)
     share_w = remote(wpart.at[near, :], wpart.at[near, :], z_sem.at[12], z_sem.at[13], other_core)
-    for load in loads:
+    token_half = x0.shape[0] // 2
+    keep = pl.ds(ylo * token_half, token_half)
+    give = pl.ds((1 - ylo) * token_half, token_half)
+    swap3 = remote(mine3.at[:, give], theirs3, z_sem.at[2], z_sem.at[3], partner)
+
+    def project(i):
+        if i == 1:
+            for load in loads[2:]:
+                load.wait()
+            mine3[0] = dot_nn(x0[...], down[...])
+            mine3[1] = dot_nt(x0[...], up[...])
+        elif i == 2:
+            mine3[2] = dot_nt(g16[...], up[...])
+            swap3.start()
+            wide = x0[keep, :].astype(f32)
+            n0[...] = jnp.broadcast_to(jnp.sum(wide * wide, axis=1, keepdims=True), n0.shape)
+
+    def collect(b):
+        block_sum(b, yh_n, x_n, core_copy, part, rc, sums, rax, rby,
+                  ax_send, ax_recv, by_send, by_recv)
+
+    for load in loads[:2]:
         load.wait()
     swap_u.start()
     swap_w.start()
-
-    u = up[...]
-    w = down[...]
-    values = x0[...]
-    token_half = x0.shape[0] // 2
-    keep = pl.ds(ylo * token_half, token_half)
-    give = pl.ds((1 - ylo) * token_half, token_half)
-    mine3[0] = dot_nn(values, w)
-    mine3[1] = dot_nt(values, u)
-    mine3[2] = dot_nt(g16[...], u)
-    swap3 = remote(mine3.at[:, give], theirs3, z_sem.at[2], z_sem.at[3], partner)
-    swap3.start()
-    wide = x0[keep, :].astype(f32)
-    n0[...] = jnp.broadcast_to(jnp.sum(wide * wide, axis=1, keepdims=True), n0.shape)
-
-    def collect(b):
-        block_sum(b, yh_n, x_n, core_copy, part, rc, sums, rax, rby,
-                  ax_send, ax_recv, by_send, by_recv)
-
+    load_w.wait()
+    base[:, 0:rank] = mine_w[...]
+    base[:, rank:2 * rank] = mine_u[...]
     products(z)
     core_copy(z).start()
     for i in range(1, hops + 1):
@@ -941,6 +950,8 @@
                 ring_r(i, j).wait_recv()
                 if (i + 1, j) in used_r:
                     ring_r(i + 1, j).start()
+        if i < hops:
+            project(i)
         products(zp(z_n - i))
         core_copy(zp(z_n - i)).start()
         if i == 1:
@@ -1060,7 +1071,7 @@
     lax.fori_loop(0, yh_n * x_n, settle, 0)
 
 
-def grams_of(sections, shards, x0, g16, down, up, mine_u, base):
+def grams_of(sections, shards, x0, g16, down, up, mine_u):
     x_n = 4
     yh_n = shards // (2 * x_n)
     rows, width = x0.shape
@@ -1082,7 +1093,7 @@
             jax.ShapeDtypeStruct((rank, width // 2), bf16),
             jax.ShapeDtypeStruct((width // 2, rank), bf16),
         ),
-        in_specs=[pl.BlockSpec(memory_space=pl.ANY)] * 4 + [vm] * 2,
+        in_specs=[pl.BlockSpec(memory_space=pl.ANY)] * 4 + [vm],
         out_specs=(vm,) * 5,
         scratch_shapes=[
             pltpu.VMEM((sections // 2, 2, height, rank), bf16),
@@ -1093,7 +1104,8 @@
             pltpu.VMEM((3, rows, rank), f32), pltpu.VMEM((3, rows // 2, rank), f32),
             pltpu.VMEM((rank, rank), bf16), pltpu.VMEM((2, rank, rank), bf16),
             pltpu.VMEM((rows, width), bf16), pltpu.VMEM((rows, width), bf16),
-            pltpu.VMEM((width, rank), bf16), pltpu.VMEM((rank, width), bf16), dma((4,)),
+            pltpu.VMEM((width, rank), bf16), pltpu.VMEM((rank, width), bf16),
+            pltpu.VMEM((height, 2 * rank), bf16), pltpu.VMEM((height, rank), bf16), dma((5,)),
             dma((14,)), dma((sections // 2,)), dma((sections // 2,)),
             dma((sections // 2,)), dma((sections // 2,)),
             dma((yh_n * x_n,)), dma((yh_n * x_n,)),
@@ -1103,7 +1115,7 @@
         ],
         compiler_params=pltpu.CompilerParams(
             collective_id=3, has_side_effects=True, vmem_limit_bytes=60 * 1024 * 1024),
-    )(x0, g16, down, up, mine_u, base)
+    )(x0, g16, down, up, mine_u)
 
 
 def finish_kernel(sections, own_w, own_u, nxt_u, bump_u, x1, grad_down, grad_up, advance):
@@ -1149,9 +1161,7 @@
     up_t = upward.T
 
     mine_u = lax.dynamic_slice_in_dim(up_t, d * part, part, 0)
-    mine_w = lax.dynamic_slice_in_dim(down, d * part, part, 0)
-    base = jnp.concatenate([mine_w, mine_u], axis=1)
-    pyh, n0, grams, upart, wpart = grams_of(sections, shards, x0, g16, down, upward, mine_u, base)
+    pyh, n0, grams, upart, wpart = grams_of(sections, shards, x0, g16, down, upward, mine_u)
     grams = grams.reshape(sections // 2, 2 * rank, 4 * rank)
     x1, own_w, own_u, nxt_u, bump_u = recurrence(
         sections, shards, pyh, n0, grams, x0, g16, upward, down, upart, wpart, mine_u)

time: 226 us -> 226 us (level)
  no operation moved by 1% of the time
where the time goes in v11:
time: 226 us; the launch traced here: 223 us
  Pallas kernels  221 us (98%)
    pallas_call x1, Pallas kernels, recurrence(): pl.pallas_call(functools.partial(recurrence_kernel, sections, chunks, per...  143 us
    pallas_call x1, Pallas kernels, grams_of(): pl.pallas_call(functools.partial(gram_kernel, yh_n, x_n, sections), out_s...  68.8 us
    pallas_call x1, Pallas kernels, finish(): pl.pallas_call(functools.partial(finish_kernel, sections), grid=(width //...  8.39 us

profile of v11, /device:TPU:1, one launch (start us, length us, event | category | flops | bytes accessed | tf_op | source)
XLA Modules:
  0.0 223.0 jit_solution(119436475002340660)
XLA Ops:
  0.6 1.0 constant_dynamic-slice_fusion
  1.7 0.8 copy.7
  2.4 68.8 %shard_map.67 = (f32[3,64,256]{2,1,0:T(8,128)}, f32[64,128]{1,0:T(8,128)}, bf16[2,4,2,128,512]{4,3,2,1,0:T(8,128)(2,1)}, bf16[128,3584]{1,0:T(8,128)(2,1)}, bf16[3584,128]{1,0:T(8,128)(2,1)}) custom-call(bf16[128,7168]{1,0:T(8,128)(2,1)} %bitcast.16, bf16[128,7168]{1,0:T(8,128)(2,1)} %bitcast.18, bf16[7168,128]{1,0:T(8,128)(2,1)} %bitcast.20, ...), custom_call_target="tpu_custom_call" | custom-call | tf_op jit(solution)/shard_map/pallas_call | solution.py:1087
  71.2 143.4 %shard_map.68 = (bf16[128,7168]{1,0:T(8,128)(2,1)}, bf16[2,4,2,448,128]{4,3,2,1,0:T(8,128)(2,1)}, bf16[2,4,2,448,128]{4,3,2,1,0:T(8,128)(2,1)}, bf16[2,4,2,448,128]{4,3,2,1,0:T(8,128)(2,1)}, bf16[128,128]{1,0:T(8,128)(2,1)}) custom-call(f32[3,64,256]{2,1,0:T(8,128)} %get-tuple-element.16.pyh, f32[64,128]{1,0:T(8,128)} %get-tuple-element.17.n0, ...), custom_call_target="tpu_custom_call" | custom-call | tf_op jit(solution)/shard_map/pallas_call | solution.py:672
  214.6 8.4 %shard_map.69 = (bf16[7168,128]{1,0:T(8,128)(2,1)}, bf16[128,7168]{1,0:T(8,128)(2,1)}, bf16[128,7168]{1,0:T(8,128)(2,1)}) custom-call(bf16[7168,128]{1,0:T(8,128)(2,1)} %bitcast.23, bf16[7168,128]{1,0:T(8,128)(2,1)} %bitcast.24, bf16[7168,128]{1,0:T(8,128)(2,1)} %bitcast.25, bf16[128,128]{1,0:T(8,128)(2,1)} %get-tuple-element.24.bump_u, ...), custom_call_target="tpu_custom_call" | custom-call | tf_op jit(solution)/shard_map/pallas_call | solution.py:1135

commit v12 on v11

--- a/solution.py
+++ b/solution.py
@@ -1094,7 +1094,7 @@
             jax.ShapeDtypeStruct((width // 2, rank), bf16),
         ),
         in_specs=[pl.BlockSpec(memory_space=pl.ANY)] * 4 + [vm],
-        out_specs=(vm,) * 5,
+        out_specs=(vm,) * 3 + (pl.BlockSpec(memory_space=pl.ANY),) * 2,
         scratch_shapes=[
             pltpu.VMEM((sections // 2, 2, height, rank), bf16),
             buf(yh_n * x_n, 2, rank), buf(yh_n * x_n, rank), buf(yh_n, x_n, rank),

time: 226 us -> 226 us (level); the launches traced: 223 us -> 225 us
    pallas_call x1, Pallas kernels: 143 us -> 146 us  [recurrence(): pl.pallas_call(functools.partial(recurrence_kernel, sections, chunks, per...]
where the time goes in v12:
time: 226 us; the launch traced here: 225 us
  Pallas kernels  223 us (99%)
    pallas_call x1, Pallas kernels, recurrence(): pl.pallas_call(functools.partial(recurrence_kernel, sections, chunks, per...  146 us
    pallas_call x1, Pallas kernels, grams_of(): pl.pallas_call(functools.partial(gram_kernel, yh_n, x_n, sections), out_s...  68.7 us
    pallas_call x1, Pallas kernels, finish(): pl.pallas_call(functools.partial(finish_kernel, sections), grid=(width //...  8.39 us

profile of v12, /device:TPU:1, one launch (start us, length us, event | category | flops | bytes accessed | tf_op | source)
XLA Modules:
  0.0 225.3 jit_solution(5364654187547260939)
XLA Ops:
  0.6 1.0 constant_dynamic-slice_fusion
  1.7 0.8 copy.7
  2.4 68.7 %shard_map.67 = (f32[3,64,256]{2,1,0:T(8,128)}, f32[64,128]{1,0:T(8,128)}, bf16[2,4,2,128,512]{4,3,2,1,0:T(8,128)(2,1)}, bf16[128,3584]{1,0:T(8,128)(2,1)}, bf16[3584,128]{1,0:T(8,128)(2,1)}) custom-call(bf16[128,7168]{1,0:T(8,128)(2,1)} %bitcast.16, bf16[128,7168]{1,0:T(8,128)(2,1)} %bitcast.18, bf16[7168,128]{1,0:T(8,128)(2,1)} %bitcast.20, ...), custom_call_target="tpu_custom_call" | custom-call | tf_op jit(solution)/shard_map/pallas_call | solution.py:1087
  71.1 145.8 %shard_map.68 = (bf16[128,7168]{1,0:T(8,128)(2,1)}, bf16[2,4,2,448,128]{4,3,2,1,0:T(8,128)(2,1)}, bf16[2,4,2,448,128]{4,3,2,1,0:T(8,128)(2,1)}, bf16[2,4,2,448,128]{4,3,2,1,0:T(8,128)(2,1)}, bf16[128,128]{1,0:T(8,128)(2,1)}) custom-call(f32[3,64,256]{2,1,0:T(8,128)} %get-tuple-element.16.pyh, f32[64,128]{1,0:T(8,128)} %get-tuple-element.17.n0, ...), custom_call_target="tpu_custom_call" | custom-call | tf_op jit(solution)/shard_map/pallas_call | solution.py:672
  216.9 8.4 %shard_map.69 = (bf16[7168,128]{1,0:T(8,128)(2,1)}, bf16[128,7168]{1,0:T(8,128)(2,1)}, bf16[128,7168]{1,0:T(8,128)(2,1)}) custom-call(bf16[7168,128]{1,0:T(8,128)(2,1)} %bitcast.23, bf16[7168,128]{1,0:T(8,128)(2,1)} %bitcast.24, bf16[7168,128]{1,0:T(8,128)(2,1)} %bitcast.25, bf16[128,128]{1,0:T(8,128)(2,1)} %get-tuple-element.24.bump_u, ...), custom_call_target="tpu_custom_call" | custom-call | tf_op jit(solution)/shard_map/pallas_call | solution.py:1135
